TPU v7x, 32 devices: a whole 2x2x4 slice. The times are simulated.
32 devices in a mesh: freq: 2 (over x), tm: 8 (over z, core), batch: 2 (over y).
Axes of the slice: x: 2, y: 2, z: 4, core: 2. Of those that a mesh axis runs over, the one named last changes fastest.
Arguments:
- patches: bfloat16 [16, 8, 256, 384], P('batch', 'freq', 'tm'), may hold values from -6 to 6
- patch_mask: int32 [16, 8, 256], P('batch', 'freq', 'tm'), may hold values 0 or 1
- clip_lengths: int32 [16], P('batch'), may hold values from 1 to 256
- target_index: int32 [16, 8, 256], P('batch', 'freq', 'tm'), may hold values from 0 to 127
- targets: bfloat16 [16, 128, 384], P('batch'), may hold values from -0.41992188 to 0.41992188
- out_grad: bfloat16 [16, 8, 256, 384], P('batch', 'freq', 'tm'), may hold values from -6 to 6
- mask_embed: bfloat16 [384], replicated, may hold values from -4 to 4
- ln1_gain: bfloat16 [384], replicated, may hold values from 0.25 to 1.75
- ln1_shift: bfloat16 [384], replicated, may hold values from -1.5 to 1.5
- w_qkv: bfloat16 [384, 1152], replicated, may hold values from -0.3125 to 0.3125
- bias_q: bfloat16 [384], replicated, may hold values from -1.5 to 1.5
- bias_v: bfloat16 [384], replicated, may hold values from -0.25 to 0.25
- w_out: bfloat16 [384, 384], replicated, may hold values from -1.5 to 1.5
- bias_out: bfloat16 [384], replicated, may hold values from -1.5 to 1.5
- ln2_gain: bfloat16 [384], replicated, may hold values from 0.25 to 1.75
- ln2_shift: bfloat16 [384], replicated, may hold values from -1.5 to 1.5
- w_up: bfloat16 [384, 1536], replicated, may hold values from -0.3125 to 0.3125
- bias_up: bfloat16 [1536], replicated, may hold values from -1.5 to 1.5
- w_down: bfloat16 [1536, 384], replicated, may hold values from -0.15625 to 0.15625
- bias_down: bfloat16 [384], replicated, may hold values from -1.5 to 1.5
Outputs:
- block_out: bfloat16 [16, 8, 256, 384], P('batch', 'freq', 'tm')
- input_grad: bfloat16 [16, 8, 256, 384], P('batch', 'freq', 'tm')
- grad_mask_embed: float32 [384], replicated
- grad_ln1_gain: float32 [384], replicated
- grad_ln1_shift: float32 [384], replicated
- grad_w_qkv: float32 [384, 1152], replicated
- grad_bias_q: float32 [384], replicated
- grad_bias_v: float32 [384], replicated
- grad_w_out: float32 [384, 384], replicated
- grad_bias_out: float32 [384], replicated
- grad_ln2_gain: float32 [384], replicated
- grad_ln2_shift: float32 [384], replicated
- grad_w_up: float32 [384, 1536], replicated
- grad_bias_up: float32 [1536], replicated
- grad_w_down: float32 [1536, 384], replicated
- grad_bias_down: float32 [384], replicated
- soft_accuracy: float32 [16], P('batch')
All inputs are finite; a program needn't handle non-finite values. No bound on the sum of `patch_mask` on one device may be relied on, other than what follows from the above.
Results may differ from a plain program's by a relative error of at most 0.014.
Values may be sent and summed in bfloat16 or wider, within the bound.
A program may use at most 256 MiB of HBM per device.

v0:
```python
import jax
import jax.numpy as jnp
from jax import lax
from jax.sharding import PartitionSpec as P

D = 384
HEADS = 6
HEAD_DIM = 64
BLOCK_CLIPS = 4


def layer_norm(inputs, gain_vec, shift_vec):
    center = inputs - jnp.mean(inputs, axis=-1, keepdims=True)
    spread = jnp.mean(center * center, axis=-1, keepdims=True)
    return center * lax.rsqrt(spread + 1e-06) * gain_vec + shift_vec


def gelu_exact(inputs):
    return jax.nn.gelu(inputs, approximate=False)


def inner_rows(left_mat, right_mat):
    return lax.dot_general(
        left_mat, right_mat, (((0,), (0,)), ((), ())), preferred_element_type=jnp.float32
    )


def times_transpose(left_mat, right_mat):
    return lax.dot_general(
        left_mat, right_mat, (((1,), (1,)), ((), ())), preferred_element_type=jnp.float32
    )


def gather_keys(local):
    wider = lax.all_gather(local, "freq", axis=1, tiled=True)
    return lax.all_gather(wider, "tm", axis=2, tiled=True)


def gather_again(local):
    wider = lax.all_gather(local, "freq", axis=1, tiled=True)
    return lax.all_gather(wider, "tm", axis=2, tiled=True)


def split_heads(full_kv):
    blocks = full_kv.shape[0]
    flat_rows = full_kv.reshape(blocks, -1, 2 * D)
    key_rows = flat_rows[:, :, :D].reshape(blocks, -1, HEADS, HEAD_DIM)
    value_rows = flat_rows[:, :, D:].reshape(blocks, -1, HEADS, HEAD_DIM)
    return (key_rows, value_rows)


def masked_scores(queries, key_rows, lengths, full_kv):
    scores = jnp.einsum(
        "bqhd,bkhd->bhqk", queries, key_rows, preferred_element_type=jnp.float32
    ) * HEAD_DIM ** (-0.5)
    positions = lax.broadcasted_iota(
        jnp.int32, (full_kv.shape[0], full_kv.shape[1], full_kv.shape[2]), 2
    )
    usable = (positions < lengths[:, None, None]).reshape(full_kv.shape[0], -1)
    return jnp.where(usable[:, None, None, :], scores, -1000000000.0)


def attend_forward(queries, full_kv, lengths):
    key_rows, value_rows = split_heads(full_kv)
    scores = masked_scores(queries, key_rows, lengths, full_kv)
    row_max = jnp.max(scores, axis=-1, keepdims=True)
    raised = jnp.exp(scores - row_max)
    row_total = jnp.sum(raised, axis=-1, keepdims=True)
    attn_prob = (raised / row_total).astype(jnp.bfloat16)
    mixed = jnp.einsum("bhqk,bkhd->bqhd", attn_prob, value_rows, preferred_element_type=jnp.float32)
    return (mixed.astype(jnp.bfloat16), row_max + jnp.log(row_total))


def attend_backward(queries, full_kv, lengths, grad_mixed, log_total):
    key_rows, value_rows = split_heads(full_kv)
    scores = masked_scores(queries, key_rows, lengths, full_kv)
    attn_prob = jnp.exp(scores - log_total)
    grad_prob = jnp.einsum(
        "bqhd,bkhd->bhqk", grad_mixed, value_rows, preferred_element_type=jnp.float32
    )
    center = jnp.sum(attn_prob * grad_prob, axis=-1, keepdims=True)
    grad_scores = (attn_prob * (grad_prob - center)).astype(jnp.bfloat16)
    scale = HEAD_DIM ** (-0.5)
    grad_queries = (
        jnp.einsum("bhqk,bkhd->bqhd", grad_scores, key_rows, preferred_element_type=jnp.float32)
        * scale
    )
    grad_keys = (
        jnp.einsum("bhqk,bqhd->bkhd", grad_scores, queries, preferred_element_type=jnp.float32)
        * scale
    )
    grad_values = jnp.einsum(
        "bhqk,bqhd->bkhd",
        attn_prob.astype(jnp.bfloat16),
        grad_mixed,
        preferred_element_type=jnp.float32,
    )
    blocks = full_kv.shape[0]
    grad_full = jnp.concatenate(
        [grad_keys.reshape(blocks, -1, D), grad_values.reshape(blocks, -1, D)], axis=-1
    )
    grad_full = grad_full.reshape(full_kv.shape)
    own_part = lax.psum_scatter(
        grad_full.astype(jnp.bfloat16), "tm", scatter_dimension=2, tiled=True
    ).astype(jnp.float32)
    own_part = lax.psum_scatter(
        own_part.astype(jnp.bfloat16), "freq", scatter_dimension=1, tiled=True
    ).astype(jnp.float32)
    return (grad_queries.astype(jnp.bfloat16), own_part.astype(jnp.bfloat16))


def per_device(
    patches,
    patch_mask,
    clip_lengths,
    target_index,
    targets,
    out_grad,
    mask_embed,
    ln1_gain,
    ln1_shift,
    w_qkv,
    bias_q,
    bias_v,
    w_out,
    bias_out,
    ln2_gain,
    ln2_shift,
    w_up,
    bias_up,
    w_down,
    bias_down,
):
    clips, freq_rows, time_rows, width = patches.shape
    clip_rows = freq_rows * time_rows
    tokens = clips * clip_rows
    groups = clips // BLOCK_CLIPS
    masked = (patch_mask == 1)[..., None]
    flat_mask = masked.reshape(tokens, 1)
    start = jnp.where(masked, mask_embed.astype(jnp.float32), patches.astype(jnp.float32)).reshape(
        tokens, width
    )
    normed, first_back = jax.vjp(
        layer_norm, start, ln1_gain.astype(jnp.float32), ln1_shift.astype(jnp.float32)
    )
    normed_low = normed.astype(jnp.bfloat16)
    project = jnp.dot(normed_low, w_qkv, preferred_element_type=jnp.float32)
    queries = (project[:, :D] + bias_q.astype(jnp.float32)).astype(jnp.bfloat16)
    key_part = project[:, D : 2 * D]
    value_part = project[:, 2 * D :] + bias_v.astype(jnp.float32)
    local_kv = jnp.concatenate([key_part, value_part], axis=-1).astype(jnp.bfloat16)
    local_kv = local_kv.reshape(groups, BLOCK_CLIPS, freq_rows, time_rows, 2 * D)
    query_blocks = queries.reshape(groups, BLOCK_CLIPS, clip_rows, HEADS, HEAD_DIM)
    length_blocks = clip_lengths.reshape(groups, BLOCK_CLIPS)

    def forward_block(element):
        full_kv = gather_keys(element[1])
        return attend_forward(element[0], full_kv, element[2])

    mixed, log_total = lax.map(forward_block, (query_blocks, local_kv, length_blocks))
    mixed_rows = mixed.reshape(tokens, D)
    middle = (
        start
        + jnp.dot(mixed_rows, w_out, preferred_element_type=jnp.float32)
        + bias_out.astype(jnp.float32)
    )
    second, second_back = jax.vjp(
        layer_norm, middle, ln2_gain.astype(jnp.float32), ln2_shift.astype(jnp.float32)
    )
    second_low = second.astype(jnp.bfloat16)
    hidden_up = jnp.dot(second_low, w_up, preferred_element_type=jnp.float32) + bias_up.astype(
        jnp.float32
    )
    activated_f, gelu_back = jax.vjp(gelu_exact, hidden_up)
    activated = activated_f.astype(jnp.bfloat16)
    result = (
        middle
        + jnp.dot(activated, w_down, preferred_element_type=jnp.float32)
        + bias_down.astype(jnp.float32)
    )
    block_out = result.astype(jnp.bfloat16)
    grad_down = out_grad.reshape(tokens, width)
    grad_w_down = inner_rows(activated, grad_down)
    grad_bias_down = jnp.sum(grad_down.astype(jnp.float32), axis=0)
    grad_act = times_transpose(grad_down, w_down)
    grad_up = gelu_back(grad_act)[0].astype(jnp.bfloat16)
    grad_w_up = inner_rows(second_low, grad_up)
    grad_bias_up = jnp.sum(grad_up.astype(jnp.float32), axis=0)
    grad_second = times_transpose(grad_up, w_up)
    grad_middle_norm, grad_ln2_gain, grad_ln2_shift = second_back(grad_second)
    grad_middle = grad_down.astype(jnp.float32) + grad_middle_norm
    grad_branch = grad_middle.astype(jnp.bfloat16)
    grad_w_out = inner_rows(mixed_rows, grad_branch)
    grad_bias_out = jnp.sum(grad_branch.astype(jnp.float32), axis=0)
    grad_mixed = times_transpose(grad_branch, w_out).astype(jnp.bfloat16)
    grad_mixed = grad_mixed.reshape(groups, BLOCK_CLIPS, clip_rows, HEADS, HEAD_DIM)

    def backward_block(element):
        full_kv = gather_again(element[1])
        return attend_backward(element[0], full_kv, element[2], element[3], element[4])

    grad_queries, grad_kv = lax.map(
        backward_block, (query_blocks, local_kv, length_blocks, grad_mixed, log_total)
    )
    grad_query_rows = grad_queries.reshape(tokens, D)
    grad_kv_rows = grad_kv.reshape(tokens, 2 * D)
    grad_project = jnp.concatenate([grad_query_rows, grad_kv_rows], axis=-1)
    grad_w_qkv = inner_rows(normed_low, grad_project)
    grad_bias_q = jnp.sum(grad_query_rows.astype(jnp.float32), axis=0)
    grad_bias_v = jnp.sum(grad_kv_rows[:, D:].astype(jnp.float32), axis=0)
    grad_normed = times_transpose(grad_project, w_qkv)
    grad_start_norm, grad_ln1_gain, grad_ln1_shift = first_back(grad_normed)
    grad_start = grad_middle + grad_start_norm
    grad_mask_embed = jnp.sum(jnp.where(flat_mask, grad_start, 0.0), axis=0)
    input_grad = jnp.where(flat_mask, 0.0, grad_start).astype(jnp.bfloat16).reshape(patches.shape)
    summed = lax.psum(
        (
            grad_mask_embed,
            grad_ln1_gain,
            grad_ln1_shift,
            grad_w_qkv,
            grad_bias_q,
            grad_bias_v,
            grad_w_out,
            grad_bias_out,
            grad_ln2_gain,
            grad_ln2_shift,
            grad_w_up,
            grad_bias_up,
            grad_w_down,
            grad_bias_down,
        ),
        ("freq", "tm", "batch"),
    )
    out_rows = block_out.reshape(clips, clip_rows, width)
    logits = jnp.einsum("cqd,cnd->cqn", out_rows, targets, preferred_element_type=jnp.float32)
    logit_max = jnp.max(logits, axis=-1, keepdims=True)
    raised = jnp.exp(logits - logit_max)
    cand_prob = raised / jnp.sum(raised, axis=-1, keepdims=True)
    cand_ids = lax.broadcasted_iota(jnp.int32, cand_prob.shape, 2)
    picked = jnp.sum(
        jnp.where(cand_ids == target_index.reshape(clips, clip_rows)[..., None], cand_prob, 0.0),
        axis=-1,
    )
    positions = lax.axis_index("tm") * time_rows + lax.broadcasted_iota(
        jnp.int32, (clips, freq_rows, time_rows), 2
    )
    live_rows = (
        ((patch_mask == 1) & (positions < clip_lengths[:, None, None]))
        .reshape(clips, clip_rows)
        .astype(jnp.float32)
    )
    prob_sum, counted = lax.psum(
        (jnp.sum(picked * live_rows, axis=1), jnp.sum(live_rows, axis=1)), ("freq", "tm")
    )
    soft_accuracy = prob_sum / jnp.maximum(counted, 1.0)
    block_grid = block_out.reshape(patches.shape)
    return (
        block_grid,
        input_grad,
        summed[0],
        summed[1],
        summed[2],
        summed[3],
        summed[4],
        summed[5],
        summed[6],
        summed[7],
        summed[8],
        summed[9],
        summed[10],
        summed[11],
        summed[12],
        summed[13],
        soft_accuracy,
    )


def solution(mesh):
    in_specs = (
        P("batch", "freq", "tm", None),
        P("batch", "freq", "tm"),
        P("batch"),
        P("batch", "freq", "tm"),
        P("batch", None, None),
        P("batch", "freq", "tm", None),
        P(),
        P(),
        P(),
        P(),
        P(),
        P(),
        P(),
        P(),
        P(),
        P(),
        P(),
        P(),
        P(),
        P(),
    )
    out_specs = (
        P("batch", "freq", "tm", None),
        P("batch", "freq", "tm", None),
        P(),
        P(),
        P(),
        P(),
        P(),
        P(),
        P(),
        P(),
        P(),
        P(),
        P(),
        P(),
        P(),
        P(),
        P("batch"),
    )
    return jax.shard_map(
        per_device, mesh=mesh, in_specs=in_specs, out_specs=out_specs, check_vma=False
    )
```

profile of v0, /device:TPU:25, one launch (start us, length us, event | category | flops | bytes accessed | tf_op | source)
XLA Modules:
  0.0 1617.1 jit_solution(8345233267946131010)
XLA Ops:
  26.1 444.9 %while.24 = (s32[]{:T(128)}, bf16[2,4,128,6,64]{2,1,0,4,3:T(4,128)(2,1)}, f32[2,4,6,128,1]{3,2,1,4,0:T(8,128)}, bf16[2,4,4,32,768]{4,3,1,0,2:T(8,128)(2,1)S(1)},...) while((s32[]{:T(128)}, bf16[2,4,128,6,64]{2,1,0,4,3:T(4,128)(2,1)}, ...), condition=%wide.region_5.6_spmd, body=%wide.region_2.5_spmd.sunk | while | flops 1686311936 | bytes 244748528 | solution.py:160
  27.5 30.2 %all-gather.17.cloned.1.call-done = bf16[1,4,8,32,768]{4,3,1,0,2:T(8,128)(2,1)} async-done(((bf16[1,4,4,32,768]{4,3,1,0,2:T(8,128)(2,1)}), bf16[1,4,8,32,768]{4,3,1,0,2:T(8,128)(2,1)}) %all-gather.17.cloned.1.call-update) | async-done | bytes 1572880 | tf_op jit(solution)/shard_map/while/body/eval_jaxpr/all_gather | solution.py:35
  61.9 113.5 %all-gather.19.cloned.1.call-done = bf16[1,4,8,256,768]{4,2,1,0,3:T(8,128)(2,1)} async-done(((bf16[1,4,8,32,768]{4,2,1,0,3:T(8,128)(2,1)}), bf16[1,4,8,256,768]{4,2,1,0,3:T(8,128)(2,1)}) %all-gather.19.cloned.1.call-update) | async-done | bytes 12582928 | tf_op jit(solution)/shard_map/while/body/eval_jaxpr/all_gather | solution.py:36
  207.7 14.7 fusion.129
  234.3 12.2 fusion.131
  249.6 30.1 %all-gather.17.cloned.1.call-done = bf16[1,4,8,32,768]{4,3,1,0,2:T(8,128)(2,1)} async-done(((bf16[1,4,4,32,768]{4,3,1,0,2:T(8,128)(2,1)}), bf16[1,4,8,32,768]{4,3,1,0,2:T(8,128)(2,1)}) %all-gather.17.cloned.1.call-update) | async-done | bytes 1572880 | tf_op jit(solution)/shard_map/while/body/eval_jaxpr/all_gather | solution.py:35
  283.9 113.5 %all-gather.19.cloned.1.call-done = bf16[1,4,8,256,768]{4,2,1,0,3:T(8,128)(2,1)} async-done(((bf16[1,4,8,32,768]{4,2,1,0,3:T(8,128)(2,1)}), bf16[1,4,8,256,768]{4,2,1,0,3:T(8,128)(2,1)}) %all-gather.19.cloned.1.call-update) | async-done | bytes 12582928 | tf_op jit(solution)/shard_map/while/body/eval_jaxpr/all_gather | solution.py:36
  429.6 14.7 fusion.129
  456.3 12.2 fusion.131
  477.1 16.3 %multiply_convert_fusion.2 = (bf16[1024,1536]{1,0:T(8,128)(2,1)}, f32[1024,1536]{1,0:T(8,128)S(1)}, f32[1024,1536]{1,0:T(8,128)S(1)}) fusion(f32[1536]{0:T(1024)S(1)} %convert_element_type.124, bf16[384,1536]{1,0:T(8,128)(2,1)S(1)} %copy-done, f32[1024,384]{1,0:T(8,128)S(1)} %get-tuple-element.228, f32[384]{0:T(512)S(1)} %convert_element_type.122, ...), kind=kOutput, calls=%fused_computation.62 | convolution fusion | flops 1313734656 | bytes 18498560 | tf_op jit(solution)/shard_map/dot_general | solution.py:171
  511.3 914.6 %while.25 = (s32[]{:T(128)}, bf16[2,4,128,6,64]{2,4,3,1,0:T(8,128)(2,1)}, bf16[2,4,4,32,768]{4,3,2,1,0:T(8,128)(2,1)}, bf16[2,4,4,32,768]{4,3,1,0,2:T(8,128)(2,1...) while((s32[]{:T(128)}, ...), condition=%wide.region_14.15_spmd, body=%wide.region_10.14_spmd.sunk | while | flops 4155905024 | bytes 551883200 | solution.py:202
  516.7 29.6 %all-gather.21.cloned.1.call-done = bf16[1,4,8,32,768]{4,3,1,0,2:T(8,128)(2,1)} async-done(((bf16[1,4,4,32,768]{4,3,1,0,2:T(8,128)(2,1)}), bf16[1,4,8,32,768]{4,3,1,0,2:T(8,128)(2,1)}) %all-gather.21.cloned.1.call-update) | async-done | bytes 1572880 | tf_op jit(solution)/shard_map/while/body/eval_jaxpr/all_gather | solution.py:40
  551.5 112.6 %all-gather.23.cloned.1.call-done = bf16[1,4,8,256,768]{4,2,1,0,3:T(8,128)(2,1)} async-done(((bf16[1,4,8,32,768]{4,2,1,0,3:T(8,128)(2,1)}), bf16[1,4,8,256,768]{4,2,1,0,3:T(8,128)(2,1)}) %all-gather.23.cloned.1.call-update) | async-done | bytes 12582928 | tf_op jit(solution)/shard_map/while/body/eval_jaxpr/all_gather | solution.py:41
  696.1 14.6 fusion.142
  710.7 12.9 fusion.145
  723.5 18.5 %multiply_reduce_fusion.8 = (f32[4,6,128]{2,1,0:T(8,128)S(1)}, f32[4,6,128,2048]{3,2,1,0:T(8,128)}) fusion(f32[4,6,128,2048]{3,2,1,0:T(8,128)} %fusion.142, f32[4,6,128]{2,1,0:T(8,128)S(1)} %copy-done.18, pred[4,2048]{1,0:T(4,128)(4,1)S(1)} %broadcast_compare_fusion.6, bf16[4,2048,6,64]{1,3,2,0:T(8,128)(2,1)} %bitcast.204, ...), kind=kOutput, calls=%fused_computation.22.clone.1 | convolution fusion | flops 836760576 | bytes 57049088 | tf_op jit(solution)/shard_map/while/body/eval_jaxpr/bqhd,bkhd->bhqk/dot_general | solution.py:78
  742.0 16.9 %multiply_convert_fusion.5 = bf16[4,6,128,2048]{3,2,1,0:T(8,128)(2,1)S(1)} fusion(f32[4,6,128,2048]{3,2,1,0:T(8,128)} %get-tuple-element.334, f32[4,6,128,2048]{3,2,1,0:T(8,128)} %fusion.142, f32[4,6,128]{2,1,0:T(8,128)S(1)} %get-tuple-element.335, f32[4,6,128]{2,1,0:T(8,128)S(1)} %copy-done.18, pred[4,2048]{1,0:T(4,128)(4,1)S(1)} %broadcast_compare_fusion.6), kind=kLoop, calls=%fused_computation.21.clone.1 | loop fusion | flops 37748736 | bytes 62947328 | tf_op jit(solution)/shard_map/while/body/eval_jaxpr/convert_element_type | solution.py:82
  807.1 127.3 %reduce-scatter.3.cloned.1.call-done = bf16[4,8,32,768]{3,1,0,2:T(8,128)(2,1)} async-done(((bf16[4,8,256,768]{3,1,0,2:T(8,128)(2,1)}), bf16[4,8,32,768]{3,1,0,2:T(8,128)(2,1)}) %reduce-scatter.3.cloned.1.call-update) | async-done | bytes 1572880 | tf_op jit(solution)/shard_map/while/body/eval_jaxpr/reduce_scatter | solution.py:103
  937.9 11.7 fusion.144
  949.6 15.7 reduce-scatter.5.cloned.1.call-done
  968.5 29.1 %all-gather.21.cloned.1.call-done = bf16[1,4,8,32,768]{4,3,1,0,2:T(8,128)(2,1)} async-done(((bf16[1,4,4,32,768]{4,3,1,0,2:T(8,128)(2,1)}), bf16[1,4,8,32,768]{4,3,1,0,2:T(8,128)(2,1)}) %all-gather.21.cloned.1.call-update) | async-done | bytes 1572880 | tf_op jit(solution)/shard_map/while/body/eval_jaxpr/all_gather | solution.py:40
  1002.7 112.6 %all-gather.23.cloned.1.call-done = bf16[1,4,8,256,768]{4,2,1,0,3:T(8,128)(2,1)} async-done(((bf16[1,4,8,32,768]{4,2,1,0,3:T(8,128)(2,1)}), bf16[1,4,8,256,768]{4,2,1,0,3:T(8,128)(2,1)}) %all-gather.23.cloned.1.call-update) | async-done | bytes 12582928 | tf_op jit(solution)/shard_map/while/body/eval_jaxpr/all_gather | solution.py:41
  1147.4 14.6 fusion.142
  1162.0 12.9 fusion.145
  1174.8 18.5 %multiply_reduce_fusion.8 = (f32[4,6,128]{2,1,0:T(8,128)S(1)}, f32[4,6,128,2048]{3,2,1,0:T(8,128)}) fusion(f32[4,6,128,2048]{3,2,1,0:T(8,128)} %fusion.142, f32[4,6,128]{2,1,0:T(8,128)S(1)} %copy-done.18, pred[4,2048]{1,0:T(4,128)(4,1)S(1)} %broadcast_compare_fusion.6, bf16[4,2048,6,64]{1,3,2,0:T(8,128)(2,1)} %bitcast.204, ...), kind=kOutput, calls=%fused_computation.22.clone.1 | convolution fusion | flops 836760576 | bytes 57049088 | tf_op jit(solution)/shard_map/while/body/eval_jaxpr/bqhd,bkhd->bhqk/dot_general | solution.py:78
  1193.3 16.9 %multiply_convert_fusion.5 = bf16[4,6,128,2048]{3,2,1,0:T(8,128)(2,1)S(1)} fusion(f32[4,6,128,2048]{3,2,1,0:T(8,128)} %get-tuple-element.334, f32[4,6,128,2048]{3,2,1,0:T(8,128)} %fusion.142, f32[4,6,128]{2,1,0:T(8,128)S(1)} %get-tuple-element.335, f32[4,6,128]{2,1,0:T(8,128)S(1)} %copy-done.18, pred[4,2048]{1,0:T(4,128)(4,1)S(1)} %broadcast_compare_fusion.6), kind=kLoop, calls=%fused_computation.21.clone.1 | loop fusion | flops 37748736 | bytes 62947328 | tf_op jit(solution)/shard_map/while/body/eval_jaxpr/convert_element_type | solution.py:82
  1258.4 127.3 %reduce-scatter.3.cloned.1.call-done = bf16[4,8,32,768]{3,1,0,2:T(8,128)(2,1)} async-done(((bf16[4,8,256,768]{3,1,0,2:T(8,128)(2,1)}), bf16[4,8,32,768]{3,1,0,2:T(8,128)(2,1)}) %reduce-scatter.3.cloned.1.call-update) | async-done | bytes 1572880 | tf_op jit(solution)/shard_map/while/body/eval_jaxpr/reduce_scatter | solution.py:103
  1389.2 11.7 fusion.144
  1400.9 15.7 reduce-scatter.5.cloned.1.call-done
  1445.3 30.7 %all-reduce.2 = (f32[8]{0:T(128)S(1)}, f32[8]{0:T(128)S(1)}) all-reduce(f32[8]{0:T(128)S(1)} %get-tuple-element.160, f32[8]{0:T(128)S(1)} %get-tuple-element.159), channel_id=1, replica_groups=mesh['freq'=2,'tm'=8,'batch'=2] {'freq','tm'}, use_global_device_ids=true, to_apply=%region_45.46 | all-reduce | flops 16 | bytes 128 | tf_op jit(solution)/shard_map/psum | solution.py:253
  1484.3 40.5 %all-reduce = (f32[384]{0:T(512)}, f32[384]{0:T(512)}, f32[384]{0:T(512)}, f32[384]{0:T(512)}, f32[384]{0:T(512)}, /*index=5*/f32[384]{0:T(512)}, f32[384]{0:T(512)}, f32[384]{0:T(512)}, f32[1536]{0:T(1024)}, f32[384]{0:T(512)}) all-reduce(f32[384]{0:T(512)S(1)} %get-tuple-element.223, ...), channel_id=1, replica_groups=mesh['freq'=2,'tm'=8,'batch'=2] {'freq','tm','batch'}, use_global_device_ids=true, to_apply=%region_18.19 | all-reduce | flops 4992 | bytes 39936 | tf_op jit(solution)/shard_map/psum | solution.py:216
  1525.2 76.6 %all-reduce.5.cloned.1.call-done = (f32[384,1152]{1,0:T(8,128)}, f32[384,384]{1,0:T(8,128)}, f32[384,1536]{1,0:T(8,128)}, f32[1536,384]{1,0:T(8,128)}) async-done(((f32[384,1152]{1,0:T(8,128)}, f32[384,384]{1,0:T(8,128)}, f32[384,1536]{1,0:T(8,128)}, f32[1536,384]{1,0:T(8,128)}), (f32[384,1152]{1,0:T(8,128)}, f32[384,384]{1,0:T(8,128)}, f32[384,1536]{1,0:T(8,128)}, ...) | async-done | bytes 7077904 | tf_op jit(solution)/shard_map/psum | solution.py:216
  (282 shorter events, 364.0 us)
Async XLA Ops:
  8.0 469.1 %copy-start = (bf16[384,1536]{1,0:T(8,128)(2,1)S(1)}, bf16[384,1536]{1,0:T(8,128)(2,1)}, u32[]{:S(2)}) copy-start(bf16[384,1536]{1,0:T(8,128)(2,1)} %param.40) | copy-start | bytes 3538948
  26.4 31.2 %all-gather.17.cloned.1.call-start = ((), (), s32[]{:S(2)}) async-start(), calls=%async_computation.3 | async-start | bytes 2359296 | tf_op jit(solution)/shard_map/while/body/eval_jaxpr/all_gather | solution.py:35
  27.5 147.9 %all-gather.19.cloned.1.call-start = ((), (), s32[]{:S(2)}) async-start(), calls=%async_computation.4 | async-start | bytes 14155776 | tf_op jit(solution)/shard_map/while/body/eval_jaxpr/all_gather | solution.py:36
  248.5 31.1 %all-gather.17.cloned.1.call-start = ((), (), s32[]{:S(2)}) async-start(), calls=%async_computation.3 | async-start | bytes 2359296 | tf_op jit(solution)/shard_map/while/body/eval_jaxpr/all_gather | solution.py:35
  249.5 147.8 %all-gather.19.cloned.1.call-start = ((), (), s32[]{:S(2)}) async-start(), calls=%async_computation.4 | async-start | bytes 14155776 | tf_op jit(solution)/shard_map/while/body/eval_jaxpr/all_gather | solution.py:36
  476.6 26.7 %copy-start.10 = (f32[1024,384]{1,0:T(8,128)}, f32[1024,384]{1,0:T(8,128)S(1)}, u32[]{:S(2)}) copy-start(f32[1024,384]{1,0:T(8,128)S(1)} %get-tuple-element.228) | copy-start | bytes 4718596
  477.1 16.3 %copy-start.13 = (bf16[8,4,32,384]{3,2,1,0:T(8,128)(2,1)S(1)}, bf16[8,4,32,384]{3,2,1,0:T(8,128)(2,1)}, u32[]{:S(2)}) copy-start(bf16[8,4,32,384]{3,2,1,0:T(8,128)(2,1)} %param.29) | copy-start | bytes 2359300
  477.1 16.3 %copy-start.49 = (bf16[1536,384]{1,0:T(8,128)(2,1)S(1)}, bf16[1536,384]{1,0:T(8,128)(2,1)}, u32[]{:S(2)}) copy-start(bf16[1536,384]{1,0:T(8,128)(2,1)} %param.42) | copy-start | bytes 3538948
  515.5 157.6 %copy-start.6 = (bf16[2,4,4,32,768]{4,3,1,0,2:T(8,128)(2,1)}, bf16[2,4,4,32,768]{4,3,1,0,2:T(8,128)(2,1)S(1)}, u32[]{:S(2)}) copy-start(bf16[2,4,4,32,768]{4,3,1,0,2:T(8,128)(2,1)S(1)} %get-tuple-element.378) | copy-start | bytes 4718596 | tf_op jit(solution)/shard_map/while
  515.5 180.6 %copy-start.4 = (bf16[2,4,128,6,64]{2,4,3,1,0:T(8,128)(2,1)}, bf16[2,4,128,6,64]{2,4,3,1,0:T(8,128)(2,1)S(1)}, u32[]{:S(2)}) copy-start(bf16[2,4,128,6,64]{2,4,3,1,0:T(8,128)(2,1)S(1)} %get-tuple-element.380) | copy-start | bytes 2359300 | tf_op jit(solution)/shard_map/while
  515.6 30.8 %all-gather.21.cloned.1.call-start = ((), (), s32[]{:S(2)}) async-start(), calls=%async_computation.5 | async-start | bytes 2359296 | tf_op jit(solution)/shard_map/while/body/eval_jaxpr/all_gather | solution.py:40
  516.7 147.4 %all-gather.23.cloned.1.call-start = ((), (), s32[]{:S(2)}) async-start(), calls=%async_computation.6 | async-start | bytes 14155776 | tf_op jit(solution)/shard_map/while/body/eval_jaxpr/all_gather | solution.py:41
  549.8 384.6 %reduce-scatter.3.cloned.1.call-start = ((), (), s32[]{:S(2)}) async-start(), calls=%async_computation.7 | async-start | bytes 14155776 | tf_op jit(solution)/shard_map/while/body/eval_jaxpr/reduce_scatter | solution.py:103
  807.1 158.2 %reduce-scatter.5.cloned.1.call-start = ((), (), s32[]{:S(2)}) async-start(), calls=%async_computation.8 | async-start | bytes 2359296 | tf_op jit(solution)/shard_map/while/body/eval_jaxpr/reduce_scatter | solution.py:106
  937.9 29.5 %copy-start.5 = (bf16[2,4,128,6,64]{2,4,3,1,0:T(8,128)(2,1)S(1)}, bf16[2,4,128,6,64]{2,4,3,1,0:T(8,128)(2,1)}, u32[]{:S(2)}) copy-start(bf16[2,4,128,6,64]{2,4,3,1,0:T(8,128)(2,1)} %copy-done.4) | copy-start | bytes 2359300 | tf_op jit(solution)/shard_map/while
  937.9 29.5 %copy-start.7 = (bf16[2,4,4,32,768]{4,3,1,0,2:T(8,128)(2,1)S(1)}, bf16[2,4,4,32,768]{4,3,1,0,2:T(8,128)(2,1)}, u32[]{:S(2)}) copy-start(bf16[2,4,4,32,768]{4,3,1,0,2:T(8,128)(2,1)} %copy-done.6) | copy-start | bytes 4718596 | tf_op jit(solution)/shard_map/while
  967.3 157.1 %copy-start.6 = (bf16[2,4,4,32,768]{4,3,1,0,2:T(8,128)(2,1)}, bf16[2,4,4,32,768]{4,3,1,0,2:T(8,128)(2,1)S(1)}, u32[]{:S(2)}) copy-start(bf16[2,4,4,32,768]{4,3,1,0,2:T(8,128)(2,1)S(1)} %get-tuple-element.378) | copy-start | bytes 4718596 | tf_op jit(solution)/shard_map/while
  967.3 180.1 %copy-start.4 = (bf16[2,4,128,6,64]{2,4,3,1,0:T(8,128)(2,1)}, bf16[2,4,128,6,64]{2,4,3,1,0:T(8,128)(2,1)S(1)}, u32[]{:S(2)}) copy-start(bf16[2,4,128,6,64]{2,4,3,1,0:T(8,128)(2,1)S(1)} %get-tuple-element.380) | copy-start | bytes 2359300 | tf_op jit(solution)/shard_map/while
  967.4 30.3 %all-gather.21.cloned.1.call-start = ((), (), s32[]{:S(2)}) async-start(), calls=%async_computation.5 | async-start | bytes 2359296 | tf_op jit(solution)/shard_map/while/body/eval_jaxpr/all_gather | solution.py:40
  968.5 146.9 %all-gather.23.cloned.1.call-start = ((), (), s32[]{:S(2)}) async-start(), calls=%async_computation.6 | async-start | bytes 14155776 | tf_op jit(solution)/shard_map/while/body/eval_jaxpr/all_gather | solution.py:41
  1001.1 384.6 %reduce-scatter.3.cloned.1.call-start = ((), (), s32[]{:S(2)}) async-start(), calls=%async_computation.7 | async-start | bytes 14155776 | tf_op jit(solution)/shard_map/while/body/eval_jaxpr/reduce_scatter | solution.py:103
  1258.3 158.2 %reduce-scatter.5.cloned.1.call-start = ((), (), s32[]{:S(2)}) async-start(), calls=%async_computation.8 | async-start | bytes 2359296 | tf_op jit(solution)/shard_map/while/body/eval_jaxpr/reduce_scatter | solution.py:106
  1389.2 29.5 %copy-start.5 = (bf16[2,4,128,6,64]{2,4,3,1,0:T(8,128)(2,1)S(1)}, bf16[2,4,128,6,64]{2,4,3,1,0:T(8,128)(2,1)}, u32[]{:S(2)}) copy-start(bf16[2,4,128,6,64]{2,4,3,1,0:T(8,128)(2,1)} %copy-done.4) | copy-start | bytes 2359300 | tf_op jit(solution)/shard_map/while
  1389.2 29.5 %copy-start.7 = (bf16[2,4,4,32,768]{4,3,1,0,2:T(8,128)(2,1)S(1)}, bf16[2,4,4,32,768]{4,3,1,0,2:T(8,128)(2,1)}, u32[]{:S(2)}) copy-start(bf16[2,4,4,32,768]{4,3,1,0,2:T(8,128)(2,1)} %copy-done.6) | copy-start | bytes 4718596 | tf_op jit(solution)/shard_map/while
  1426.0 175.8 %all-reduce.5.cloned.1.call-start = ((), (), s32[]{:S(2)}) async-start(), calls=%async_computation.2 | async-start | bytes 14155776 | tf_op jit(solution)/shard_map/psum | solution.py:216
  1437.0 39.0 %copy-start.26 = (pred[8,4,32]{2,1,0:T(4,128)(4,1)S(1)}, pred[8,4,32]{2,1,0:T(4,128)(4,1)}, u32[]{:S(2)}) copy-start(pred[8,4,32]{2,1,0:T(4,128)(4,1)} %copy-done.25) | copy-start | bytes 3076
  1437.0 39.1 %copy-start.19 = (bf16[2,4,128,6,64]{2,4,3,1,0:T(8,128)(2,1)S(1)}, bf16[2,4,128,6,64]{2,4,3,1,0:T(8,128)(2,1)}, u32[]{:S(2)}) copy-start(bf16[2,4,128,6,64]{2,4,3,1,0:T(8,128)(2,1)} %get-tuple-element.95) | copy-start | bytes 2359300
  1437.0 39.3 %copy-start.14 = (bf16[8,4,32,384]{3,2,1,0:T(8,128)(2,1)S(1)}, bf16[8,4,32,384]{3,2,1,0:T(8,128)(2,1)}, u32[]{:S(2)}) copy-start(bf16[8,4,32,384]{3,2,1,0:T(8,128)(2,1)} %param.29) | copy-start | bytes 2359300
  1437.1 40.8 %copy-start.9 = (f32[8,4,32,384]{3,2,1,0:T(8,128)S(1)}, f32[8,4,32,384]{3,2,1,0:T(8,128)}, u32[]{:S(2)}) copy-start(f32[8,4,32,384]{3,2,1,0:T(8,128)} %copy-done.8) | copy-start | bytes 4718596
  1437.1 40.8 %copy-start.33 = (f32[1024]{0:T(1024)S(1)}, f32[1024]{0:T(1024)}, u32[]{:S(2)}) copy-start(f32[1024]{0:T(1024)} %copy-done.32) | copy-start | bytes 12292
  1437.1 40.8 %copy-start.35 = (f32[1024]{0:T(1024)S(1)}, f32[1024]{0:T(1024)}, u32[]{:S(2)}) copy-start(f32[1024]{0:T(1024)} %copy-done.34) | copy-start | bytes 12292
  1437.1 40.8 %copy-start.37 = (f32[384]{0:T(512)S(1)}, f32[384]{0:T(512)}, u32[]{:S(2)}) copy-start(f32[384]{0:T(512)} %copy-done.36) | copy-start | bytes 4612
  (39 other events, 228.1 us)
Sparse Core Ops, SparseCore 0:
  29.5 28.1 all-gather.16
  61.2 114.1 all-gather.18
  251.6 28.0 all-gather.16
  283.2 114.1 all-gather.18
  518.3 28.0 all-gather.20
  549.9 114.1 all-gather.22
  807.2 127.2 reduce-scatter.2
  938.0 27.2 reduce-scatter.4
  970.4 27.2 all-gather.20
  1001.2 114.1 all-gather.22
  1258.5 127.2 reduce-scatter.2
  1389.3 27.2 reduce-scatter.4
Sparse Core Ops, SparseCore 1:
  1437.0 164.7 all-reduce.4
where the time goes:
time: 1630 us; the launch traced here: 1620 us
  waiting for transfers between devices  934 us (57%)
  local copies, waits for them, and re-layouts  257 us (16%)
  matrix products  229 us (14%)
  other arithmetic  96.1 us (6%)
  blocking collectives  71.1 us (4%)
  between operations  16.4 us (1%)
    reduce_scatter x2, waiting for transfers between devices, attend_backward(): lax.psum_scatter(grad_full.astype(jnp.bfloat16), 'tm', scatter_dimension=...  255 us
    all_gather x2, waiting for transfers between devices, gather_keys(): return lax.all_gather(wider, 'tm', axis=2, tiled=True)  227 us
    all_gather x2, waiting for transfers between devices, gather_again(): return lax.all_gather(wider, 'tm', axis=2, tiled=True)  225 us
    psum x1, waiting for transfers between devices, per_device(): lax.psum((grad_mask_embed, grad_ln1_gain, grad_ln1_shift, grad_w_qkv, gra...  76.6 us
    all_gather x2, waiting for transfers between devices, gather_keys(): wider = lax.all_gather(local, 'freq', axis=1, tiled=True)  60.2 us
    all_gather x2, waiting for transfers between devices, gather_again(): wider = lax.all_gather(local, 'freq', axis=1, tiled=True)  58.8 us
    dot_general x4, matrix products, masked_scores(): jnp.einsum('bqhd,bkhd->bhqk', queries, key_rows, preferred_element_type=j...  58.5 us
    slice x6, local copies, waits for them, and re-layouts, split_heads(): key_rows = flat_rows[:, :, :D].reshape(blocks, -1, HEADS, HEAD_DIM)  46.4 us
  transfers between devices with their start and end apart: 13, of which 13 were waited for; matrix products, arithmetic and copies ran while one was open for 3% of the time, Pallas kernels for 0%

commit v1 on v0

v1 whole, which is shorter than its diff:
```python
import functools

import jax
import jax.numpy as jnp
from jax import lax
from jax.experimental import pallas as pl
from jax.experimental.pallas import tpu as pltpu
from jax.sharding import PartitionSpec as P

D = 384
HEADS = 6
HEAD_DIM = 64
PAIRS = HEADS // 2
PAIR = 2 * HEAD_DIM
SCALE = HEAD_DIM ** (-0.5)
DEAD = -1e9
MESH = pl.DeviceIdType.MESH
VMEM_LIMIT = 60 * 2**20


def mm(left_mat, right_mat):
    return jnp.dot(left_mat, right_mat, preferred_element_type=jnp.float32)


def mm_nt(left_mat, right_mat):
    return lax.dot_general(
        left_mat, right_mat, (((1,), (1,)), ((), ())), preferred_element_type=jnp.float32
    )


def mm_tn(left_mat, right_mat):
    return lax.dot_general(
        left_mat, right_mat, (((0,), (0,)), ((), ())), preferred_element_type=jnp.float32
    )


class Plan:
    def __init__(self, mesh, clips):
        self.freq = mesh.shape["freq"]
        self.tm = mesh.shape["tm"]
        self.clips = clips
        self.share = self.freq * self.tm // clips
        self.blocks = self.tm // self.share
        assert self.freq * self.blocks == clips and self.blocks * self.share == self.tm


def exchange_kernel(plan, count, *refs):
    ins, outs = refs[:count], refs[count : 2 * count]
    send_sem, recv_sem, local_sem = refs[2 * count :]
    time_id = lax.axis_index("tm")
    part = time_id % plan.share
    me = lax.axis_index("freq") * plan.blocks + time_id // plan.share

    def device(member):
        return {"freq": member // plan.blocks, "tm": (member % plan.blocks) * plan.share + part}

    barrier = pltpu.get_barrier_semaphore()
    for step in range(1, plan.clips):
        pl.semaphore_signal(
            barrier, inc=1, device_id=device(lax.rem(me + step, plan.clips)), device_id_type=MESH
        )
    pl.semaphore_wait(barrier, plan.clips - 1)
    copies = []
    for i in range(count):
        for step in range(1, plan.clips):
            peer = lax.rem(me + step, plan.clips)
            copy = pltpu.make_async_remote_copy(
                src_ref=ins[i].at[peer],
                dst_ref=outs[i].at[me],
                send_sem=send_sem.at[i, step],
                recv_sem=recv_sem.at[i, step],
                device_id=device(peer),
                device_id_type=MESH,
            )
            copy.start()
            copies.append(copy)
        copy = pltpu.make_async_copy(ins[i].at[me], outs[i].at[me], local_sem.at[i])
        copy.start()
        copies.append(copy)
    for copy in copies:
        copy.wait()


def exchange(plan, collective_id, *arrays):
    count = len(arrays)
    return pl.pallas_call(
        functools.partial(exchange_kernel, plan, count),
        out_shape=[jax.ShapeDtypeStruct(x.shape, x.dtype) for x in arrays],
        in_specs=[pl.BlockSpec(memory_space=pl.ANY)] * count,
        out_specs=[pl.BlockSpec(memory_space=pl.ANY)] * count,
        scratch_shapes=[
            pltpu.SemaphoreType.DMA((count, plan.clips)),
            pltpu.SemaphoreType.DMA((count, plan.clips)),
            pltpu.SemaphoreType.DMA((count,)),
        ],
        compiler_params=pltpu.CompilerParams(collective_id=collective_id, has_side_effects=True),
        name="exchange",
    )(*arrays)


def forward_kernel(q_ref, k_ref, v_ref, bias_ref, mixed_ref, total_ref):
    lane = lax.broadcasted_iota(jnp.int32, (1, PAIR), 1)
    q_pair, k_pair, v_pair, bias = q_ref[...], k_ref[...], v_ref[...], bias_ref[...]
    outs = []
    for e in range(2):
        own = (lane // HEAD_DIM) == e
        scores = mm_nt(jnp.where(own, q_pair, jnp.zeros_like(q_pair)), k_pair) + bias
        row_max = jnp.max(scores, axis=1, keepdims=True)
        raised = jnp.exp(scores - row_max)
        row_total = jnp.sum(raised, axis=1, keepdims=True)
        outs.append(mm(raised.astype(jnp.bfloat16), v_pair) / row_total)
        total_ref[0, e, :] = (row_max + jnp.log(row_total))[:, 0]
    mixed_ref[...] = jnp.where(lane < HEAD_DIM, outs[0], outs[1])


def attend_forward(queries, key_rows, value_rows, bias):
    rows, keys = queries.shape[0], key_rows.shape[0]
    block = min(256, rows)
    return pl.pallas_call(
        forward_kernel,
        grid=(PAIRS, rows // block),
        in_specs=[
            pl.BlockSpec((block, PAIR), lambda p, i: (i, p)),
            pl.BlockSpec((keys, PAIR), lambda p, i: (0, p)),
            pl.BlockSpec((keys, PAIR), lambda p, i: (0, p)),
            pl.BlockSpec((1, keys), lambda p, i: (0, 0)),
        ],
        out_specs=[
            pl.BlockSpec((block, PAIR), lambda p, i: (i, p)),
            pl.BlockSpec((1, 2, block), lambda p, i: (p, 0, i)),
        ],
        out_shape=[
            jax.ShapeDtypeStruct((rows, D), jnp.float32),
            jax.ShapeDtypeStruct((PAIRS, 2, rows), jnp.float32),
        ],
        compiler_params=pltpu.CompilerParams(vmem_limit_bytes=VMEM_LIMIT),
        name="attend_forward",
    )(queries, key_rows, value_rows, bias)


def backward_kernel(
    q_ref, k_ref, kt_ref, v_ref, do_ref, bias_ref, total_ref, center_ref,
    dqt_ref, dk_ref, dv_ref, dqt_sum,
):
    lane = lax.broadcasted_iota(jnp.int32, (1, PAIR), 1)
    step = pl.program_id(1)

    @pl.when(step == 0)
    def _():
        dqt_sum[...] = jnp.zeros_like(dqt_sum)

    q_pair, k_pair, v_pair, do_pair = q_ref[...], k_ref[...], v_ref[...], do_ref[...]
    bias = bias_ref[...]
    grad_k, grad_v = [], []
    for e in range(2):
        own = (lane // HEAD_DIM) == e
        head = slice(e * HEAD_DIM, (e + 1) * HEAD_DIM)
        q_own = jnp.where(own, q_pair, jnp.zeros_like(q_pair))
        do_own = jnp.where(own, do_pair, jnp.zeros_like(do_pair))
        prob = jnp.exp(mm_nt(k_pair, q_own) + bias - total_ref[0, e : e + 1, :])
        grad_prob = mm_nt(v_pair, do_own)
        grad_scores = (prob * (grad_prob - center_ref[0, e : e + 1, :])).astype(jnp.bfloat16)
        grad_v.append(mm(prob.astype(jnp.bfloat16), do_own))
        grad_k.append(mm(grad_scores, q_own))
        dqt_sum[head, :] += mm(kt_ref[head, :], grad_scores)
    dk_ref[...] = (grad_k[0] + grad_k[1]).astype(dk_ref.dtype)
    dv_ref[...] = (grad_v[0] + grad_v[1]).astype(dv_ref.dtype)

    @pl.when(step == pl.num_programs(1) - 1)
    def _():
        dqt_ref[...] = (dqt_sum[...] * SCALE).astype(dqt_ref.dtype)


def attend_backward(queries, key_rows, value_rows, grad_mixed, bias, total, center):
    rows, keys = queries.shape[0], key_rows.shape[0]
    block = min(512, keys)
    return pl.pallas_call(
        backward_kernel,
        grid=(PAIRS, keys // block),
        in_specs=[
            pl.BlockSpec((rows, PAIR), lambda p, i: (0, p)),
            pl.BlockSpec((block, PAIR), lambda p, i: (i, p)),
            pl.BlockSpec((PAIR, block), lambda p, i: (p, i)),
            pl.BlockSpec((block, PAIR), lambda p, i: (i, p)),
            pl.BlockSpec((rows, PAIR), lambda p, i: (0, p)),
            pl.BlockSpec((block, 1), lambda p, i: (i, 0)),
            pl.BlockSpec((1, 2, rows), lambda p, i: (p, 0, 0)),
            pl.BlockSpec((1, 2, rows), lambda p, i: (p, 0, 0)),
        ],
        out_specs=[
            pl.BlockSpec((PAIR, rows), lambda p, i: (p, 0)),
            pl.BlockSpec((block, PAIR), lambda p, i: (i, p)),
            pl.BlockSpec((block, PAIR), lambda p, i: (i, p)),
        ],
        out_shape=[
            jax.ShapeDtypeStruct((D, rows), jnp.bfloat16),
            jax.ShapeDtypeStruct((keys, D), jnp.bfloat16),
            jax.ShapeDtypeStruct((keys, D), jnp.bfloat16),
        ],
        scratch_shapes=[pltpu.VMEM((PAIR, rows), jnp.float32)],
        compiler_params=pltpu.CompilerParams(vmem_limit_bytes=VMEM_LIMIT),
        name="attend_backward",
    )(queries, key_rows, key_rows.T, value_rows, grad_mixed, bias, total, center)


def layer_norm(inputs, gain_vec, shift_vec):
    center = inputs - jnp.mean(inputs, axis=-1, keepdims=True)
    spread = jnp.mean(center * center, axis=-1, keepdims=True)
    return center * lax.rsqrt(spread + 1e-06) * gain_vec + shift_vec


def gelu_exact(inputs):
    return jax.nn.gelu(inputs, approximate=False)


def per_device(
    plan, batches,
    patches, patch_mask, clip_lengths, target_index, targets, out_grad,
    mask_embed, ln1_gain, ln1_shift, w_qkv, bias_q, bias_v, w_out, bias_out,
    ln2_gain, ln2_shift, w_up, bias_up, w_down, bias_down,
):
    f32 = jnp.float32
    clips, freq_rows, time_rows, width = patches.shape
    block_rows = freq_rows * time_rows
    tokens = clips * block_rows
    time_id = lax.axis_index("tm")
    part = time_id % plan.share
    clip = lax.axis_index("freq") * plan.blocks + time_id // plan.share
    length = lax.dynamic_index_in_dim(clip_lengths, clip, keepdims=False)
    groups = [
        [block * plan.share + j for j in range(plan.share)] for block in range(plan.blocks)
    ]

    masked_patches = jnp.where((patch_mask == 1)[..., None], mask_embed, patches)
    code = (target_index * 2 + patch_mask).reshape(clips, 1, block_rows)
    start_low, grad_low, code = exchange(plan, 0, masked_patches, out_grad, code)
    start = start_low.reshape(tokens, width).astype(f32)
    grad_down = grad_low.reshape(tokens, width)
    code = code.reshape(tokens)
    flat_mask = (code % 2 == 1)[:, None]
    target = code // 2

    def live(owner):
        shape = (clips, freq_rows, time_rows)
        blocks = lax.broadcasted_iota(jnp.int32, shape, 0) % plan.blocks
        step = lax.broadcasted_iota(jnp.int32, shape, 2)
        return (((blocks * plan.share + owner) * time_rows + step) < length).reshape(tokens)

    normed, first_back = jax.vjp(layer_norm, start, ln1_gain.astype(f32), ln1_shift.astype(f32))
    normed_low = normed.astype(jnp.bfloat16)
    project = mm(normed_low, w_qkv)
    queries = (project[:, :D] + bias_q.astype(f32)).astype(jnp.bfloat16)
    queries = (queries.astype(f32) * SCALE).astype(jnp.bfloat16)
    local_kv = jnp.concatenate(
        [project[:, D : 2 * D], project[:, 2 * D :] + bias_v.astype(f32)], axis=-1
    ).astype(jnp.bfloat16)
    full_kv = lax.all_gather(local_kv, "tm", axis=0, tiled=True, axis_index_groups=groups)
    key_rows, value_rows = full_kv[:, :D], full_kv[:, D:]
    usable = jnp.concatenate([live(j) for j in range(plan.share)])
    bias = jnp.where(usable, 0.0, DEAD).astype(f32)

    mixed_f, total = attend_forward(queries, key_rows, value_rows, bias[None, :])
    mixed = mixed_f.astype(jnp.bfloat16)
    middle = start + mm(mixed, w_out) + bias_out.astype(f32)
    second, second_back = jax.vjp(layer_norm, middle, ln2_gain.astype(f32), ln2_shift.astype(f32))
    second_low = second.astype(jnp.bfloat16)
    hidden_up = mm(second_low, w_up) + bias_up.astype(f32)
    activated_f, gelu_back = jax.vjp(gelu_exact, hidden_up)
    activated = activated_f.astype(jnp.bfloat16)
    result = middle + mm(activated, w_down) + bias_down.astype(f32)
    block_out = result.astype(jnp.bfloat16)
    grad_w_down = mm_tn(activated, grad_down)
    grad_bias_down = jnp.sum(grad_down.astype(f32), axis=0)
    grad_up = gelu_back(mm_nt(grad_down, w_down))[0].astype(jnp.bfloat16)
    grad_w_up = mm_tn(second_low, grad_up)
    grad_bias_up = jnp.sum(grad_up.astype(f32), axis=0)
    grad_middle_norm, grad_ln2_gain, grad_ln2_shift = second_back(mm_nt(grad_up, w_up))
    grad_middle = grad_down.astype(f32) + grad_middle_norm
    grad_branch = grad_middle.astype(jnp.bfloat16)
    grad_w_out = mm_tn(mixed, grad_branch)
    grad_bias_out = jnp.sum(grad_branch.astype(f32), axis=0)
    grad_mixed = mm_nt(grad_branch, w_out).astype(jnp.bfloat16)

    center = jnp.sum(
        (grad_mixed.astype(f32) * mixed_f).reshape(tokens, HEADS, HEAD_DIM), axis=-1
    ).T.reshape(PAIRS, 2, tokens)
    grad_q_t, grad_k, grad_v = attend_backward(
        queries, key_rows, value_rows, grad_mixed, bias[:, None], total, center
    )
    grad_kv = lax.psum_scatter(
        jnp.concatenate([grad_k, grad_v], axis=-1), "tm", scatter_dimension=0, tiled=True,
        axis_index_groups=groups,
    )
    grad_project = jnp.concatenate([grad_q_t.T, grad_kv], axis=-1)
    grad_w_qkv = mm_tn(normed_low, grad_project)
    grad_bias_q = jnp.sum(grad_project[:, :D].astype(f32), axis=0)
    grad_bias_v = jnp.sum(grad_project[:, 2 * D :].astype(f32), axis=0)
    grad_start_norm, grad_ln1_gain, grad_ln1_shift = first_back(mm_nt(grad_project, w_qkv))
    grad_start = grad_middle + grad_start_norm
    grad_mask_embed = jnp.sum(jnp.where(flat_mask, grad_start, 0.0), axis=0)
    input_grad = jnp.where(flat_mask, 0.0, grad_start).astype(jnp.bfloat16)

    own_targets = lax.dynamic_index_in_dim(targets, clip, keepdims=False)
    logits = mm_nt(block_out, own_targets)
    raised = jnp.exp(logits - jnp.max(logits, axis=-1, keepdims=True))
    cand_ids = lax.broadcasted_iota(jnp.int32, raised.shape, 1)
    hit = jnp.sum(jnp.where(cand_ids == target[:, None], raised, 0.0), axis=-1)
    picked = hit / jnp.sum(raised, axis=-1)
    counts = ((code % 2 == 1) & live(part)).astype(f32)
    slot = (jnp.arange(clips) == clip).astype(f32)
    score = jnp.concatenate([slot * jnp.sum(picked * counts), slot * jnp.sum(counts)])

    block_grid, input_grid = exchange(
        plan, 1, block_out.reshape(patches.shape), input_grad.reshape(patches.shape)
    )
    everywhere = ("freq", "tm", "batch")
    grad_w_out, grad_w_up, grad_w_down, grad_w_qkv = [
        g.astype(f32)
        for g in lax.psum(
            tuple(g.astype(jnp.bfloat16) for g in (grad_w_out, grad_w_up, grad_w_down, grad_w_qkv)),
            everywhere,
        )
    ]
    vectors = (
        grad_mask_embed, grad_ln1_gain, grad_ln1_shift, grad_bias_q, grad_bias_v, grad_bias_out,
        grad_ln2_gain, grad_ln2_shift, grad_bias_up, grad_bias_down,
    )
    batch_slot = (jnp.arange(batches) == lax.axis_index("batch")).astype(f32)
    packed = jnp.concatenate(vectors + ((batch_slot[:, None] * score[None, :]).reshape(-1),))
    packed = lax.psum(packed, everywhere)
    pieces, at = [], 0
    for vector in vectors:
        pieces.append(packed[at : at + vector.shape[0]])
        at += vector.shape[0]
    scores = lax.dynamic_index_in_dim(
        packed[at:].reshape(batches, 2, clips), lax.axis_index("batch"), keepdims=False
    )
    soft_accuracy = scores[0] / jnp.maximum(scores[1], 1.0)
    (grad_mask_embed, grad_ln1_gain, grad_ln1_shift, grad_bias_q, grad_bias_v, grad_bias_out,
     grad_ln2_gain, grad_ln2_shift, grad_bias_up, grad_bias_down) = pieces
    return (
        block_grid, input_grid, grad_mask_embed, grad_ln1_gain, grad_ln1_shift, grad_w_qkv,
        grad_bias_q, grad_bias_v, grad_w_out, grad_bias_out, grad_ln2_gain, grad_ln2_shift,
        grad_w_up, grad_bias_up, grad_w_down, grad_bias_down, soft_accuracy,
    )


def solution(mesh):
    rows = P("batch", "freq", "tm", None)
    whole = P()
    in_specs = (
        rows, P("batch", "freq", "tm"), P("batch"), P("batch", "freq", "tm"),
        P("batch", None, None), rows,
    ) + (whole,) * 14
    out_specs = (rows, rows) + (whole,) * 14 + (P("batch"),)

    def body(*args):
        plan = Plan(mesh, args[0].shape[0])
        return per_device(plan, mesh.shape["batch"], *args)

    return jax.shard_map(
        body, mesh=mesh, in_specs=in_specs, out_specs=out_specs, check_vma=False
    )
```

time: 1630 us -> 392 us (0.24)
  waiting for transfers between devices: 934 us -> 66.9 us
  local copies, waits for them, and re-layouts: 257 us -> 26.3 us
  matrix products: 229 us -> 50.5 us
  Pallas kernels: 0 us -> 143 us
  other arithmetic: 96.1 us -> 45.5 us
  blocking collectives: 71.1 us -> 38.5 us
    all_gather x8 -> x1, waiting for transfers between devices: 571 us -> 8.74 us  [per_device(): lax.all_gather(local_kv, 'tm', axis=0, tiled=True, axis_index_groups=groups)]
    reduce_scatter x4 -> x1, waiting for transfers between devices: 286 us -> 0.01 us  [per_device(): lax.psum_scatter(jnp.concatenate([grad_k, grad_v], axis=-1), 'tm', scatte...]
    dot_general x26 -> x13, matrix products: 226 us -> 50.5 us  [the longest x4 24.2 us: mm(): return jnp.dot(left_mat, right_mat, preferred_element_type=jnp.float32)]
    pallas_call x0 -> x4, Pallas kernels: none -> 143 us  [the longest x2 79.3 us: exchange(): pl.pallas_call(functools.partial(exchange_kernel, plan, count), out_shape...]
    slice x13 -> x4, local copies, waits for them, and re-layouts: 92.4 us -> 1.31 us  [the longest x2 1.21 us: per_device(): pieces.append(packed[at:at + vector.shape[0]])]
    all_gather x8 -> x0, local copies, waits for them, and re-layouts: 49.9 us -> none  [the longest x2 18.1 us: gather_again(): return lax.all_gather(wider, 'tm', axis=2, tiled=True)]
    concatenate x4 -> x6, local copies, waits for them, and re-layouts: 38.9 us -> 0.83 us  [the longest x5 0.82 us: per_device(): usable = jnp.concatenate([live(j) for j in range(plan.share)])]
    psum x2 -> x1, blocking collectives: 71.1 us -> 38.5 us  [per_device(): packed = lax.psum(packed, everywhere)]
  transfers between devices with their start and end apart: 13 -> 3, of which waited for: 13 -> 2; matrix products, arithmetic and copies ran while one was open for 3% -> 11% of each run, Pallas kernels for 0% -> 11%
where the time goes in v1:
time: 392 us; the launch traced here: 386 us
  Pallas kernels  143 us (36%)
  waiting for transfers between devices  66.9 us (17%)
  matrix products  50.5 us (13%)
  other arithmetic  45.5 us (12%)
  blocking collectives  38.5 us (10%)
  local copies, waits for them, and re-layouts  26.3 us (7%)
  between operations  14.6 us (4%)
    pallas_call x2, Pallas kernels, exchange(): pl.pallas_call(functools.partial(exchange_kernel, plan, count), out_shape...  79.3 us
    psum x1, waiting for transfers between devices, per_device(): lax.psum(tuple((g.astype(jnp.bfloat16) for g in (grad_w_out, grad_w_up, g...  58.1 us
    psum x1, blocking collectives, per_device(): packed = lax.psum(packed, everywhere)  38.5 us
    pallas_call x1, Pallas kernels, attend_backward(): pl.pallas_call(backward_kernel, grid=(PAIRS, keys // block), in_specs=[pl...  38.2 us
    pallas_call x1, Pallas kernels, attend_forward(): pl.pallas_call(forward_kernel, grid=(PAIRS, rows // block), in_specs=[pl....  25.9 us
    dot_general x4, matrix products, mm(): return jnp.dot(left_mat, right_mat, preferred_element_type=jnp.float32)  24.2 us
    dot_general x5, matrix products, mm_nt(): lax.dot_general(left_mat, right_mat, (((1,), (1,)), ((), ())), preferred_...  13.8 us
    dot_general x4, matrix products, mm_tn(): lax.dot_general(left_mat, right_mat, (((0,), (0,)), ((), ())), preferred_...  12.5 us
  transfers between devices with their start and end apart: 3, of which 2 were waited for; matrix products, arithmetic and copies ran while one was open for 11% of the time, Pallas kernels for 11%

profile of v1, /device:TPU:25, one launch (start us, length us, event | category | flops | bytes accessed | tf_op | source)
XLA Modules:
  0.0 386.2 jit_solution(4111646465846599171)
XLA Ops:
  9.5 2.2 broadcast_select_fusion.refs_0_
  11.7 37.9 %exchange.2 = (bf16[8,4,32,384]{3,2,1,0:T(8,128)(2,1)}, bf16[8,4,32,384]{3,2,1,0:T(8,128)(2,1)}, s32[8,1,128]{2,1,0:T(1,128)}) custom-call(bf16[8,4,32,384]{3,2,1,0:T(8,128)(2,1)} %broadcast_select_fusion.refs_0_, bf16[8,4,32,384]{3,2,1,0:T(8,128)(2,1)} %refs_1_.1, s32[8,1,128]{2,1,0:T(1,128)} %reshape.511.refs_2_), custom_call_target="tpu_custom_call" | custom-call | tf_op jit(solution)/shard_map/exchange/pallas_call | solution.py:86
  49.6 1.5 convert_reduce_fusion.1
  51.1 1.6 fusion.18
  53.4 1.4 fusion.54
  63.8 8.7 %all-gather.2.cloned.1.call-done = bf16[2048,768]{1,0:T(8,128)(2,1)} async-done(((bf16[1024,768]{1,0:T(8,128)(2,1)}), bf16[2048,768]{1,0:T(8,128)(2,1)}) %all-gather.2.cloned.1.call-update) | async-done | bytes 3145744 | tf_op jit(solution)/shard_map/all_gather | solution.py:257
  72.5 4.3 %slice_bitcast_fusion = (bf16[384,2048]{0,1:T(8,128)(2,1)}, bf16[2048,384]{1,0:T(8,128)(2,1)}, bf16[2048,384]{1,0:T(8,128)(2,1)}) fusion(bf16[2048,768]{1,0:T(8,128)(2,1)} %all-gather.2.cloned.1.call-done), kind=kLoop, calls=%fused_computation.144 | loop fusion | bytes 7864320 | tf_op jit(solution)/shard_map/transpose | solution.py:203
  76.8 25.9 %attend_forward.1 = (f32[1024,384]{1,0:T(8,128)}, f32[3,2,1024]{2,1,0:T(2,128)}) custom-call(bf16[1024,384]{1,0:T(8,128)(2,1)} %get-tuple-element.61.q_ref, bf16[2048,384]{1,0:T(8,128)(2,1)} %get-tuple-element.64.k_ref, bf16[2048,384]{1,0:T(8,128)(2,1)} %get-tuple-element.63.v_ref, f32[1,2048]{1,0:T(1,128)} %add_select_fusion.bias_ref), custom_call_target="tpu_custom_call" | custom-call | tf_op jit(solution)/shard_map/attend_forward/pallas_call | solution.py:119
  102.7 2.2 fusion.52
  105.6 16.2 %multiply_convert_fusion = (bf16[1024,1536]{1,0:T(8,128)(2,1)}, f32[1024,1536]{1,0:T(8,128)S(1)}, f32[1024,1536]{1,0:T(8,128)S(1)}) fusion(f32[1536]{0:T(1024)S(1)} %copy-done.39, bf16[384,1536]{1,0:T(8,128)(2,1)S(1)} %copy-done, f32[1024,384]{1,0:T(8,128)S(1)} %get-tuple-element.77, f32[384]{0:T(512)S(1)} %copy-done.32, f32[384]{0:T(512)S(1)} %copy-done.23, ...), kind=kOutput, calls=%fused_computation.4 | convolution fusion | flops 1313734656 | bytes 18498560 | tf_op jit(solution)/shard_map/dot_general | solution.py:22
  121.8 4.2 %convert_reduce_fusion = (f32[1536]{0:T(1024)}, bf16[1024,1536]{1,0:T(8,128)(2,1)S(1)}) fusion(f32[1024,1536]{1,0:T(8,128)S(1)} %get-tuple-element.59, bf16[1024,384]{1,0:T(8,128)(2,1)S(1)} %bitcast.72, bf16[1536,384]{1,0:T(8,128)(2,1)S(1)} %copy-done.60, f32[1024,1536]{1,0:T(8,128)S(1)} %get-tuple-element.78, f32[1536]{0:T(1024)S(1)} %copy-done.39), kind=kOutput, calls=%fused_computation.2 | convolution fusion | flops 1234696704 | bytes 17707008 | tf_op jit(solution)/shard_map/dot_general | solution.py:26
  126.1 2.6 multiply_reduce_fusion
  131.4 2.1 convert_multiply_fusion
  133.5 3.1 copy.48
  136.6 2.2 reduce_sum.211
  140.2 2.6 copy.49.kt_ref
  142.8 38.2 %attend_backward.1 = (bf16[384,1024]{1,0:T(8,128)(2,1)}, bf16[2048,384]{1,0:T(8,128)(2,1)}, bf16[2048,384]{1,0:T(8,128)(2,1)}) custom-call(bf16[1024,384]{1,0:T(8,128)(2,1)} %get-tuple-element.61.q_ref, bf16[2048,384]{1,0:T(8,128)(2,1)} %get-tuple-element.64.k_ref, bf16[384,2048]{1,0:T(8,128)(2,1)} %copy.49.kt_ref, ...), custom_call_target="tpu_custom_call" | custom-call | tf_op jit(solution)/shard_map/attend_backward/pallas_call | solution.py:177
  180.9 3.8 pad_maximum_fusion
  188.8 1.9 convert_reduce_fusion.2
  193.2 2.3 copy.50
  195.5 4.3 %add_convert_fusion.1 = bf16[1024,384]{1,0:T(8,128)(2,1)S(1)} fusion(f32[1024,384]{1,0:T(8,128)S(1)} %get-tuple-element.77, bf16[1024,1536]{1,0:T(8,128)(2,1)} %get-tuple-element.58, bf16[1536,384]{1,0:T(8,128)(2,1)} %param.38, f32[384]{0:T(512)} %convert_element_type.150), kind=kOutput, calls=%fused_computation.58 | convolution fusion | flops 1209139200 | bytes 6686208 | tf_op jit(solution)/shard_map/dot_general | solution.py:22
  206.9 2.0 convert_reduce_fusion.5
  208.8 2.9 convolution_convert_fusion.4
  211.8 4.9 %convolution_convert_fusion.1 = bf16[1536,384]{1,0:T(8,128)(2,1)} fusion(bf16[1024,1536]{1,0:T(8,128)(2,1)} %get-tuple-element.58, bf16[1024,384]{1,0:T(8,128)(2,1)S(1)} %bitcast.73), kind=kOutput, calls=%fused_computation.20 | convolution fusion | flops 1208549376 | bytes 5111808 | tf_op jit(solution)/shard_map/dot_general | solution.py:32
  216.7 2.6 convolution_convert_fusion.2
  219.3 3.6 fusion.47
  226.4 2.1 convolution_convert_fusion
  230.0 38.5 %psum.35 = f32[5024]{0:T(1024)S(1)} all-reduce(f32[5024]{0:T(1024)S(1)} %constant_dynamic-update-slice_fusion), channel_id=1, replica_groups=mesh['freq'=2,'tm'=8,'batch'=2] {'freq','tm','batch'}, use_global_device_ids=true, to_apply=%region_25.26 | all-reduce | flops 5024 | bytes 40192 | tf_op jit(solution)/shard_map/psum | solution.py:330
  270.4 41.4 %exchange.3 = (bf16[8,4,32,384]{3,2,1,0:T(8,128)(2,1)}, bf16[8,4,32,384]{3,2,1,0:T(8,128)(2,1)}) custom-call(bf16[8,4,32,384]{3,2,1,0:T(8,128)(2,1)} %bitcast.75, bf16[8,4,32,384]{3,2,1,0:T(8,128)(2,1)} %bitcast.78), custom_call_target="tpu_custom_call" | custom-call | tf_op jit(solution)/shard_map/exchange/pallas_call | solution.py:86
  313.0 58.1 %all-reduce.3.cloned.1.call-done = (bf16[384,1152]{1,0:T(8,128)(2,1)}, bf16[384,384]{1,0:T(8,128)(2,1)}, bf16[384,1536]{1,0:T(8,128)(2,1)}, bf16[1536,384]{1,0:T(8,128)(2,1)}) async-done(((bf16[384,1152]{1,0:T(8,128)(2,1)}, bf16[384,384]{1,0:T(8,128)(2,1)}, bf16[384,1536]{1,0:T(8,128)(2,1)}, bf16[1536,384]{1,0:T(8,128)(2,1)}), (bf16[384,1152]{1,0:T(8,128)(2,1)}, bf16[384,384]{1,0:T(8,128)(2,1)}, ...) | async-done | bytes 3538960 | tf_op jit(solution)/shard_map/psum | solution.py:319
  371.1 3.1 convert_element_type.170
  374.2 1.6 convert_element_type.172
  (216 shorter events, 41.7 us)
Async XLA Ops:
  7.2 98.1 %copy-start = (bf16[384,1536]{1,0:T(8,128)(2,1)S(1)}, bf16[384,1536]{1,0:T(8,128)(2,1)}, u32[]{:S(2)}) copy-start(bf16[384,1536]{1,0:T(8,128)(2,1)} %param.36) | copy-start | bytes 3538948
  7.2 65.3 %all-gather.2.cloned.1.call-start = ((), (), s32[]{:S(2)}) async-start(), calls=%async_computation.1 | async-start | bytes 4718592 | tf_op jit(solution)/shard_map/all_gather | solution.py:257
  11.7 41.1 %copy-start.52 = (bf16[384]{0:T(512)(128)(2,1)S(1)}, bf16[384]{0:T(512)(128)(2,1)}, u32[]{:S(2)}) copy-start(bf16[384]{0:T(512)(128)(2,1)} %param.27) | copy-start | bytes 2308
  11.7 41.2 %copy-start.53 = (bf16[384]{0:T(512)(128)(2,1)S(1)}, bf16[384]{0:T(512)(128)(2,1)}, u32[]{:S(2)}) copy-start(bf16[384]{0:T(512)(128)(2,1)} %param.28) | copy-start | bytes 2308
  11.7 41.2 %copy-start.54 = (bf16[384]{0:T(512)(128)(2,1)S(1)}, bf16[384]{0:T(512)(128)(2,1)}, u32[]{:S(2)}) copy-start(bf16[384]{0:T(512)(128)(2,1)} %param.30) | copy-start | bytes 2308
  11.7 41.2 %copy-start.55 = (bf16[384]{0:T(512)(128)(2,1)S(1)}, bf16[384]{0:T(512)(128)(2,1)}, u32[]{:S(2)}) copy-start(bf16[384]{0:T(512)(128)(2,1)} %param.31) | copy-start | bytes 2308
  49.6 3.3 copy-start.1
  49.6 3.7 copy-start.17
  52.8 2.0 copy-start.27
  57.4 2.4 copy-start.56
  57.4 2.4 copy-start.57
  57.4 3.0 copy-start.42
  57.4 3.6 copy-start.58
  57.4 161.8 %reduce-scatter.2.cloned.1.call-start = ((), (), s32[]{:S(2)}) async-start(), calls=%async_computation.2 | async-start | bytes 4718592 | tf_op jit(solution)/shard_map/reduce_scatter | solution.py:290
  58.6 2.9 copy-start.45
  58.7 2.9 copy-start.47
  76.8 25.9 %copy-start.15 = (bf16[384,384]{1,0:T(8,128)(2,1)S(1)}, bf16[384,384]{1,0:T(8,128)(2,1)}, u32[]{:S(2)}) copy-start(bf16[384,384]{1,0:T(8,128)(2,1)} %param.32) | copy-start | bytes 884740
  105.6 16.2 %copy-start.5 = (bf16[8,4,32,384]{3,2,1,0:T(8,128)(2,1)S(1)}, bf16[8,4,32,384]{3,2,1,0:T(8,128)(2,1)}, u32[]{:S(2)}) copy-start(bf16[8,4,32,384]{3,2,1,0:T(8,128)(2,1)} %get-tuple-element.30) | copy-start | bytes 2359300
  105.6 16.2 %copy-start.60 = (bf16[1536,384]{1,0:T(8,128)(2,1)S(1)}, bf16[1536,384]{1,0:T(8,128)(2,1)}, u32[]{:S(2)}) copy-start(bf16[1536,384]{1,0:T(8,128)(2,1)} %param.38) | copy-start | bytes 3538948
  126.1 2.6 copy-start.11
  130.5 2.9 copy-start.8
  184.8 186.3 %all-reduce.3.cloned.1.call-start = ((), (), s32[]{:S(2)}) async-start(), calls=%async_computation.3 | async-start | bytes 7077888 | tf_op jit(solution)/shard_map/psum | solution.py:319
  195.5 6.5 %copy-start.35 = (s32[1024]{0:T(1024)S(1)}, s32[1024]{0:T(1024)}, u32[]{:S(2)}) copy-start(s32[1024]{0:T(1024)} %add_select_fusion.1) | copy-start | bytes 12292
  200.7 4.3 %copy-start.59 = (f32[2]{0:T(128)S(1)}, f32[2]{0:T(128)}, u32[]{:S(2)}) copy-start(f32[2]{0:T(128)} %compare_convert_fusion) | copy-start | bytes 28
  206.9 4.9 %copy-start.6 = (bf16[8,4,32,384]{3,2,1,0:T(8,128)(2,1)S(1)}, bf16[8,4,32,384]{3,2,1,0:T(8,128)(2,1)}, u32[]{:S(2)}) copy-start(bf16[8,4,32,384]{3,2,1,0:T(8,128)(2,1)} %get-tuple-element.30) | copy-start | bytes 2359300
  211.8 4.9 %copy-start.12 = (bf16[1024,1536]{1,0:T(8,128)(2,1)S(1)}, bf16[1024,1536]{1,0:T(8,128)(2,1)}, u32[]{:S(2)}) copy-start(bf16[1024,1536]{1,0:T(8,128)(2,1)} %copy-done.11) | copy-start | bytes 9437188
  211.8 4.9 %copy-start.24 = (f32[384]{0:T(512)S(1)}, f32[384]{0:T(512)}, u32[]{:S(2)}) copy-start(f32[384]{0:T(512)} %convert_element_type.145) | copy-start | bytes 4612
  211.8 4.9 %copy-start.33 = (f32[384]{0:T(512)S(1)}, f32[384]{0:T(512)}, u32[]{:S(2)}) copy-start(f32[384]{0:T(512)} %convert_element_type.146) | copy-start | bytes 4612
  219.3 3.6 copy-start.28
  219.3 3.6 copy-start.31
  371.1 3.1 copy-start.16
  375.8 2.2 copy-start.20
  (34 other events, 46.7 us)
Sparse Core Ops, SparseCore 0:
  57.6 14.8 all-gather.1
  184.9 12.0 reduce-scatter.1
  228.7 142.3 all-reduce.2

commit v2 on v1

v2 whole, which is shorter than its diff:
```python
import functools

import jax
import jax.numpy as jnp
from jax import lax
from jax.experimental import pallas as pl
from jax.experimental.pallas import tpu as pltpu
from jax.sharding import PartitionSpec as P

D = 384
FF = 1536
HEADS = 6
HEAD_DIM = 64
PAIRS = HEADS // 2
PAIR = 2 * HEAD_DIM
SCALE = HEAD_DIM ** (-0.5)
DEAD = -1e9
EPS = 1e-06
VEC_ROWS = 16
MESH = pl.DeviceIdType.MESH
VMEM_LIMIT = 60 * 2**20
ANY = pl.BlockSpec(memory_space=pl.ANY)
VMEM = pl.BlockSpec(memory_space=pltpu.VMEM)
BF16 = jnp.bfloat16
F32 = jnp.float32


def mm(left_mat, right_mat):
    return jnp.dot(left_mat, right_mat, preferred_element_type=F32)


def mm_nt(left_mat, right_mat):
    return lax.dot_general(
        left_mat, right_mat, (((1,), (1,)), ((), ())), preferred_element_type=F32
    )


def mm_tn(left_mat, right_mat):
    return lax.dot_general(
        left_mat, right_mat, (((0,), (0,)), ((), ())), preferred_element_type=F32
    )


def row(ref):
    return ref[...].astype(F32).reshape(1, -1)


def normalize(rows):
    center = rows - jnp.mean(rows, axis=-1, keepdims=True)
    scale = lax.rsqrt(jnp.mean(center * center, axis=-1, keepdims=True) + EPS)
    return center * scale, scale


def normalize_back(grad_hat, hat, scale):
    first = jnp.mean(grad_hat, axis=-1, keepdims=True)
    second = jnp.mean(grad_hat * hat, axis=-1, keepdims=True)
    return scale * (grad_hat - first - hat * second)


def sum_rows(rows):
    return jnp.sum(rows, axis=0, keepdims=True)


def columns(ints):
    freq_rows, time_rows = ints.shape
    shape = (time_rows, time_rows)
    eye = lax.broadcasted_iota(jnp.int32, shape, 0) == lax.broadcasted_iota(jnp.int32, shape, 1)
    parts = [
        jnp.sum(jnp.where(eye, ints[f : f + 1, :], 0), axis=1, keepdims=True)
        for f in range(freq_rows)
    ]
    return jnp.concatenate(parts, axis=0)


class Plan:
    def __init__(self, mesh, patches):
        self.freq = mesh.shape["freq"]
        self.tm = mesh.shape["tm"]
        self.batch = mesh.shape["batch"]
        self.clips, self.freq_rows, self.time_rows, _ = patches.shape
        self.share = self.freq * self.tm // self.clips
        self.blocks = self.tm // self.share
        self.block_rows = self.freq_rows * self.time_rows
        self.rows = self.clips * self.block_rows
        self.keys = self.share * self.rows
        assert self.freq * self.blocks == self.clips and self.blocks * self.share == self.tm

    def place(self):
        time_id = lax.axis_index("tm")
        return lax.axis_index("freq") * self.blocks + time_id // self.share, time_id % self.share

    def member(self, member, part):
        return {
            "freq": member // self.blocks,
            "tm": (member % self.blocks) * self.share + part,
        }

    def sharer(self, part):
        time_id = lax.axis_index("tm")
        return {"tm": time_id // self.share * self.share + part}

    def key_time(self, place):
        part = place // self.rows
        block = (place // self.block_rows) % self.clips % self.blocks
        return (block * self.share + part) * self.time_rows + place % self.time_rows


def greet(devices):
    barrier = pltpu.get_barrier_semaphore()
    for device in devices:
        pl.semaphore_signal(barrier, inc=1, device_id=device, device_id_type=MESH)
    pl.semaphore_wait(barrier, len(devices))


def remote(src, dst, send_sem, recv_sem, device):
    return pltpu.make_async_remote_copy(
        src_ref=src, dst_ref=dst, send_sem=send_sem, recv_sem=recv_sem,
        device_id=device, device_id_type=MESH,
    )


def project_kernel(
    plan, patches, mask, target, embed, gain, shift, w_ref, bias_q, bias_v,
    start_out, q_out, kv_out, mask_out, target_out,
    taken, mask_in, target_in, start_buf, q_buf, kv_buf,
    send_sem, recv_sem, local_sem, kv_send, kv_recv, out_sem,
):
    me, part = plan.place()
    n = plan.clips
    peers = [lax.rem(me + step, n) for step in range(n)]
    sharers = [lax.rem(part + step, plan.share) for step in range(plan.share)]
    greet(
        [plan.member(peers[step], part) for step in range(1, n)]
        + [plan.sharer(sharers[step]) for step in range(1, plan.share)]
    )
    streams = ((mask, mask_in), (target, target_in), (patches, taken))
    arrivals = []
    for step in range(n):
        copies = []
        for i, (src, dst) in enumerate(streams):
            if step == 0:
                copy = pltpu.make_async_copy(src.at[me], dst.at[me], local_sem.at[i])
            else:
                copy = remote(
                    src.at[peers[step]], dst.at[me], send_sem.at[i, step], recv_sem.at[i, step],
                    plan.member(peers[step], part),
                )
            copy.start()
            copies.append(copy)
        arrivals.append(copies)
    gain_row, shift_row, embed_row = row(gain), row(shift), row(embed)
    bias_q_row, bias_v_row = row(bias_q), row(bias_v)
    waits = []
    for step in range(n):
        source = lax.rem(me + n - step, n)
        for copy in arrivals[step]:
            if step == 0:
                copy.wait()
            else:
                copy.wait_recv()
        masked = columns(mask_in[source]) == 1
        rows = taken[source].astype(F32)
        start = jnp.where(masked, embed_row, rows)
        start_buf[source] = start.astype(BF16)
        hat, _ = normalize(start)
        normed = (hat * gain_row + shift_row).astype(BF16)
        project = mm(normed, w_ref[...])
        queries = (project[:, :D] + bias_q_row).astype(BF16)
        q_buf[source] = (queries.astype(F32) * SCALE).astype(BF16)
        kv_buf[source, :, :D] = project[:, D : 2 * D].astype(BF16)
        kv_buf[source, :, D:] = (project[:, 2 * D :] + bias_v_row).astype(BF16)
        for other in range(1, plan.share):
            copy = remote(
                kv_buf.at[source], kv_out.at[part, source], kv_send.at[other, step],
                kv_recv.at[other, step], plan.sharer(sharers[other]),
            )
            copy.start()
            waits.append(copy)
        for i, (src, dst) in enumerate(
            (
                (kv_buf.at[source], kv_out.at[part, source]),
                (q_buf.at[source], q_out.at[source]),
                (start_buf.at[source], start_out.at[source]),
            )
        ):
            copy = pltpu.make_async_copy(src, dst, out_sem.at[i, step])
            copy.start()
            waits.append(copy)
    for i, (src, dst) in enumerate(((mask_in, mask_out), (target_in, target_out))):
        copy = pltpu.make_async_copy(src, dst, local_sem.at[i])
        copy.start()
        waits.append(copy)
    for step in range(1, n):
        for copy in arrivals[step]:
            copy.wait_send()
    for copy in waits:
        copy.wait()


def project_rows(plan, patches, mask, target, embed, gain, shift, w_qkv, bias_q, bias_v):
    n, rows = plan.clips, plan.block_rows
    ints = jax.ShapeDtypeStruct(mask.shape, jnp.int32)
    dma = pltpu.SemaphoreType.DMA
    return pl.pallas_call(
        functools.partial(project_kernel, plan),
        out_shape=[
            jax.ShapeDtypeStruct((n, rows, D), BF16),
            jax.ShapeDtypeStruct((n, rows, D), BF16),
            jax.ShapeDtypeStruct((plan.share, n, rows, 2 * D), BF16),
            ints,
            ints,
        ],
        in_specs=[ANY] * 3 + [VMEM] * 6,
        out_specs=[ANY] * 5,
        scratch_shapes=[
            pltpu.VMEM(patches.shape, BF16),
            pltpu.VMEM(mask.shape, jnp.int32),
            pltpu.VMEM(mask.shape, jnp.int32),
            pltpu.VMEM((n, rows, D), BF16),
            pltpu.VMEM((n, rows, D), BF16),
            pltpu.VMEM((n, rows, 2 * D), BF16),
            dma((3, n)), dma((3, n)), dma((3,)),
            dma((plan.share, n)), dma((plan.share, n)), dma((3, n)),
        ],
        compiler_params=pltpu.CompilerParams(
            collective_id=0, has_side_effects=True, vmem_limit_bytes=VMEM_LIMIT
        ),
        name="project_rows",
    )(patches, mask, target, embed, gain, shift, w_qkv, bias_q, bias_v)


def forward_kernel(plan, place, q_ref, k_ref, v_ref, mixed_ref, total_ref):
    lane = lax.broadcasted_iota(jnp.int32, (1, PAIR), 1)
    q_pair, k_pair, v_pair = q_ref[...], k_ref[...], v_ref[...]
    key_id = lax.broadcasted_iota(jnp.int32, (1, plan.keys), 1)
    bias = jnp.where(plan.key_time(key_id) < place[1], 0.0, DEAD)
    outs = []
    for e in range(2):
        own = (lane // HEAD_DIM) == e
        scores = mm_nt(jnp.where(own, q_pair, jnp.zeros_like(q_pair)), k_pair) + bias
        row_max = jnp.max(scores, axis=1, keepdims=True)
        raised = jnp.exp(scores - row_max)
        row_total = jnp.sum(raised, axis=1, keepdims=True)
        outs.append(mm(raised.astype(BF16), v_pair) / row_total)
        total_ref[0, e, :] = (row_max + jnp.log(row_total))[:, 0]
    mixed_ref[...] = jnp.where(lane < HEAD_DIM, outs[0], outs[1])


def attend_forward(plan, place, queries, kv):
    rows, keys = plan.rows, plan.keys
    block = min(256, rows)
    return pl.pallas_call(
        functools.partial(forward_kernel, plan),
        grid_spec=pltpu.PrefetchScalarGridSpec(
            num_scalar_prefetch=1,
            grid=(PAIRS, rows // block),
            in_specs=[
                pl.BlockSpec((block, PAIR), lambda p, i, s: (i, p)),
                pl.BlockSpec((keys, PAIR), lambda p, i, s: (0, p)),
                pl.BlockSpec((keys, PAIR), lambda p, i, s: (0, PAIRS + p)),
            ],
            out_specs=[
                pl.BlockSpec((block, PAIR), lambda p, i, s: (i, p)),
                pl.BlockSpec((1, 2, block), lambda p, i, s: (p, 0, i)),
            ],
        ),
        out_shape=[
            jax.ShapeDtypeStruct((rows, D), F32),
            jax.ShapeDtypeStruct((PAIRS, 2, rows), F32),
        ],
        compiler_params=pltpu.CompilerParams(vmem_limit_bytes=VMEM_LIMIT),
        cost_estimate=pl.CostEstimate(
            flops=4 * rows * keys * D, bytes_accessed=8 * rows * D, transcendentals=rows * keys
        ),
        name="attend_forward",
    )(place, queries, kv, kv)


def gelu_parts(rows):
    lower = 0.5 * (1.0 + lax.erf(rows * 0.7071067811865476))
    slope = lower + rows * (jnp.exp(-0.5 * rows * rows) * 0.3989422804014327)
    return rows * lower, slope


def feed_kernel(
    plan, place, mixed, start, grad, mask, target, targets, w_out, bias_out, gain, shift,
    w_up, bias_up, w_down, bias_down,
    block_out, grad_middle, grad_mixed, center, grad_w_up, grad_w_down, grad_w_out, vec,
    middle, second, down_sum, second_sum, act_buf, up_buf,
):
    step = pl.program_id(0)
    steps = pl.num_programs(0)
    rows = plan.rows
    tile = min(256, rows)
    tiles = [slice(i * tile, (i + 1) * tile) for i in range(rows // tile)]
    gain_row, shift_row = row(gain), row(shift)

    @pl.when(step == 0)
    def _():
        vec[...] = jnp.zeros_like(vec)
        for part in tiles:
            rows_in = start[part, :].astype(F32) + mm(mixed[part, :].astype(BF16), w_out[...])
            rows_in = rows_in + row(bias_out)
            middle[part, :] = rows_in
            hat, _ = normalize(rows_in)
            second[part, :] = (hat * gain_row + shift_row).astype(BF16)
        down_sum[...] = jnp.zeros_like(down_sum)
        second_sum[...] = jnp.zeros_like(second_sum)

    bias_row = row(bias_up.at[0])
    for part in tiles:
        hidden = mm(second[part, :], w_up[...]) + bias_row
        active, slope = gelu_parts(hidden)
        active = active.astype(BF16)
        act_buf[part, :] = active
        down_sum[part, :] += mm(active, w_down[...])
        grad_up = (mm_nt(grad[part, :], w_down[...]) * slope).astype(BF16)
        up_buf[part, :] = grad_up
        second_sum[part, :] += mm_nt(grad_up, w_up[...])
    grad_w_down[...] = mm_tn(act_buf[...], grad[...])
    grad_w_up[...] = mm_tn(second[...], up_buf[...])
    vec[pl.ds(9 + step, 1), :] = sum_rows(up_buf[...].astype(F32))

    @pl.when(step == steps - 1)
    def _():
        clip, length, batch = place[0], place[1], place[2]
        head_of = lax.broadcasted_iota(jnp.int32, (8, D), 1) // HEAD_DIM
        picks = (head_of == lax.broadcasted_iota(jnp.int32, (8, D), 0)).astype(BF16)
        cand = lax.broadcasted_iota(jnp.int32, (1, targets.shape[1]), 1)
        vec[8:9, :] = sum_rows(grad[...].astype(F32))
        total_hit = jnp.zeros((1, 1), F32)
        total_count = jnp.zeros((1, 1), F32)
        per_tile = tile // plan.block_rows
        for t, part in enumerate(tiles):
            result = middle[part, :] + down_sum[part, :] + row(bias_down)
            result = result.astype(BF16)
            block_out[part, :] = result
            hat, scale = normalize(middle[part, :])
            grad_second = second_sum[part, :]
            vec[6:7, :] += sum_rows(grad_second * hat)
            vec[7:8, :] += sum_rows(grad_second)
            back = normalize_back(grad_second * gain_row, hat, scale)
            back = grad[part, :].astype(F32) + back
            grad_middle[part, :] = back
            branch = back.astype(BF16)
            act_buf[part, :] = branch
            vec[5:6, :] += sum_rows(branch.astype(F32))
            down = mm_nt(branch, w_out[...]).astype(BF16)
            grad_mixed[part, :] = down
            product = down.astype(F32) * mixed[part, :]
            high = product.astype(BF16)
            low = (product - high.astype(F32)).astype(BF16)
            center[:, part] = mm_nt(picks, high) + mm_nt(picks, low)
            logits = mm_nt(result, targets[0])
            raised = jnp.exp(logits - jnp.max(logits, axis=1, keepdims=True))
            sources = range(t * per_tile, (t + 1) * per_tile)
            target_col = jnp.concatenate([columns(target[s]) for s in sources], axis=0)
            mask_col = jnp.concatenate([columns(mask[s]) for s in sources], axis=0)
            hit = jnp.sum(jnp.where(cand == target_col, raised, 0.0), axis=1, keepdims=True)
            hit = hit / jnp.sum(raised, axis=1, keepdims=True)
            ids = lax.broadcasted_iota(jnp.int32, (tile, 1), 0) + t * tile + place[3] * rows
            counted = jnp.where((plan.key_time(ids) < length) & (mask_col == 1), 1.0, 0.0)
            total_hit += jnp.sum(hit * counted, axis=0, keepdims=True)
            total_count += jnp.sum(counted, axis=0, keepdims=True)
        grad_w_out[...] = mm_tn(mixed[...].astype(BF16), act_buf[...])
        lane = lax.broadcasted_iota(jnp.int32, (1, D), 1)
        slot = batch * 2 * plan.clips + clip
        scores = jnp.where(lane == slot, total_hit, 0.0)
        vec[13:14, :] = scores + jnp.where(lane == slot + plan.clips, total_count, 0.0)


def feed_forward(
    plan, place, mixed, start, grad, mask, target, targets, w_out, bias_out, gain, shift,
    w_up, bias_up, w_down, bias_down,
):
    rows = plan.rows
    steps = FF // D

    def full(shape):
        return pl.BlockSpec(shape, lambda i, s: (0,) * len(shape))

    return pl.pallas_call(
        functools.partial(feed_kernel, plan),
        grid_spec=pltpu.PrefetchScalarGridSpec(
            num_scalar_prefetch=1,
            grid=(steps,),
            in_specs=[
                full((rows, D)), full((rows, D)), full((rows, D)),
                full(mask.shape), full(mask.shape),
                pl.BlockSpec((1,) + targets.shape[1:], lambda i, s: (s[0], 0, 0)),
                full((D, D)), full((D,)), full((D,)), full((D,)),
                pl.BlockSpec((D, D), lambda i, s: (0, i)),
                pl.BlockSpec((1, 1, D), lambda i, s: (i, 0, 0)),
                pl.BlockSpec((D, D), lambda i, s: (i, 0)),
                full((D,)),
            ],
            out_specs=[
                full((rows, D)), full((rows, D)), full((rows, D)), full((8, rows)),
                pl.BlockSpec((D, D), lambda i, s: (0, i)),
                pl.BlockSpec((D, D), lambda i, s: (i, 0)),
                full((D, D)), full((VEC_ROWS, D)),
            ],
            scratch_shapes=[
                pltpu.VMEM((rows, D), F32), pltpu.VMEM((rows, D), BF16),
                pltpu.VMEM((rows, D), F32), pltpu.VMEM((rows, D), F32),
                pltpu.VMEM((rows, D), BF16), pltpu.VMEM((rows, D), BF16),
            ],
        ),
        out_shape=[
            jax.ShapeDtypeStruct((rows, D), BF16),
            jax.ShapeDtypeStruct((rows, D), F32),
            jax.ShapeDtypeStruct((rows, D), BF16),
            jax.ShapeDtypeStruct((8, rows), F32),
            jax.ShapeDtypeStruct((D, FF), F32),
            jax.ShapeDtypeStruct((FF, D), F32),
            jax.ShapeDtypeStruct((D, D), F32),
            jax.ShapeDtypeStruct((VEC_ROWS, D), F32),
        ],
        compiler_params=pltpu.CompilerParams(vmem_limit_bytes=VMEM_LIMIT),
        cost_estimate=pl.CostEstimate(
            flops=12 * rows * FF * D, bytes_accessed=20 * rows * D, transcendentals=2 * rows * FF
        ),
        name="feed_forward",
    )(
        place, mixed, start, grad, mask, target, targets, w_out, bias_out, gain, shift,
        w_up, bias_up.reshape(steps, 1, D), w_down, bias_down,
    )


def backward_kernel(
    plan, block, place, q_ref, k_ref, v_ref, do_ref, total_ref, center_ref,
    dq_ref, dk_ref, dv_ref, dqt_sum,
):
    lane = lax.broadcasted_iota(jnp.int32, (1, PAIR), 1)
    pair, step = pl.program_id(0), pl.program_id(1)

    @pl.when(step == 0)
    def _():
        dqt_sum[...] = jnp.zeros_like(dqt_sum)

    q_pair, k_pair, v_pair, do_pair = q_ref[...], k_ref[...], v_ref[...], do_ref[...]
    k_turned = k_pair.T
    key_id = lax.broadcasted_iota(jnp.int32, (block, 1), 0) + step * block
    bias = jnp.where(plan.key_time(key_id) < place[1], 0.0, DEAD)
    grad_k, grad_v = [], []
    for e in range(2):
        own = (lane // HEAD_DIM) == e
        head = slice(e * HEAD_DIM, (e + 1) * HEAD_DIM)
        q_own = jnp.where(own, q_pair, jnp.zeros_like(q_pair))
        do_own = jnp.where(own, do_pair, jnp.zeros_like(do_pair))
        prob = jnp.exp(mm_nt(k_pair, q_own) + bias - total_ref[0, e : e + 1, :])
        grad_prob = mm_nt(v_pair, do_own)
        center = center_ref[pl.ds(2 * pair + e, 1), :]
        grad_scores = (prob * (grad_prob - center)).astype(BF16)
        grad_v.append(mm(prob.astype(BF16), do_own))
        grad_k.append(mm(grad_scores, q_own))
        dqt_sum[head, :] += mm(k_turned[head, :], grad_scores)
    dk_ref[...] = (grad_k[0] + grad_k[1]).astype(dk_ref.dtype)
    dv_ref[...] = (grad_v[0] + grad_v[1]).astype(dv_ref.dtype)

    @pl.when(step == pl.num_programs(1) - 1)
    def _():
        dq_ref[...] = (dqt_sum[...] * SCALE).T.astype(dq_ref.dtype)


def attend_backward(plan, place, queries, kv, grad_mixed, total, center):
    rows, keys = plan.rows, plan.keys
    block = min(512, keys)
    return pl.pallas_call(
        functools.partial(backward_kernel, plan, block),
        grid_spec=pltpu.PrefetchScalarGridSpec(
            num_scalar_prefetch=1,
            grid=(PAIRS, keys // block),
            in_specs=[
                pl.BlockSpec((rows, PAIR), lambda p, i, s: (0, p)),
                pl.BlockSpec((block, PAIR), lambda p, i, s: (i, p)),
                pl.BlockSpec((block, PAIR), lambda p, i, s: (i, PAIRS + p)),
                pl.BlockSpec((rows, PAIR), lambda p, i, s: (0, p)),
                pl.BlockSpec((1, 2, rows), lambda p, i, s: (p, 0, 0)),
                pl.BlockSpec((8, rows), lambda p, i, s: (0, 0)),
            ],
            out_specs=[
                pl.BlockSpec((rows, PAIR), lambda p, i, s: (0, p)),
                pl.BlockSpec((block, PAIR), lambda p, i, s: (i, p)),
                pl.BlockSpec((block, PAIR), lambda p, i, s: (i, p)),
            ],
            scratch_shapes=[pltpu.VMEM((PAIR, rows), F32)],
        ),
        out_shape=[
            jax.ShapeDtypeStruct((rows, D), BF16),
            jax.ShapeDtypeStruct((keys, D), BF16),
            jax.ShapeDtypeStruct((keys, D), BF16),
        ],
        compiler_params=pltpu.CompilerParams(vmem_limit_bytes=VMEM_LIMIT),
        cost_estimate=pl.CostEstimate(
            flops=10 * rows * keys * D, bytes_accessed=10 * rows * D, transcendentals=rows * keys
        ),
        name="attend_backward",
    )(place, queries, kv, kv, grad_mixed, total, center)


def finish_kernel(
    plan, cut, dq, start, grad_middle, mask, dk_all, dv_all, w_ref, gain, shift, dw_out, vec,
    input_grad, reduced, vec_out,
    dk_buf, dv_buf, hat_buf, grad_buf, weight, away, core_in, plane_send, plane_in,
    depth_send, depth_in, total, rows_buf, vec_buf, vec_core, vec_plane, vec_depth,
    kv_send, kv_recv, kv_local, rows_ss, rows_rs, rows_local, core_sem, plane_ss, plane_rs,
    depth_ss, depth_rs, up_ss, up_rs, wide_ss, wide_rs, last_sem, vec_core_sem,
    vec_plane_ss, vec_plane_rs, vec_depth_ss, vec_depth_rs, out_sem,
):
    n, rows, block_rows = plan.clips, plan.rows, plan.block_rows
    half, chunk, piece = cut.half, cut.chunk, cut.piece
    me, part = plan.place()
    time_id = lax.axis_index("tm")
    core, depth = time_id % 2, time_id // 2
    n_plane, n_depth = cut.n_plane, cut.n_depth
    plane = lax.axis_index("freq") * plan.batch + lax.axis_index("batch")
    partner = {"tm": time_id + 1 - 2 * core}
    peers = [lax.rem(me + k, n) for k in range(n)]
    sharers = [lax.rem(part + k, plan.share) for k in range(plan.share)]
    planes = [lax.rem(plane + k, n_plane) for k in range(n_plane)]
    depths = [lax.rem(depth + k, n_depth) for k in range(n_depth)]
    in_plane = [{"freq": v // plan.batch, "batch": v % plan.batch} for v in planes]
    in_depth = [{"tm": v * 2 + core} for v in depths]

    def spot(first, count):
        return pl.ds(pl.multiple_of(first, 16), count)

    greet(
        [plan.member(peers[k], part) for k in range(1, n)]
        + [plan.sharer(sharers[k]) for k in range(1, plan.share)]
        + [partner]
        + in_plane[1:]
        + in_depth[1:]
    )
    kv_copies = []
    for i, (src, dst) in enumerate(((dk_all, dk_buf), (dv_all, dv_buf))):
        for k in range(1, plan.share):
            copy = remote(
                src.at[sharers[k]], dst.at[k], kv_send.at[i, k], kv_recv.at[i, k],
                plan.sharer(sharers[k]),
            )
            copy.start()
            kv_copies.append(copy)
        copy = pltpu.make_async_copy(src.at[part], dst.at[0], kv_local.at[i])
        copy.start()
        kv_copies.append(copy)

    gain_row, shift_row = row(gain), row(shift)
    tile = min(256, rows)
    normed = []
    for i in range(rows // tile):
        span = slice(i * tile, (i + 1) * tile)
        hat, _ = normalize(start[span, :].astype(F32))
        hat_buf[span, :] = hat
        normed.append((hat * gain_row + shift_row).astype(BF16))
    normed = jnp.concatenate(normed, axis=0)
    weight[3 * D :, :] = dw_out[...]
    weight[:D, :] = mm_tn(normed, dq[...])
    grad_buf[...] = mm_nt(dq[...], w_ref[:, :D])
    vec_buf[...] = vec[...]
    vec_buf[3:4, :] = sum_rows(dq[...].astype(F32))
    for copy in kv_copies:
        copy.wait()
    for i, buf in enumerate((dk_buf, dv_buf)):
        summed = buf[0].astype(F32)
        for k in range(1, plan.share):
            summed = summed + buf[k].astype(F32)
        summed = summed.astype(BF16)
        at = slice((1 + i) * D, (2 + i) * D)
        weight[at, :] = mm_tn(normed, summed)
        grad_buf[...] += mm_nt(summed, w_ref[:, at])
        if i == 1:
            vec_buf[4:5, :] = sum_rows(summed.astype(F32))

    away[...] = weight[spot((1 - core) * half, half), :].astype(BF16)
    core_copy = remote(away, core_in, core_sem.at[0], core_sem.at[1], partner)
    core_copy.start()

    row_copies = []
    grad_embed = jnp.zeros((1, D), F32)
    grad_gain = jnp.zeros((1, D), F32)
    grad_shift = jnp.zeros((1, D), F32)
    for k in range(n):
        owner = peers[k]
        span = spot(owner * block_rows, block_rows)
        _, scale = normalize(start[span, :].astype(F32))
        hat = hat_buf[span, :]
        grad_normed = grad_buf[span, :]
        grad_gain += sum_rows(grad_normed * hat)
        grad_shift += sum_rows(grad_normed)
        grad_start = grad_middle[span, :] + normalize_back(grad_normed * gain_row, hat, scale)
        masked = columns(mask[owner]) == 1
        grad_embed += sum_rows(jnp.where(masked, grad_start, 0.0))
        rows_buf[owner] = jnp.where(masked, 0.0, grad_start).astype(BF16)
        if k == 0:
            copy = pltpu.make_async_copy(rows_buf.at[owner], input_grad.at[me], rows_local)
        else:
            copy = remote(
                rows_buf.at[owner], input_grad.at[me], rows_ss.at[k], rows_rs.at[k],
                plan.member(owner, part),
            )
        copy.start()
        row_copies.append(copy)
    vec_buf[0:1, :] = grad_embed
    vec_buf[1:2, :] = grad_gain
    vec_buf[2:3, :] = grad_shift
    vec_copy = remote(vec_buf, vec_core, vec_core_sem.at[0], vec_core_sem.at[1], partner)
    vec_copy.start()

    core_copy.wait()
    plane_send[...] = (weight[spot(core * half, half), :] + core_in[...].astype(F32)).astype(BF16)
    plane_copies = []
    for k in range(1, n_plane):
        copy = remote(
            plane_send.at[spot(planes[k] * chunk, chunk)], plane_in.at[k],
            plane_ss.at[k], plane_rs.at[k], in_plane[k],
        )
        copy.start()
        plane_copies.append(copy)
    vec_copy.wait()
    vec_plane[plane] = vec_buf[...] + vec_core[...]
    vec_plane_copies = []
    for k in range(1, n_plane):
        copy = remote(
            vec_plane.at[plane], vec_plane.at[plane], vec_plane_ss.at[k], vec_plane_rs.at[k],
            in_plane[k],
        )
        copy.start()
        vec_plane_copies.append(copy)
    mine = plane_send[spot(plane * chunk, chunk), :].astype(F32)
    for k in range(1, n_plane):
        plane_copies[k - 1].wait()
        mine = mine + plane_in[k].astype(F32)

    depth_copies = []
    home = core * half + plane * chunk
    if cut.scatter:
        depth_send[...] = mine.astype(BF16)
        for k in range(1, n_depth):
            copy = remote(
                depth_send.at[spot(depths[k] * piece, piece)], depth_in.at[k],
                depth_ss.at[k], depth_rs.at[k], in_depth[k],
            )
            copy.start()
            depth_copies.append(copy)
    else:
        depth_in[depth] = mine.astype(BF16)
        for k in range(1, n_depth):
            copy = remote(
                depth_in.at[depth], depth_in.at[depth], depth_ss.at[k], depth_rs.at[k], in_depth[k]
            )
            copy.start()
            depth_copies.append(copy)
    for copy in vec_plane_copies:
        copy.wait()
    summed = vec_plane[0]
    for k in range(1, n_plane):
        summed = summed + vec_plane[k]
    vec_depth[depth] = summed
    vec_depth_copies = []
    for k in range(1, n_depth):
        copy = remote(
            vec_depth.at[depth], vec_depth.at[depth], vec_depth_ss.at[k], vec_depth_rs.at[k],
            in_depth[k],
        )
        copy.start()
        vec_depth_copies.append(copy)
    if cut.scatter:
        mine = depth_send[spot(depth * piece, piece), :].astype(F32)
        for k in range(1, n_depth):
            depth_copies[k - 1].wait()
            mine = mine + depth_in[k].astype(F32)
        own = spot(home + depth * piece, piece)
        total[own, :] = mine.astype(BF16)
        up_copies = []
        for k in range(1, n_depth):
            copy = remote(total.at[own], total.at[own], up_ss.at[k], up_rs.at[k], in_depth[k])
            copy.start()
            up_copies.append(copy)
        for copy in up_copies:
            copy.wait()
    else:
        for copy in depth_copies:
            copy.wait()
        mine = depth_in[0].astype(F32)
        for k in range(1, n_depth):
            mine = mine + depth_in[k].astype(F32)
        total[spot(home, chunk), :] = mine.astype(BF16)
    own = spot(home, chunk)
    wide_copies = []
    for k in range(1, n_plane):
        copy = remote(total.at[own], total.at[own], wide_ss.at[k], wide_rs.at[k], in_plane[k])
        copy.start()
        wide_copies.append(copy)
    for copy in vec_depth_copies:
        copy.wait()
    summed = vec_depth[0]
    for k in range(1, n_depth):
        summed = summed + vec_depth[k]
    vec_out[...] = summed
    for copy in wide_copies:
        copy.wait()
    own = spot(core * half, half)
    last = remote(total.at[own], total.at[own], last_sem.at[0], last_sem.at[1], partner)
    last.start()
    last.wait()
    copy = pltpu.make_async_copy(total, reduced, out_sem)
    copy.start()
    for other in row_copies:
        other.wait()
    copy.wait()


class Cut:
    def __init__(self, plan):
        self.rows = 4 * D
        self.n_plane = plan.freq * plan.batch
        self.n_depth = plan.tm // 2
        self.half = self.rows // 2
        self.chunk = self.half // self.n_plane
        self.piece = self.chunk // self.n_depth
        self.scatter = self.piece % 16 == 0 and self.piece * self.n_depth == self.chunk
        assert self.chunk * self.n_plane == self.half and self.chunk % 16 == 0


def finish(plan, dq, start, grad_middle, mask, dk_all, dv_all, w_qkv, gain, shift, dw_out, vec):
    n, rows = plan.clips, plan.rows
    cut = Cut(plan)
    dma = pltpu.SemaphoreType.DMA
    depth_shape = (cut.n_depth, cut.piece if cut.scatter else cut.chunk, D)
    vec_shape = (VEC_ROWS, D)
    return pl.pallas_call(
        functools.partial(finish_kernel, plan, cut),
        out_shape=[
            jax.ShapeDtypeStruct((n, plan.block_rows, D), BF16),
            jax.ShapeDtypeStruct((cut.rows, D), BF16),
            jax.ShapeDtypeStruct(vec_shape, F32),
        ],
        in_specs=[VMEM] * 4 + [ANY] * 2 + [VMEM] * 5,
        out_specs=[ANY, ANY, VMEM],
        scratch_shapes=[
            pltpu.VMEM((plan.share, rows, D), BF16),
            pltpu.VMEM((plan.share, rows, D), BF16),
            pltpu.VMEM((rows, D), F32),
            pltpu.VMEM((rows, D), F32),
            pltpu.VMEM((cut.rows, D), F32),
            pltpu.VMEM((cut.half, D), BF16),
            pltpu.VMEM((cut.half, D), BF16),
            pltpu.VMEM((cut.half, D), BF16),
            pltpu.VMEM((cut.n_plane, cut.chunk, D), BF16),
            pltpu.VMEM((cut.chunk, D), BF16),
            pltpu.VMEM(depth_shape, BF16),
            pltpu.VMEM((cut.rows, D), BF16),
            pltpu.VMEM((n, plan.block_rows, D), BF16),
            pltpu.VMEM(vec_shape, F32),
            pltpu.VMEM(vec_shape, F32),
            pltpu.VMEM((cut.n_plane,) + vec_shape, F32),
            pltpu.VMEM((cut.n_depth,) + vec_shape, F32),
            dma((2, plan.share)), dma((2, plan.share)), dma((2,)),
            dma((n,)), dma((n,)), dma(()), dma((2,)),
            dma((cut.n_plane,)), dma((cut.n_plane,)), dma((cut.n_depth,)), dma((cut.n_depth,)),
            dma((cut.n_depth,)), dma((cut.n_depth,)), dma((cut.n_plane,)), dma((cut.n_plane,)),
            dma((2,)), dma((2,)),
            dma((cut.n_plane,)), dma((cut.n_plane,)), dma((cut.n_depth,)), dma((cut.n_depth,)),
            dma(()),
        ],
        compiler_params=pltpu.CompilerParams(
            collective_id=1, has_side_effects=True, vmem_limit_bytes=VMEM_LIMIT
        ),
        name="finish",
    )(dq, start, grad_middle, mask, dk_all, dv_all, w_qkv, gain, shift, dw_out, vec)


def unpack_kernel(plan, place, reduced, vec, *outs):
    w_qkv, w_out, bias_up, soft = outs[:4]
    for p in range(3):
        w_qkv[:, p * D : (p + 1) * D] = reduced[p * D : (p + 1) * D, :].astype(F32)
    w_out[...] = reduced[3 * D :, :].astype(F32)
    for i, out in enumerate(outs[4:]):
        out[...] = vec[i, :]
    for i in range(FF // D):
        bias_up[i * D : (i + 1) * D] = vec[9 + i, :]
    scores = vec[13:14, :]
    lane = lax.broadcasted_iota(jnp.int32, (plan.clips, D), 1)
    slot = place[2] * 2 * plan.clips + lax.broadcasted_iota(jnp.int32, (plan.clips, D), 0)
    hits = jnp.sum(jnp.where(lane == slot, scores, 0.0), axis=1, keepdims=True)
    counts = jnp.sum(jnp.where(lane == slot + plan.clips, scores, 0.0), axis=1, keepdims=True)
    soft[...] = hits / jnp.maximum(counts, 1.0)


def unpack(plan, place, reduced, vec):
    vector = jax.ShapeDtypeStruct((D,), F32)
    return pl.pallas_call(
        functools.partial(unpack_kernel, plan),
        grid_spec=pltpu.PrefetchScalarGridSpec(
            num_scalar_prefetch=1, grid=(), in_specs=[VMEM] * 2, out_specs=[VMEM] * 13
        ),
        out_shape=[
            jax.ShapeDtypeStruct((D, 3 * D), F32),
            jax.ShapeDtypeStruct((D, D), F32),
            jax.ShapeDtypeStruct((FF,), F32),
            jax.ShapeDtypeStruct((plan.clips, 1), F32),
        ]
        + [vector] * 9,
        compiler_params=pltpu.CompilerParams(vmem_limit_bytes=VMEM_LIMIT),
        name="unpack",
    )(place, reduced, vec)


def per_device(
    plan,
    patches, patch_mask, clip_lengths, target_index, targets, out_grad,
    mask_embed, ln1_gain, ln1_shift, w_qkv, bias_q, bias_v, w_out, bias_out,
    ln2_gain, ln2_shift, w_up, bias_up, w_down, bias_down,
):
    n, rows, block_rows = plan.clips, plan.rows, plan.block_rows
    clip, part = plan.place()
    length = lax.dynamic_index_in_dim(clip_lengths, clip, keepdims=False)
    place = jnp.stack([clip, length, lax.axis_index("batch"), part]).astype(jnp.int32)
    members = [
        [f * plan.tm + b * plan.share + j for f in range(plan.freq) for b in range(plan.blocks)]
        for j in range(plan.share)
    ]

    def swap(blocks):
        return lax.all_to_all(
            blocks, ("freq", "tm"), 0, 0, axis_index_groups=members, tiled=True
        )

    start, queries, kv, mask, target = project_rows(
        plan, patches.reshape(n, block_rows, D), patch_mask, target_index,
        mask_embed, ln1_gain, ln1_shift, w_qkv, bias_q, bias_v,
    )
    start, out_grad = lax.optimization_barrier((start, out_grad))
    grad = swap(out_grad.reshape(n, block_rows, D)).reshape(rows, D)
    start = start.reshape(rows, D)
    queries = queries.reshape(rows, D)
    kv = kv.reshape(plan.keys, 2 * D)
    mixed, total = attend_forward(plan, place, queries, kv)
    block_out, grad_middle, grad_mixed, center, grad_w_up, grad_w_down, grad_w_out, vec = (
        feed_forward(
            plan, place, mixed, start, grad, mask, target, targets, w_out, bias_out,
            ln2_gain, ln2_shift, w_up, bias_up, w_down, bias_down,
        )
    )
    block_grid = swap(block_out.reshape(n, block_rows, D)).reshape(patches.shape)
    grad_w_up, grad_w_down = lax.psum((grad_w_up, grad_w_down), ("freq", "tm", "batch"))
    dq, dk_all, dv_all = attend_backward(plan, place, queries, kv, grad_mixed, total, center)
    input_grad, reduced, vec = finish(
        plan, dq, start, grad_middle, mask,
        dk_all.reshape(plan.share, rows, D), dv_all.reshape(plan.share, rows, D),
        w_qkv, ln1_gain, ln1_shift, grad_w_out, vec,
    )
    grad_w_qkv, grad_w_out, grad_bias_up, soft, *vectors = unpack(plan, place, reduced, vec)
    (grad_mask_embed, grad_ln1_gain, grad_ln1_shift, grad_bias_q, grad_bias_v, grad_bias_out,
     grad_ln2_gain, grad_ln2_shift, grad_bias_down) = vectors
    return (
        block_grid, input_grad.reshape(patches.shape), grad_mask_embed, grad_ln1_gain,
        grad_ln1_shift, grad_w_qkv, grad_bias_q, grad_bias_v, grad_w_out, grad_bias_out,
        grad_ln2_gain, grad_ln2_shift, grad_w_up, grad_bias_up, grad_w_down, grad_bias_down,
        soft.reshape(n),
    )


def solution(mesh):
    rows = P("batch", "freq", "tm", None)
    whole = P()
    in_specs = (
        rows, P("batch", "freq", "tm"), P("batch"), P("batch", "freq", "tm"),
        P("batch", None, None), rows,
    ) + (whole,) * 14
    out_specs = (rows, rows) + (whole,) * 14 + (P("batch"),)

    def body(*args):
        return per_device(Plan(mesh, args[0]), *args)

    return jax.shard_map(
        body, mesh=mesh, in_specs=in_specs, out_specs=out_specs, check_vma=False
    )
```

time: 392 us -> 278 us (0.71)
  matrix products: 50.5 us -> 0 us
  Pallas kernels: 143 us -> 187 us
  other arithmetic: 45.5 us -> 2.52 us
  blocking collectives: 38.5 us -> 0 us
  local copies, waits for them, and re-layouts: 26.3 us -> 8.18 us
  waiting for transfers between devices: 66.9 us -> 49.8 us
  starting transfers between devices: 0.56 us -> 10.9 us
    dot_general x13 -> x0, matrix products: 50.5 us -> none  [the longest x4 24.2 us: mm(): return jnp.dot(left_mat, right_mat, preferred_element_type=jnp.float32)]
    pallas_call x4 -> x6, Pallas kernels: 143 us -> 187 us  [the longest x1 58.3 us: finish(): pl.pallas_call(functools.partial(finish_kernel, plan, cut), out_shape=[ja...]
    psum x1 -> x0, blocking collectives: 38.5 us -> none  [per_device(): packed = lax.psum(packed, everywhere)]
    reduce_sum x13 -> x0, other arithmetic: 16 us -> none  [the longest x1 2.19 us: per_device(): jnp.sum((grad_mixed.astype(f32) * mixed_f).reshape(tokens, HEADS, HEAD_DI...]
    convert_element_type x16 -> x0, other arithmetic: 11.9 us -> none  [the longest x4 6.8 us: per_device(): g.astype(f32)]
    all_to_all x0 -> x2, starting transfers between devices: none -> 10.9 us  [swap(): lax.all_to_all(blocks, ('freq', 'tm'), 0, 0, axis_index_groups=members, t...]
    all_gather x1 -> x0, waiting for transfers between devices: 8.74 us -> none  [per_device(): lax.all_gather(local_kv, 'tm', axis=0, tiled=True, axis_index_groups=groups)]
    psum x1, waiting for transfers between devices: 58.1 us -> 49.8 us  [per_device(): lax.psum((grad_w_up, grad_w_down), ('freq', 'tm', 'batch'))]
  transfers between devices with their start and end apart: 3 -> 3, of which waited for: 2 -> 1; matrix products, arithmetic and copies ran while one was open for 11% -> 1% of each run, Pallas kernels for 11% -> 49%
where the time goes in v2:
time: 278 us; the launch traced here: 272 us
  Pallas kernels  187 us (67%)
  waiting for transfers between devices  49.8 us (18%)
  between operations  14.1 us (5%)
  starting transfers between devices  10.9 us (4%)
  local copies, waits for them, and re-layouts  8.18 us (3%)
    pallas_call x1, Pallas kernels, finish(): pl.pallas_call(functools.partial(finish_kernel, plan, cut), out_shape=[ja...  58.3 us
    psum x1, waiting for transfers between devices, per_device(): lax.psum((grad_w_up, grad_w_down), ('freq', 'tm', 'batch'))  49.8 us
    pallas_call x1, Pallas kernels, attend_backward(): pl.pallas_call(functools.partial(backward_kernel, plan, block), grid_spec...  44.9 us
    pallas_call x1, Pallas kernels, project_rows(): pl.pallas_call(functools.partial(project_kernel, plan), out_shape=[jax.Sh...  27.2 us
    pallas_call x1, Pallas kernels, feed_forward(): pl.pallas_call(functools.partial(feed_kernel, plan), grid_spec=pltpu.Pref...  26.5 us
    pallas_call x1, Pallas kernels, attend_forward(): pl.pallas_call(functools.partial(forward_kernel, plan), grid_spec=pltpu.P...  26.4 us
    all_to_all x2, starting transfers between devices, swap(): lax.all_to_all(blocks, ('freq', 'tm'), 0, 0, axis_index_groups=members, t...  10.9 us
    unnamed x16, local copies, waits for them, and re-layouts  6.99 us
  transfers between devices with their start and end apart: 3, of which 1 were waited for; matrix products, arithmetic and copies ran while one was open for 1% of the time, Pallas kernels for 49%

profile of v2, /device:TPU:25, one launch (start us, length us, event | category | flops | bytes accessed | tf_op | source)
XLA Modules:
  0.0 272.5 jit_solution(8343594640520638456)
XLA Ops:
  7.2 0.0 copy-start.4
  7.2 0.0 copy-start.5
  7.2 27.2 %project_rows.1 = (bf16[8,128,384]{2,1,0:T(8,128)(2,1)}, bf16[8,128,384]{2,1,0:T(8,128)(2,1)}, bf16[2,8,128,768]{3,2,1,0:T(8,128)(2,1)}, s32[8,4,32]{2,1,0:T(4,128)}, s32[8,4,32]{2,1,0:T(4,128)}) custom-call(bf16[8,128,384]{2,1,0:T(8,128)(2,1)} %bitcast.19, s32[8,4,32]{2,1,0:T(4,128)} %mask.1, s32[8,4,32]{2,1,0:T(4,128)} %target.1, bf16[384]{0:T(512)(128)(2,1)} %embed.1, ...), custom_call_target="tpu_custom_call" | custom-call | tf_op jit(solution)/shard_map/project_rows/pallas_call | solution.py:204
  34.5 5.5 %all-to-all-start = ((bf16[8,128,384]{2,1,0:T(8,128)(2,1)}), bf16[8,128,384]{2,1,0:T(8,128)(2,1)S(1)}, u32[]{:S(2)}, u32[]{:S(2)}) async-start(bf16[8,128,384]{2,1,0:T(8,128)(2,1)} %bitcast.20), calls=%async_computation | async-start | bytes 1572864 | tf_op jit(solution)/shard_map/all_to_all | solution.py:827
  39.9 0.0 all-reduce.3.cloned.1.call-start
  39.9 0.0 copy-done.4
  39.9 0.6 reshape.86.bias_up
  40.5 0.0 copy-done.5
  40.5 0.6 dynamic_slice.4
  41.1 1.2 pad_add_fusion.place
  42.3 26.4 %attend_forward.1 = (f32[1024,384]{1,0:T(8,128)}, f32[3,2,1024]{2,1,0:T(2,128)}) custom-call(s32[4]{0:T(128)} %pad_add_fusion.place, bf16[1024,384]{1,0:T(8,128)(2,1)} %bitcast.27, bf16[2048,768]{1,0:T(8,128)(2,1)} %bitcast.23, bf16[2048,768]{1,0:T(8,128)(2,1)} %bitcast.24), custom_call_target="tpu_custom_call" | custom-call | flops 3221225472 | bytes 3145728 | tf_op jit(solution)/shard_map/attend_forward/pallas_call | solution.py:252
  68.8 0.0 all-to-all-done
  68.8 0.0 copy-start.2
  68.8 0.9 copy-done.2
  69.7 26.5 %feed_forward.1 = (bf16[1024,384]{1,0:T(8,128)(2,1)}, f32[1024,384]{1,0:T(8,128)}, bf16[1024,384]{1,0:T(8,128)(2,1)}, f32[8,1024]{1,0:T(8,128)}, f32[384,1536]{1...) custom-call(s32[4]{0:T(128)} %pad_add_fusion.place, ...), custom_call_target="tpu_custom_call" | custom-call | flops 7247757312 | bytes 7864320 | tf_op jit(solution)/shard_map/feed_forward/pallas_call | solution.py:382
  96.1 0.0 all-reduce.3.cloned.1.call-update
  96.2 5.4 %all-to-all-start.1 = ((bf16[8,128,384]{2,1,0:T(8,128)(2,1)}), bf16[8,128,384]{2,1,0:T(8,128)(2,1)S(1)}, u32[]{:S(2)}, u32[]{:S(2)}) async-start(bf16[8,128,384]{2,1,0:T(8,128)(2,1)} %bitcast.9), calls=%async_computation.1 | async-start | bytes 1572864 | tf_op jit(solution)/shard_map/all_to_all | solution.py:827
  101.6 44.9 %attend_backward.1 = (bf16[1024,384]{1,0:T(8,128)(2,1)}, bf16[2048,384]{1,0:T(8,128)(2,1)}, bf16[2048,384]{1,0:T(8,128)(2,1)}) custom-call(s32[4]{0:T(128)} %pad_add_fusion.place, bf16[1024,384]{1,0:T(8,128)(2,1)} %bitcast.28, bf16[2048,768]{1,0:T(8,128)(2,1)} %bitcast.25, bf16[2048,768]{1,0:T(8,128)(2,1)} %bitcast.26, ...), custom_call_target="tpu_custom_call" | custom-call | flops 8053063680 | bytes 3932160 | tf_op jit(solution)/shard_map/attend_backward/pallas_call | solution.py:469
  146.5 58.3 %finish.1 = (bf16[8,128,384]{2,1,0:T(8,128)(2,1)}, bf16[1536,384]{1,0:T(8,128)(2,1)}, f32[16,384]{1,0:T(8,128)}) custom-call(bf16[1024,384]{1,0:T(8,128)(2,1)} %get-tuple-element.65.dq, bf16[1024,384]{1,0:T(8,128)(2,1)} %bitcast.18, f32[1024,384]{1,0:T(8,128)} %get-tuple-element.66.grad_middle, s32[8,4,32]{2,1,0:T(4,128)} %get-tuple-element.59.mask, ...), custom_call_target="tpu_custom_call" | custom-call | tf_op jit(solution)/shard_map/finish/pallas_call | solution.py:733
  204.8 0.0 copy-start.3
  204.8 3.6 %unpack.1 = (f32[384,1152]{1,0:T(8,128)}, f32[384,384]{1,0:T(8,128)}, f32[1536]{0:T(1024)}, f32[8,1]{1,0:T(8,128)}, f32[384]{0:T(512)}, /*index=5*/f32[384]{0:T(...) custom-call(s32[4]{0:T(128)} %pad_add_fusion.place, ...), custom_call_target="tpu_custom_call" | custom-call | tf_op jit(solution)/shard_map/unpack/pallas_call | solution.py:794
  208.4 1.3 reduce
  209.7 0.0 all-to-all-done.1
  209.7 49.8 %all-reduce.3.cloned.1.call-done = (f32[384,1536]{1,0:T(8,128)}, f32[1536,384]{1,0:T(8,128)}) async-done(((f32[384,1536]{1,0:T(8,128)}, f32[1536,384]{1,0:T(8,128)}), (f32[384,1536]{1,0:T(8,128)}, f32[1536,384]{1,0:T(8,128)})) %all-reduce.3.cloned.1.call-update) | async-done | bytes 4718608 | tf_op jit(solution)/shard_map/psum | solution.py:848
  259.5 0.0 copy-start.1
  259.5 0.9 copy.42
  260.4 0.0 copy-done.3
  260.4 0.9 copy.43
  261.3 0.4 copy-done.1
  261.7 1.4 copy.44
  263.1 1.1 copy-done
  264.2 1.4 copy.45
  (1 shorter events, 0.0 us)
Async XLA Ops:
  7.2 32.7 %copy-start.4 = (bf16[1536]{0:T(1024)(128)(2,1)S(1)}, bf16[1536]{0:T(1024)(128)(2,1)}, u32[]{:S(2)}) copy-start(bf16[1536]{0:T(1024)(128)(2,1)} %param.37) | copy-start | bytes 9220
  7.2 33.3 %copy-start.5 = (s32[8]{0:T(128)S(1)}, s32[8]{0:T(128)}, u32[]{:S(2)}) copy-start(s32[8]{0:T(128)} %param.22) | copy-start | bytes 100
  34.5 34.3 %all-to-all-start = ((bf16[8,128,384]{2,1,0:T(8,128)(2,1)}), bf16[8,128,384]{2,1,0:T(8,128)(2,1)S(1)}, u32[]{:S(2)}, u32[]{:S(2)}) async-start(bf16[8,128,384]{2,1,0:T(8,128)(2,1)} %bitcast.20), calls=%async_computation | async-start | bytes 1572864 | tf_op jit(solution)/shard_map/all_to_all | solution.py:827
  39.9 219.6 %all-reduce.3.cloned.1.call-start = ((), (), s32[]{:S(2)}) async-start(), calls=%async_computation.2 | async-start | bytes 9437184 | tf_op jit(solution)/shard_map/psum | solution.py:848
  68.8 0.9 copy-start.2
  96.2 113.5 %all-to-all-start.1 = ((bf16[8,128,384]{2,1,0:T(8,128)(2,1)}), bf16[8,128,384]{2,1,0:T(8,128)(2,1)S(1)}, u32[]{:S(2)}, u32[]{:S(2)}) async-start(bf16[8,128,384]{2,1,0:T(8,128)(2,1)} %bitcast.9), calls=%async_computation.1 | async-start | bytes 1572864 | tf_op jit(solution)/shard_map/all_to_all | solution.py:827
  204.8 55.6 %copy-start.3 = (bf16[8,128,384]{2,1,0:T(8,128)(2,1)S(1)}, bf16[8,128,384]{2,1,0:T(8,128)(2,1)}, u32[]{:S(2)}) copy-start(bf16[8,128,384]{2,1,0:T(8,128)(2,1)} %get-tuple-element.71) | copy-start | bytes 2359300
  259.5 2.2 copy-start.1
  261.7 2.5 copy-start
Sparse Core Ops, SparseCore 0:
  96.3 163.1 all-reduce.2

commit v3 on v2

v3 whole, which is shorter than its diff:
```python
import functools

import jax
import jax.numpy as jnp
from jax import lax
from jax.experimental import pallas as pl
from jax.experimental.pallas import tpu as pltpu
from jax.sharding import PartitionSpec as P

D = 384
FF = 1536
HEADS = 6
HEAD_DIM = 64
PAIRS = HEADS // 2
PAIR = 2 * HEAD_DIM
SCALE = HEAD_DIM ** (-0.5)
DEAD = -1e9
EPS = 1e-06
VEC_ROWS = 16
MESH = pl.DeviceIdType.MESH
VMEM_LIMIT = 60 * 2**20
ANY = pl.BlockSpec(memory_space=pl.ANY)
VMEM = pl.BlockSpec(memory_space=pltpu.VMEM)
BF16 = jnp.bfloat16
F32 = jnp.float32


def mm(left_mat, right_mat):
    return jnp.dot(left_mat, right_mat, preferred_element_type=F32)


def mm_nt(left_mat, right_mat):
    return lax.dot_general(
        left_mat, right_mat, (((1,), (1,)), ((), ())), preferred_element_type=F32
    )


def mm_tn(left_mat, right_mat):
    return lax.dot_general(
        left_mat, right_mat, (((0,), (0,)), ((), ())), preferred_element_type=F32
    )


def row(ref):
    return ref[...].astype(F32).reshape(1, -1)


def normalize(rows):
    center = rows - jnp.mean(rows, axis=-1, keepdims=True)
    scale = lax.rsqrt(jnp.mean(center * center, axis=-1, keepdims=True) + EPS)
    return center * scale, scale


def normalize_back(grad_hat, hat, scale):
    first = jnp.mean(grad_hat, axis=-1, keepdims=True)
    second = jnp.mean(grad_hat * hat, axis=-1, keepdims=True)
    return scale * (grad_hat - first - hat * second)


def sum_rows(rows):
    return jnp.sum(rows, axis=0, keepdims=True)


def columns(ints):
    freq_rows, time_rows = ints.shape
    shape = (time_rows, time_rows)
    eye = lax.broadcasted_iota(jnp.int32, shape, 0) == lax.broadcasted_iota(jnp.int32, shape, 1)
    parts = [
        jnp.sum(jnp.where(eye, ints[f : f + 1, :], 0), axis=1, keepdims=True)
        for f in range(freq_rows)
    ]
    return jnp.concatenate(parts, axis=0)


class Plan:
    def __init__(self, mesh, patches):
        self.freq = mesh.shape["freq"]
        self.tm = mesh.shape["tm"]
        self.batch = mesh.shape["batch"]
        self.clips, self.freq_rows, self.time_rows, _ = patches.shape
        self.share = self.freq * self.tm // self.clips
        self.blocks = self.tm // self.share
        self.block_rows = self.freq_rows * self.time_rows
        self.rows = self.clips * self.block_rows
        self.keys = self.share * self.rows
        assert self.freq * self.blocks == self.clips and self.blocks * self.share == self.tm

    def place(self):
        time_id = lax.axis_index("tm")
        return lax.axis_index("freq") * self.blocks + time_id // self.share, time_id % self.share

    def member(self, member, part):
        return {
            "freq": member // self.blocks,
            "tm": (member % self.blocks) * self.share + part,
        }

    def sharer(self, part):
        time_id = lax.axis_index("tm")
        return {"tm": time_id // self.share * self.share + part}

    def key_time(self, place):
        part = place // self.rows
        block = (place // self.block_rows) % self.clips % self.blocks
        return (block * self.share + part) * self.time_rows + place % self.time_rows


def greet(devices):
    barrier = pltpu.get_barrier_semaphore()
    for device in devices:
        pl.semaphore_signal(barrier, inc=1, device_id=device, device_id_type=MESH)
    pl.semaphore_wait(barrier, len(devices))


def remote(src, dst, send_sem, recv_sem, device):
    return pltpu.make_async_remote_copy(
        src_ref=src, dst_ref=dst, send_sem=send_sem, recv_sem=recv_sem,
        device_id=device, device_id_type=MESH,
    )


def front_kernel(
    plan, lengths, patches, mask, target, out_grad, embed, gain, shift, w_ref, bias_q, bias_v,
    start_out, q_out, qt_out, k_out, v_out, mixed_out, total_out, mask_out, target_out, grad_out,
    taken, mask_in, target_in, start_buf, q_buf, qt_buf, kv_buf, k_buf, v_buf, vt_buf,
    mixed_buf, total_buf, score_a, score_b,
    send_sem, recv_sem, local_sem, kv_send, kv_recv, grad_send, grad_recv, out_sem,
):
    me, part = plan.place()
    n, rows, keys, block_rows = plan.clips, plan.rows, plan.keys, plan.block_rows
    peers = [lax.rem(me + step, n) for step in range(n)]
    sharers = [lax.rem(part + step, plan.share) for step in range(plan.share)]
    greet(
        [plan.member(peers[step], part) for step in range(1, n)]
        + [plan.sharer(sharers[step]) for step in range(1, plan.share)]
    )
    streams = ((mask, mask_in), (target, target_in), (patches, taken))
    arrivals = []
    for step in range(n):
        copies = []
        for i, (src, dst) in enumerate(streams):
            if step == 0:
                copy = pltpu.make_async_copy(src.at[me], dst.at[me], local_sem.at[i])
            else:
                copy = remote(
                    src.at[peers[step]], dst.at[me], send_sem.at[i, step], recv_sem.at[i, step],
                    plan.member(peers[step], part),
                )
            copy.start()
            copies.append(copy)
        arrivals.append(copies)
    gain_row, shift_row, embed_row = row(gain), row(shift), row(embed)
    bias_q_row, bias_v_row = row(bias_q), row(bias_v)
    waits, shared = [], []

    def save(index, src, dst):
        copy = pltpu.make_async_copy(src, dst, out_sem.at[index])
        copy.start()
        waits.append(copy)

    for step in range(n):
        source = lax.rem(me + n - step, n)
        for copy in arrivals[step]:
            if step == 0:
                copy.wait()
            else:
                copy.wait_recv()
        masked = columns(mask_in[source]) == 1
        start = jnp.where(masked, embed_row, taken[source].astype(F32))
        start_buf[source] = start.astype(BF16)
        hat, _ = normalize(start)
        normed = (hat * gain_row + shift_row).astype(BF16)
        project = mm(normed, w_ref[...])
        queries = (project[:, :D] + bias_q_row).astype(BF16)
        q_buf[source] = (queries.astype(F32) * SCALE).astype(BF16)
        kv_buf[part, source, :, :D] = project[:, D : 2 * D].astype(BF16)
        kv_buf[part, source, :, D:] = (project[:, 2 * D :] + bias_v_row).astype(BF16)
        for other in range(1, plan.share):
            copy = remote(
                kv_buf.at[part, source], kv_buf.at[part, source], kv_send.at[other, step],
                kv_recv.at[other, step], plan.sharer(sharers[other]),
            )
            copy.start()
            shared.append(copy)
    for step in range(n):
        if step == 0:
            copy = pltpu.make_async_copy(out_grad.at[me], grad_out.at[me], local_sem.at[0])
        else:
            copy = remote(
                out_grad.at[peers[step]], grad_out.at[me], grad_send.at[step], grad_recv.at[step],
                plan.member(peers[step], part),
            )
        copy.start()
        waits.append(copy)
    save(0, start_buf, start_out)
    save(1, q_buf, q_out)
    save(2, mask_in, mask_out)
    save(3, target_in, target_out)
    for i in range(n):
        at = slice(i * block_rows, (i + 1) * block_rows)
        qt_buf[:, at] = q_buf[i].T
    save(4, qt_buf, qt_out)
    for copy in shared:
        copy.wait()
    length = lengths[me]
    first = kv_buf[0, 0, 0:1, :D]
    for i in range(plan.share):
        for b in range(n):
            begin = i * rows + b * block_rows
            at = slice(begin, begin + block_rows)
            ids = lax.broadcasted_iota(jnp.int32, (block_rows, 1), 0) + begin
            live = plan.key_time(ids) < length
            k_buf[at, :] = jnp.where(live, kv_buf[i, b, :, :D], first)
            value = kv_buf[i, b, :, D:]
            value = jnp.where(live, value, jnp.zeros_like(value))
            v_buf[at, :] = value
            turned = value.T
            ids = lax.broadcasted_iota(jnp.int32, (16, block_rows), 1) + begin
            top = lax.broadcasted_iota(jnp.int32, (16, block_rows), 0) == 0
            count = jnp.where((plan.key_time(ids) < length) & top, 1.0, 0.0).astype(BF16)
            for h in range(HEADS):
                vt_buf[h, :HEAD_DIM, at] = turned[h * HEAD_DIM : (h + 1) * HEAD_DIM, :]
                vt_buf[h, HEAD_DIM:, at] = count
    save(5, k_buf, k_out)
    save(6, v_buf, v_out)

    width = score_a.shape[1]
    spans = rows // width
    items = HEADS * spans
    lane = lax.broadcasted_iota(jnp.int32, (1, PAIR), 1)

    def score(item, buf):
        head, span = item // spans, item % spans
        pair = pl.ds(pl.multiple_of(head // 2 * PAIR, PAIR), PAIR)
        at = pl.ds(pl.multiple_of(span * width, width), width)
        k_own = jnp.where(lane // HEAD_DIM == head % 2, k_buf[:, pair], jnp.zeros((), BF16))
        scores = mm(k_own, qt_buf[pair, at])
        buf[...] = scores
        return jnp.max(scores, axis=0, keepdims=True)

    def blend(item, buf, top):
        head, span = item // spans, item % spans
        at = pl.ds(pl.multiple_of(span * width, width), width)
        raised = jnp.exp(buf[...] - top).astype(BF16)
        out = mm(vt_buf[head], raised)
        row_total = out[HEAD_DIM : HEAD_DIM + 1, :]
        into = pl.ds(pl.multiple_of(head * HEAD_DIM, HEAD_DIM), HEAD_DIM)
        mixed_buf[into, at] = (out[:HEAD_DIM, :] / row_total).astype(BF16)
        total_buf[head, :, at] = top + jnp.log(row_total)

    def two(i, top_a):
        top_b = score(2 * i + 1, score_b)
        blend(2 * i, score_a, top_a)
        top_a = score(2 * i + 2, score_a)
        blend(2 * i + 1, score_b, top_b)
        return top_a

    top_a = lax.fori_loop(0, items // 2 - 1, two, score(0, score_a))
    top_b = score(items - 1, score_b)
    blend(items - 2, score_a, top_a)
    blend(items - 1, score_b, top_b)
    save(7, mixed_buf, mixed_out)
    save(8, total_buf, total_out)
    for step in range(1, n):
        for copy in arrivals[step]:
            copy.wait_send()
    for copy in waits:
        copy.wait()


def front(plan, lengths, patches, mask, target, out_grad, embed, gain, shift, w_qkv, bias_q, bias_v):
    n, rows, keys, block_rows = plan.clips, plan.rows, plan.keys, plan.block_rows
    width = min(512, rows)
    assert HEADS * (rows // width) % 2 == 0
    dma = pltpu.SemaphoreType.DMA
    blocks = (n, block_rows, D)
    total = (HEADS, 1, rows)
    shapes = [
        (blocks, BF16), (blocks, BF16), ((D, rows), BF16), ((keys, D), BF16), ((keys, D), BF16),
        ((D, rows), BF16), (total, F32), (mask.shape, jnp.int32), (mask.shape, jnp.int32),
        (blocks, BF16),
    ]
    return pl.pallas_call(
        functools.partial(front_kernel, plan),
        out_shape=[jax.ShapeDtypeStruct(shape, kind) for shape, kind in shapes],
        in_specs=[pl.BlockSpec(memory_space=pltpu.SMEM)] + [ANY] * 4 + [VMEM] * 6,
        out_specs=[ANY] * 10,
        scratch_shapes=[
            pltpu.VMEM(blocks, BF16),
            pltpu.VMEM(mask.shape, jnp.int32),
            pltpu.VMEM(mask.shape, jnp.int32),
            pltpu.VMEM(blocks, BF16),
            pltpu.VMEM(blocks, BF16),
            pltpu.VMEM((D, rows), BF16),
            pltpu.VMEM((plan.share, n, block_rows, 2 * D), BF16),
            pltpu.VMEM((keys, D), BF16),
            pltpu.VMEM((keys, D), BF16),
            pltpu.VMEM((HEADS, HEAD_DIM + 16, keys), BF16),
            pltpu.VMEM((D, rows), BF16),
            pltpu.VMEM(total, F32),
            pltpu.VMEM((keys, width), F32),
            pltpu.VMEM((keys, width), F32),
            dma((3, n)), dma((3, n)), dma((3,)),
            dma((plan.share, n)), dma((plan.share, n)), dma((n,)), dma((n,)), dma((9,)),
        ],
        compiler_params=pltpu.CompilerParams(
            collective_id=0, has_side_effects=True, vmem_limit_bytes=VMEM_LIMIT
        ),
        name="front",
    )(lengths, patches, mask, target, out_grad, embed, gain, shift, w_qkv, bias_q, bias_v)


def gelu_parts(rows):
    lower = 0.5 * (1.0 + lax.erf(rows * 0.7071067811865476))
    slope = lower + rows * (jnp.exp(-0.5 * rows * rows) * 0.3989422804014327)
    return rows * lower, slope


def feed_kernel(
    plan, place, mixed, start, grad, mask, target, targets, w_out, bias_out, gain, shift,
    w_up, bias_up, w_down, bias_down,
    block_out, grad_middle, grad_mixed, grad_mixed_t, center, payload, grad_w_out, vec,
    middle, second, down_sum, second_sum, act_buf, up_buf,
):
    step = pl.program_id(0)
    steps = pl.num_programs(0)
    rows = plan.rows
    tile = min(256, rows)
    tiles = [slice(i * tile, (i + 1) * tile) for i in range(rows // tile)]
    gain_row, shift_row = row(gain), row(shift)

    @pl.when(step == 0)
    def _():
        vec[...] = jnp.zeros_like(vec)
        for part in tiles:
            rows_in = start[part, :].astype(F32) + mm_tn(mixed[:, part], w_out[...])
            rows_in = rows_in + row(bias_out)
            middle[part, :] = rows_in
            hat, _ = normalize(rows_in)
            second[part, :] = (hat * gain_row + shift_row).astype(BF16)
        down_sum[...] = jnp.zeros_like(down_sum)
        second_sum[...] = jnp.zeros_like(second_sum)

    bias_row = row(bias_up.at[0])
    for part in tiles:
        hidden = mm(second[part, :], w_up[...]) + bias_row
        active, slope = gelu_parts(hidden)
        active = active.astype(BF16)
        act_buf[part, :] = active
        down_sum[part, :] += mm(active, w_down[...])
        grad_up = (mm_nt(grad[part, :], w_down[...]) * slope).astype(BF16)
        up_buf[part, :] = grad_up
        second_sum[part, :] += mm_nt(grad_up, w_up[...])
    payload[0, 0] = mm_tn(act_buf[...], grad[...]).astype(BF16)
    payload[1, 0] = mm_tn(second[...], up_buf[...]).astype(BF16)
    vec[pl.ds(9 + step, 1), :] = sum_rows(up_buf[...].astype(F32))

    @pl.when(step == steps - 1)
    def _():
        clip, length, batch = place[0], place[1], place[2]
        cand = lax.broadcasted_iota(jnp.int32, (1, targets.shape[1]), 1)
        vec[8:9, :] = sum_rows(grad[...].astype(F32))
        total_hit = jnp.zeros((1, 1), F32)
        total_count = jnp.zeros((1, 1), F32)
        per_tile = tile // plan.block_rows
        for t, part in enumerate(tiles):
            result = middle[part, :] + down_sum[part, :] + row(bias_down)
            result = result.astype(BF16)
            block_out[part, :] = result
            hat, scale = normalize(middle[part, :])
            grad_second = second_sum[part, :]
            vec[6:7, :] += sum_rows(grad_second * hat)
            vec[7:8, :] += sum_rows(grad_second)
            back = normalize_back(grad_second * gain_row, hat, scale)
            back = grad[part, :].astype(F32) + back
            grad_middle[part, :] = back
            branch = back.astype(BF16)
            act_buf[part, :] = branch
            vec[5:6, :] += sum_rows(branch.astype(F32))
            grad_mixed[part, :] = mm_nt(branch, w_out[...]).astype(BF16)
            down = mm_nt(w_out[...], branch).astype(BF16)
            grad_mixed_t[:, part] = down
            product = down.astype(F32) * mixed[:, part].astype(F32)
            for h in range(HEADS):
                center[h, :, part] = sum_rows(product[h * HEAD_DIM : (h + 1) * HEAD_DIM, :])
            logits = mm_nt(result, targets[0])
            raised = jnp.exp(logits - jnp.max(logits, axis=1, keepdims=True))
            sources = range(t * per_tile, (t + 1) * per_tile)
            target_col = jnp.concatenate([columns(target[s]) for s in sources], axis=0)
            mask_col = jnp.concatenate([columns(mask[s]) for s in sources], axis=0)
            hit = jnp.sum(jnp.where(cand == target_col, raised, 0.0), axis=1, keepdims=True)
            hit = hit / jnp.sum(raised, axis=1, keepdims=True)
            ids = lax.broadcasted_iota(jnp.int32, (tile, 1), 0) + t * tile + place[3] * rows
            counted = jnp.where((plan.key_time(ids) < length) & (mask_col == 1), 1.0, 0.0)
            total_hit += jnp.sum(hit * counted, axis=0, keepdims=True)
            total_count += jnp.sum(counted, axis=0, keepdims=True)
        grad_w_out[...] = mm(mixed[...], act_buf[...])
        lane = lax.broadcasted_iota(jnp.int32, (1, D), 1)
        slot = batch * 2 * plan.clips + clip
        scores = jnp.where(lane == slot, total_hit, 0.0)
        vec[13:14, :] = scores + jnp.where(lane == slot + plan.clips, total_count, 0.0)


def feed_forward(
    plan, place, mixed, start, grad, mask, target, targets, w_out, bias_out, gain, shift,
    w_up, bias_up, w_down, bias_down,
):
    rows = plan.rows
    steps = FF // D

    def full(shape):
        return pl.BlockSpec(shape, lambda i, s: (0,) * len(shape))

    return pl.pallas_call(
        functools.partial(feed_kernel, plan),
        grid_spec=pltpu.PrefetchScalarGridSpec(
            num_scalar_prefetch=1,
            grid=(steps,),
            in_specs=[
                full((D, rows)), full((rows, D)), full((rows, D)),
                full(mask.shape), full(mask.shape),
                pl.BlockSpec((1,) + targets.shape[1:], lambda i, s: (s[0], 0, 0)),
                full((D, D)), full((D,)), full((D,)), full((D,)),
                pl.BlockSpec((D, D), lambda i, s: (0, i)),
                pl.BlockSpec((1, 1, D), lambda i, s: (i, 0, 0)),
                pl.BlockSpec((D, D), lambda i, s: (i, 0)),
                full((D,)),
            ],
            out_specs=[
                full((rows, D)), full((rows, D)), full((rows, D)), full((D, rows)),
                full((HEADS, 1, rows)),
                pl.BlockSpec((2, 1, D, D), lambda i, s: (0, i, 0, 0)),
                full((D, D)), full((VEC_ROWS, D)),
            ],
            scratch_shapes=[
                pltpu.VMEM((rows, D), F32), pltpu.VMEM((rows, D), BF16),
                pltpu.VMEM((rows, D), F32), pltpu.VMEM((rows, D), F32),
                pltpu.VMEM((rows, D), BF16), pltpu.VMEM((rows, D), BF16),
            ],
        ),
        out_shape=[
            jax.ShapeDtypeStruct((rows, D), BF16),
            jax.ShapeDtypeStruct((rows, D), F32),
            jax.ShapeDtypeStruct((rows, D), BF16),
            jax.ShapeDtypeStruct((D, rows), BF16),
            jax.ShapeDtypeStruct((HEADS, 1, rows), F32),
            jax.ShapeDtypeStruct((2, steps, D, D), BF16),
            jax.ShapeDtypeStruct((D, D), F32),
            jax.ShapeDtypeStruct((VEC_ROWS, D), F32),
        ],
        compiler_params=pltpu.CompilerParams(vmem_limit_bytes=VMEM_LIMIT),
        cost_estimate=pl.CostEstimate(
            flops=12 * rows * FF * D, bytes_accessed=20 * rows * D, transcendentals=2 * rows * FF
        ),
        name="feed_forward",
    )(
        place, mixed, start, grad, mask, target, targets, w_out, bias_out, gain, shift,
        w_up, bias_up.reshape(steps, 1, D), w_down, bias_down,
    )


class Ring:
    def __init__(self, cut, at, half_src, own_half, core_in, mine, plane_in, part_buf, depth_in, total, sems):
        self.cut, self.at = cut, at
        self.half_src, self.own_half, self.core_in, self.mine = half_src, own_half, core_in, mine
        self.plane_in, self.part_buf, self.depth_in, self.total = plane_in, part_buf, depth_in, total
        self.core_sem, self.plane_sem, self.depth_sem, self.up_sem, self.wide_sem = sems

    def core_copy(self):
        return remote(
            self.half_src, self.core_in, self.core_sem.at[0], self.core_sem.at[1], self.at.partner
        )

    def plane_copies(self):
        chunk = self.cut.chunk
        return [
            remote(
                self.mine.at[spot(self.at.planes[k] * chunk, chunk)], self.plane_in.at[k],
                self.plane_sem.at[0, k], self.plane_sem.at[1, k], self.at.in_plane[k],
            )
            for k in range(1, self.cut.n_plane)
        ]

    def depth_copies(self):
        piece, copies = self.cut.piece, []
        for k in range(1, self.cut.n_depth):
            if self.cut.scatter:
                src = self.part_buf.at[spot(self.at.depths[k] * piece, piece)]
                dst = self.depth_in.at[k]
            else:
                src = dst = self.depth_in.at[self.at.depth]
            copies.append(
                remote(
                    src, dst, self.depth_sem.at[0, k], self.depth_sem.at[1, k], self.at.in_depth[k]
                )
            )
        return copies

    def same(self, first, count, sems, k, device):
        own = spot(first, count)
        return remote(self.total.at[own], self.total.at[own], sems.at[0, k], sems.at[1, k], device)

    def home(self):
        return self.at.core * self.cut.half + self.at.plane * self.cut.chunk

    def up_copies(self):
        first = self.home() + self.at.depth * self.cut.piece
        return [
            self.same(first, self.cut.piece, self.up_sem, k, self.at.in_depth[k])
            for k in range(1, self.cut.n_depth)
        ]

    def wide_copies(self):
        return [
            self.same(self.home(), self.cut.chunk, self.wide_sem, k, self.at.in_plane[k])
            for k in range(1, self.cut.n_plane)
        ]

    def last_copy(self):
        own = spot(self.at.core * self.cut.half, self.cut.half)
        return remote(
            self.total.at[own], self.total.at[own], self.core_sem.at[2], self.core_sem.at[3],
            self.at.partner,
        )

    def begin(self):
        self.core_copy().start()

    def to_plane(self):
        self.core_copy().wait()
        own = self.own_half().astype(F32) + self.core_in[...].astype(F32)
        self.mine[...] = own.astype(BF16)
        for copy in self.plane_copies():
            copy.start()

    def to_depth(self):
        chunk = self.cut.chunk
        mine = self.mine[spot(self.at.plane * chunk, chunk), :].astype(F32)
        for k, copy in enumerate(self.plane_copies()):
            copy.wait()
            mine = mine + self.plane_in[k + 1].astype(F32)
        if self.cut.scatter:
            self.part_buf[...] = mine.astype(BF16)
        else:
            self.depth_in[self.at.depth] = mine.astype(BF16)
        for copy in self.depth_copies():
            copy.start()

    def back_up(self):
        piece, copies = self.cut.piece, self.depth_copies()
        if self.cut.scatter:
            mine = self.part_buf[spot(self.at.depth * piece, piece), :].astype(F32)
            for k, copy in enumerate(copies):
                copy.wait()
                mine = mine + self.depth_in[k + 1].astype(F32)
            self.total[spot(self.home() + self.at.depth * piece, piece), :] = mine.astype(BF16)
            for copy in self.up_copies():
                copy.start()
        else:
            for copy in copies:
                copy.wait()
            mine = self.depth_in[0].astype(F32)
            for k in range(1, self.cut.n_depth):
                mine = mine + self.depth_in[k].astype(F32)
            self.total[spot(self.home(), self.cut.chunk), :] = mine.astype(BF16)

    def back_wide(self):
        if self.cut.scatter:
            for copy in self.up_copies():
                copy.wait()
        for copy in self.wide_copies():
            copy.start()

    def back_core(self):
        for copy in self.wide_copies():
            copy.wait()
        self.last_copy().start()

    def end(self):
        self.last_copy().wait()


class Cut:
    def __init__(self, plan, rows):
        self.rows = rows
        self.n_plane = plan.freq * plan.batch
        self.n_depth = plan.tm // 2
        self.half = rows // 2
        self.chunk = self.half // self.n_plane
        self.piece = self.chunk // self.n_depth
        self.scatter = self.piece % 16 == 0 and self.piece * self.n_depth == self.chunk
        assert self.chunk * self.n_plane == self.half and self.chunk % 16 == 0

    def buffers(self):
        depth = self.piece if self.scatter else self.chunk
        return [
            pltpu.VMEM((self.half, D), BF16),
            pltpu.VMEM((self.half, D), BF16),
            pltpu.VMEM((self.half, D), BF16),
            pltpu.VMEM((self.n_plane, self.chunk, D), BF16),
            pltpu.VMEM((self.chunk, D), BF16),
            pltpu.VMEM((self.n_depth, depth, D), BF16),
            pltpu.VMEM((self.rows, D), BF16),
        ]

    def semaphores(self):
        dma = pltpu.SemaphoreType.DMA
        return [
            dma((4,)), dma((2, self.n_plane)), dma((2, self.n_depth)), dma((2, self.n_depth)),
            dma((2, self.n_plane)),
        ]


class Place:
    def __init__(self, plan):
        time_id = lax.axis_index("tm")
        n_plane, n_depth = plan.freq * plan.batch, plan.tm // 2
        self.core, self.depth = time_id % 2, time_id // 2
        self.plane = lax.axis_index("freq") * plan.batch + lax.axis_index("batch")
        self.partner = {"tm": time_id + 1 - 2 * self.core}
        self.planes = [lax.rem(self.plane + k, n_plane) for k in range(n_plane)]
        self.depths = [lax.rem(self.depth + k, n_depth) for k in range(n_depth)]
        self.in_plane = [{"freq": v // plan.batch, "batch": v % plan.batch} for v in self.planes]
        self.in_depth = [{"tm": v * 2 + self.core} for v in self.depths]


def spot(first, count):
    return pl.ds(pl.multiple_of(first, 16), count)


def back_kernel(
    plan, wide_cut, cut, lengths, block_rows_in, payload, q_ref, qt_ref, k_ref, v_ref, do_ref, dot_ref,
    log_total, center, start, grad_middle, mask, w_ref, gain, shift, dw_out, vec,
    block_grid, input_grad, wide_out, reduced, vec_out,
    kt_buf, score_a, score_b, prob_a, prob_b, dqt_sum, dk_all, dv_all, dk_in, dv_in,
    hat_buf, grad_buf, weight, rows_buf, vec_buf, vec_core, vec_plane, vec_depth,
    *rest,
):
    bufs, sems = rest[:14], rest[14:]
    wide_bufs, small_bufs = bufs[:7], bufs[7:]
    wide_sems, small_sems = sems[:5], sems[5:10]
    (grid_ss, grid_rs, kv_ss, kv_rs, rows_ss, rows_rs, local_sem, vec_core_sem,
     vec_plane_sem, vec_depth_sem) = sems[10:]
    n, rows, keys, block_rows = plan.clips, plan.rows, plan.keys, plan.block_rows
    me, part = plan.place()
    at = Place(plan)
    n_plane, n_depth = cut.n_plane, cut.n_depth
    peers = [lax.rem(me + k, n) for k in range(n)]
    sharers = [lax.rem(part + k, plan.share) for k in range(plan.share)]
    length = lengths[me]

    own_half_copy = pltpu.make_async_copy(
        payload.at[spot(at.core * wide_cut.half, wide_cut.half)], wide_bufs[0], local_sem.at[0]
    )
    wide = Ring(
        wide_cut, at, payload.at[spot((1 - at.core) * wide_cut.half, wide_cut.half)],
        lambda: wide_bufs[0][...], *wide_bufs[1:], wide_sems,
    )
    small = Ring(
        cut, at, small_bufs[0], lambda: weight[spot(at.core * cut.half, cut.half), :],
        *small_bufs[1:], small_sems,
    )
    greet(
        [plan.member(peers[k], part) for k in range(1, n)]
        + [plan.sharer(sharers[k]) for k in range(1, plan.share)]
        + [at.partner]
        + at.in_plane[1:]
        + at.in_depth[1:]
    )
    own_half_copy.start()
    wide.begin()
    home_copies = [
        pltpu.make_async_copy(block_rows_in.at[me], block_grid.at[me], local_sem.at[1])
    ]
    for k in range(1, n):
        home_copies.append(
            remote(
                block_rows_in.at[peers[k]], block_grid.at[me], grid_ss.at[k], grid_rs.at[k],
                plan.member(peers[k], part),
            )
        )
    for copy in home_copies:
        copy.start()

    def kv_copies():
        return [
            remote(
                src.at[sharers[k]], dst.at[k], kv_ss.at[i, k], kv_rs.at[i, k],
                plan.sharer(sharers[k]),
            )
            for i, (src, dst) in enumerate(((dk_all, dk_in), (dv_all, dv_in)))
            for k in range(1, plan.share)
        ]

    tile = min(256, rows)
    for i in range(keys // tile):
        span = slice(i * tile, (i + 1) * tile)
        ids = lax.broadcasted_iota(jnp.int32, (1, tile), 1) + i * tile
        turned = k_ref[span, :].T
        live = plan.key_time(ids) < length
        kt_buf[:, span] = jnp.where(live, turned, jnp.zeros_like(turned))
    dqt_sum[...] = jnp.zeros_like(dqt_sum)

    block = score_a.shape[0]
    per_part = rows // block
    lane = lax.broadcasted_iota(jnp.int32, (1, PAIR), 1)
    owns = [lane // HEAD_DIM == e for e in range(2)]
    zero = jnp.zeros((), BF16)
    bodies = PAIRS * per_part * plan.share

    def body(i, carry):
        order, pair = i // PAIRS, i % PAIRS
        owner = lax.rem(part + 1 + order // per_part, plan.share)
        begin = order % per_part * block
        span = pl.ds(pl.multiple_of(owner * rows + begin, block), block)
        inside = pl.ds(pl.multiple_of(begin, block), block)
        cols = pl.ds(pl.multiple_of(pair * PAIR, PAIR), PAIR)
        for e, (score_buf, prob_buf) in enumerate(((score_a, prob_a), (score_b, prob_b))):
            score_buf[...] = mm(jnp.where(owns[e], k_ref[span, cols], zero), qt_ref[cols, :])
            prob_buf[...] = mm(jnp.where(owns[e], v_ref[span, cols], zero), dot_ref[cols, :])
        grad_k, grad_v = [], []
        for e, (score_buf, prob_buf) in enumerate(((score_a, prob_a), (score_b, prob_b))):
            head = pl.ds(pl.multiple_of(pair * PAIR + e * HEAD_DIM, HEAD_DIM), HEAD_DIM)
            prob = jnp.exp(score_buf[...] - log_total[2 * pair + e])
            grad_scores = (prob * (prob_buf[...] - center[2 * pair + e])).astype(BF16)
            grad_v.append(mm(prob.astype(BF16), jnp.where(owns[e], do_ref[:, cols], zero)))
            grad_k.append(mm(grad_scores, jnp.where(owns[e], q_ref[:, cols], zero)))
            dqt_sum[head, :] += mm(kt_buf[head, span], grad_scores)
        dk_all[owner, inside, cols] = (grad_k[0] + grad_k[1]).astype(BF16)
        dv_all[owner, inside, cols] = (grad_v[0] + grad_v[1]).astype(BF16)

        def at_step(step, do):
            pl.when(i == step)(do)

        def to_plane():
            own_half_copy.wait()
            wide.to_plane()

        def send_keys():
            for copy in kv_copies():
                copy.start()

        at_step(1, to_plane)
        at_step(bodies - 6, wide.to_depth)
        at_step(bodies - 4, wide.back_up)
        at_step(bodies - 3, wide.back_wide)
        at_step(bodies - PAIRS * per_part - 1, send_keys)
        return carry

    lax.fori_loop(0, bodies, body, 0)

    gain_row, shift_row = row(gain), row(shift)
    dq = (dqt_sum[...] * SCALE).T.astype(BF16)
    normed = []
    for i in range(rows // tile):
        span = slice(i * tile, (i + 1) * tile)
        hat, _ = normalize(start[span, :].astype(F32))
        hat_buf[span, :] = hat
        normed.append((hat * gain_row + shift_row).astype(BF16))
    normed = jnp.concatenate(normed, axis=0)
    weight[3 * D :, :] = dw_out[...]
    weight[:D, :] = mm_tn(normed, dq)
    grad_buf[...] = mm_nt(dq, w_ref[:, :D])
    vec_buf[...] = vec[...]
    vec_buf[3:4, :] = sum_rows(dq.astype(F32))
    for copy in kv_copies():
        copy.wait()
    ids = lax.broadcasted_iota(jnp.int32, (rows, 1), 0)
    live = plan.key_time(ids + part * rows) < length
    for i, (own, buf) in enumerate(((dk_all, dk_in), (dv_all, dv_in))):
        summed = own[part].astype(F32)
        for k in range(1, plan.share):
            summed = summed + buf[k].astype(F32)
        summed = jnp.where(live, summed, 0.0).astype(BF16)
        cols = slice((1 + i) * D, (2 + i) * D)
        weight[cols, :] = mm_tn(normed, summed)
        grad_buf[...] += mm_nt(summed, w_ref[:, cols])
        if i == 1:
            vec_buf[4:5, :] = sum_rows(summed.astype(F32))
    small_bufs[0][...] = weight[spot((1 - at.core) * cut.half, cut.half), :].astype(BF16)
    small.begin()

    row_copies = []
    grad_embed = jnp.zeros((1, D), F32)
    grad_gain = jnp.zeros((1, D), F32)
    grad_shift = jnp.zeros((1, D), F32)
    for k in range(n):
        owner = peers[k]
        span = spot(owner * block_rows, block_rows)
        _, scale = normalize(start[span, :].astype(F32))
        hat = hat_buf[span, :]
        grad_normed = grad_buf[span, :]
        grad_gain += sum_rows(grad_normed * hat)
        grad_shift += sum_rows(grad_normed)
        grad_start = grad_middle[span, :] + normalize_back(grad_normed * gain_row, hat, scale)
        masked = columns(mask[owner]) == 1
        grad_embed += sum_rows(jnp.where(masked, grad_start, 0.0))
        rows_buf[owner] = jnp.where(masked, 0.0, grad_start).astype(BF16)
        if k == 0:
            copy = pltpu.make_async_copy(rows_buf.at[owner], input_grad.at[me], local_sem.at[2])
        else:
            copy = remote(
                rows_buf.at[owner], input_grad.at[me], rows_ss.at[k], rows_rs.at[k],
                plan.member(owner, part),
            )
        copy.start()
        row_copies.append(copy)
    vec_buf[0:1, :] = grad_embed
    vec_buf[1:2, :] = grad_gain
    vec_buf[2:3, :] = grad_shift
    vec_copy = remote(vec_buf, vec_core, vec_core_sem.at[0], vec_core_sem.at[1], at.partner)
    vec_copy.start()
    small.to_plane()
    wide.back_core()
    vec_copy.wait()
    vec_plane[at.plane] = vec_buf[...] + vec_core[...]
    vec_plane_copies = []
    for k in range(1, n_plane):
        copy = remote(
            vec_plane.at[at.plane], vec_plane.at[at.plane], vec_plane_sem.at[0, k],
            vec_plane_sem.at[1, k], at.in_plane[k],
        )
        copy.start()
        vec_plane_copies.append(copy)
    small.to_depth()
    wide.end()
    wide_copy = pltpu.make_async_copy(wide.total, wide_out, local_sem.at[0])
    wide_copy.start()
    for copy in vec_plane_copies:
        copy.wait()
    summed = vec_plane[0]
    for k in range(1, n_plane):
        summed = summed + vec_plane[k]
    vec_depth[at.depth] = summed
    vec_depth_copies = []
    for k in range(1, n_depth):
        copy = remote(
            vec_depth.at[at.depth], vec_depth.at[at.depth], vec_depth_sem.at[0, k],
            vec_depth_sem.at[1, k], at.in_depth[k],
        )
        copy.start()
        vec_depth_copies.append(copy)
    small.back_up()
    small.back_wide()
    for copy in vec_depth_copies:
        copy.wait()
    summed = vec_depth[0]
    for k in range(1, n_depth):
        summed = summed + vec_depth[k]
    vec_out[...] = summed
    small.back_core()
    small.end()
    copy = pltpu.make_async_copy(small.total, reduced, local_sem.at[3])
    copy.start()
    for other in row_copies + home_copies + [wide_copy, copy]:
        other.wait()


def back(
    plan, lengths, block_out, payload, queries, queries_t, key_rows, value_rows, grad_mixed,
    grad_mixed_t, log_total, center, start, grad_middle, mask, w_qkv, gain, shift, dw_out, vec,
):
    n, rows, keys = plan.clips, plan.rows, plan.keys
    wide_cut, cut = Cut(plan, 2 * FF), Cut(plan, 4 * D)
    dma = pltpu.SemaphoreType.DMA
    vec_shape = (VEC_ROWS, D)
    block = min(512, rows)
    blocks = (n, plan.block_rows, D)
    shared = pltpu.VMEM((plan.share, rows, D), BF16)
    pane = pltpu.VMEM((block, rows), F32)
    return pl.pallas_call(
        functools.partial(back_kernel, plan, wide_cut, cut),
        out_shape=[
            jax.ShapeDtypeStruct(blocks, BF16),
            jax.ShapeDtypeStruct(blocks, BF16),
            jax.ShapeDtypeStruct((wide_cut.rows, D), BF16),
            jax.ShapeDtypeStruct((cut.rows, D), BF16),
            jax.ShapeDtypeStruct(vec_shape, F32),
        ],
        in_specs=[pl.BlockSpec(memory_space=pltpu.SMEM)] + [ANY] * 2 + [VMEM] * 16,
        out_specs=[ANY] * 4 + [VMEM],
        scratch_shapes=[
            pltpu.VMEM((D, keys), BF16), pane, pane, pane, pane, pltpu.VMEM((D, rows), F32),
            shared, shared, shared, shared,
            pltpu.VMEM((rows, D), F32),
            pltpu.VMEM((rows, D), F32),
            pltpu.VMEM((cut.rows, D), F32),
            pltpu.VMEM(blocks, BF16),
            pltpu.VMEM(vec_shape, F32),
            pltpu.VMEM(vec_shape, F32),
            pltpu.VMEM((cut.n_plane,) + vec_shape, F32),
            pltpu.VMEM((cut.n_depth,) + vec_shape, F32),
            *wide_cut.buffers(), *cut.buffers(), *wide_cut.semaphores(), *cut.semaphores(),
            dma((n,)), dma((n,)), dma((2, plan.share)), dma((2, plan.share)), dma((n,)), dma((n,)),
            dma((4,)), dma((2,)), dma((2, cut.n_plane)), dma((2, cut.n_depth)),
        ],
        compiler_params=pltpu.CompilerParams(
            collective_id=1, has_side_effects=True, vmem_limit_bytes=VMEM_LIMIT
        ),
        name="back",
    )(
        lengths, block_out, payload, queries, queries_t, key_rows, value_rows, grad_mixed,
        grad_mixed_t, log_total, center, start, grad_middle, mask, w_qkv, gain, shift, dw_out, vec,
    )


def unpack_kernel(plan, place, reduced, wide, vec, *outs):
    w_qkv, w_out, w_up, w_down, bias_up, soft = outs[:6]
    step = pl.program_id(0)
    w_down[...] = wide[0, 0].astype(F32)
    w_up[...] = wide[1, 0].astype(F32)

    @pl.when(step < 3)
    def _():
        w_qkv[...] = reduced[0].astype(F32)

    @pl.when(step == 3)
    def _():
        w_out[...] = reduced[0].astype(F32)
        for i, out in enumerate(outs[6:]):
            out[...] = vec[i, :]
        for i in range(FF // D):
            bias_up[i * D : (i + 1) * D] = vec[9 + i, :]
        scores = vec[13:14, :]
        lane = lax.broadcasted_iota(jnp.int32, (plan.clips, D), 1)
        slot = place[2] * 2 * plan.clips + lax.broadcasted_iota(jnp.int32, (plan.clips, D), 0)
        hits = jnp.sum(jnp.where(lane == slot, scores, 0.0), axis=1, keepdims=True)
        counts = jnp.sum(jnp.where(lane == slot + plan.clips, scores, 0.0), axis=1, keepdims=True)
        soft[...] = hits / jnp.maximum(counts, 1.0)


def unpack(plan, place, reduced, wide, vec):
    vector = jax.ShapeDtypeStruct((D,), F32)

    def full(shape):
        return pl.BlockSpec(shape, lambda i, s: (0,) * len(shape))

    return pl.pallas_call(
        functools.partial(unpack_kernel, plan),
        grid_spec=pltpu.PrefetchScalarGridSpec(
            num_scalar_prefetch=1,
            grid=(4,),
            in_specs=[
                pl.BlockSpec((1, D, D), lambda i, s: (i, 0, 0)),
                pl.BlockSpec((2, 1, D, D), lambda i, s: (0, i, 0, 0)),
                full((VEC_ROWS, D)),
            ],
            out_specs=[
                pl.BlockSpec((D, D), lambda i, s: (0, jnp.minimum(i, 2))),
                full((D, D)),
                pl.BlockSpec((D, D), lambda i, s: (0, i)),
                pl.BlockSpec((D, D), lambda i, s: (i, 0)),
                full((FF,)),
                full((plan.clips, 1)),
            ]
            + [full((D,))] * 9,
        ),
        out_shape=[
            jax.ShapeDtypeStruct((D, 3 * D), F32),
            jax.ShapeDtypeStruct((D, D), F32),
            jax.ShapeDtypeStruct((D, FF), F32),
            jax.ShapeDtypeStruct((FF, D), F32),
            jax.ShapeDtypeStruct((FF,), F32),
            jax.ShapeDtypeStruct((plan.clips, 1), F32),
        ]
        + [vector] * 9,
        compiler_params=pltpu.CompilerParams(vmem_limit_bytes=VMEM_LIMIT),
        name="unpack",
    )(place, reduced.reshape(4, D, D), wide.reshape(2, FF // D, D, D), vec)


def per_device(
    plan,
    patches, patch_mask, clip_lengths, target_index, targets, out_grad,
    mask_embed, ln1_gain, ln1_shift, w_qkv, bias_q, bias_v, w_out, bias_out,
    ln2_gain, ln2_shift, w_up, bias_up, w_down, bias_down,
):
    n, rows, block_rows = plan.clips, plan.rows, plan.block_rows
    clip, part = plan.place()
    length = lax.dynamic_index_in_dim(clip_lengths, clip, keepdims=False)
    place = jnp.stack([clip, length, lax.axis_index("batch"), part]).astype(jnp.int32)
    (start, queries, queries_t, key_rows, value_rows, mixed, log_total, mask, target, grad) = front(
        plan, clip_lengths, patches.reshape(n, block_rows, D), patch_mask, target_index,
        out_grad.reshape(n, block_rows, D), mask_embed, ln1_gain, ln1_shift, w_qkv, bias_q, bias_v,
    )
    start = start.reshape(rows, D)
    queries = queries.reshape(rows, D)
    grad = grad.reshape(rows, D)
    block_out, grad_middle, grad_mixed, grad_mixed_t, center, payload, grad_w_out, vec = (
        feed_forward(
            plan, place, mixed, start, grad, mask, target, targets, w_out, bias_out,
            ln2_gain, ln2_shift, w_up, bias_up, w_down, bias_down,
        )
    )
    block_grid, input_grad, wide, reduced, vec = back(
        plan, clip_lengths, block_out.reshape(n, block_rows, D), payload.reshape(2 * FF, D),
        queries, queries_t, key_rows, value_rows, grad_mixed, grad_mixed_t, log_total, center,
        start, grad_middle, mask, w_qkv, ln1_gain, ln1_shift, grad_w_out, vec,
    )
    grad_w_qkv, grad_w_out, grad_w_up, grad_w_down, grad_bias_up, soft, *vectors = unpack(
        plan, place, reduced, wide, vec
    )
    block_grid = block_grid.reshape(patches.shape)
    (grad_mask_embed, grad_ln1_gain, grad_ln1_shift, grad_bias_q, grad_bias_v, grad_bias_out,
     grad_ln2_gain, grad_ln2_shift, grad_bias_down) = vectors
    return (
        block_grid, input_grad.reshape(patches.shape), grad_mask_embed, grad_ln1_gain,
        grad_ln1_shift, grad_w_qkv, grad_bias_q, grad_bias_v, grad_w_out, grad_bias_out,
        grad_ln2_gain, grad_ln2_shift, grad_w_up, grad_bias_up, grad_w_down, grad_bias_down,
        soft.reshape(n),
    )


def solution(mesh):
    rows = P("batch", "freq", "tm", None)
    whole = P()
    in_specs = (
        rows, P("batch", "freq", "tm"), P("batch"), P("batch", "freq", "tm"),
        P("batch", None, None), rows,
    ) + (whole,) * 14
    out_specs = (rows, rows) + (whole,) * 14 + (P("batch"),)

    def body(*args):
        return per_device(Plan(mesh, args[0]), *args)

    return jax.shard_map(
        body, mesh=mesh, in_specs=in_specs, out_specs=out_specs, check_vma=False
    )
```

time: 278 us -> 184 us (0.66)
  waiting for transfers between devices: 49.8 us -> 0 us
  between operations: 14.1 us -> 0.73 us
  Pallas kernels: 187 us -> 174 us
  starting transfers between devices: 10.9 us -> 0 us
  local copies, waits for them, and re-layouts: 8.18 us -> 4.3 us
    psum x1 -> x0, waiting for transfers between devices: 49.8 us -> none  [per_device(): lax.psum((grad_w_up, grad_w_down), ('freq', 'tm', 'batch'))]
    pallas_call x4 -> x2, Pallas kernels: 157 us -> 141 us  [the longest x1 97.4 us: back(): pl.pallas_call(functools.partial(back_kernel, plan, wide_cut, cut), out_s...]
    all_to_all x2 -> x0, starting transfers between devices: 10.9 us -> none  [swap(): lax.all_to_all(blocks, ('freq', 'tm'), 0, 0, axis_index_groups=members, t...]
    unnamed x16 -> x6, local copies, waits for them, and re-layouts: 6.99 us -> 1.77 us
    pallas_call x1, Pallas kernels: 3.56 us -> 6.52 us  [unpack(): pl.pallas_call(functools.partial(unpack_kernel, plan), grid_spec=pltpu.Pr...]
  transfers between devices with their start and end apart: 3 -> 0, of which waited for: 1 -> 0; matrix products, arithmetic and copies ran while one was open for 1% -> 0% of each run, Pallas kernels for 49% -> 0%
where the time goes in v3:
time: 184 us; the launch traced here: 181 us
  Pallas kernels  174 us (95%)
  local copies, waits for them, and re-layouts  4.3 us (2%)
  other arithmetic  2.64 us (1%)
    pallas_call x1, Pallas kernels, back(): pl.pallas_call(functools.partial(back_kernel, plan, wide_cut, cut), out_s...  97.4 us
    pallas_call x1, Pallas kernels, front(): pl.pallas_call(functools.partial(front_kernel, plan), out_shape=[jax.Shap...  43.3 us
    pallas_call x1, Pallas kernels, feed_forward(): pl.pallas_call(functools.partial(feed_kernel, plan), grid_spec=pltpu.Pref...  26.3 us
    pallas_call x1, Pallas kernels, unpack(): pl.pallas_call(functools.partial(unpack_kernel, plan), grid_spec=pltpu.Pr...  6.52 us

profile of v3, /device:TPU:25, one launch (start us, length us, event | category | flops | bytes accessed | tf_op | source)
XLA Modules:
  0.0 181.2 jit_solution(13921621736137226271)
XLA Ops:
  0.7 1.2 dynamic_slice.4
  1.9 1.3 pad_add_fusion.place
  3.2 1.3 reshape.86.bias_up
  4.5 43.3 %front.1 = (bf16[8,128,384]{2,1,0:T(8,128)(2,1)}, bf16[8,128,384]{2,1,0:T(8,128)(2,1)}, bf16[384,1024]{1,0:T(8,128)(2,1)}, bf16[2048,384]{1,0:T(8,128)(2,1)}, bf...) custom-call(s32[8]{0:T(128)} %lengths.3, ...), custom_call_target="tpu_custom_call" | custom-call | tf_op jit(solution)/shard_map/front/pallas_call | solution.py:283
  47.8 26.3 %feed_forward.1 = (bf16[1024,384]{1,0:T(8,128)(2,1)}, f32[1024,384]{1,0:T(8,128)}, bf16[1024,384]{1,0:T(8,128)(2,1)}, bf16[384,1024]{1,0:T(8,128)(2,1)}, f32[6,1...) custom-call(s32[4]{0:T(128)} %pad_add_fusion.place, ...), custom_call_target="tpu_custom_call" | custom-call | flops 7247757312 | bytes 7864320 | tf_op jit(solution)/shard_map/feed_forward/pallas_call | solution.py:414
  74.1 97.4 %back.1 = (bf16[8,128,384]{2,1,0:T(8,128)(2,1)}, bf16[8,128,384]{2,1,0:T(8,128)(2,1)}, bf16[3072,384]{1,0:T(8,128)(2,1)}, bf16[1536,384]{1,0:T(8,128)(2,1)}, f32[16,384]{1,0:T(8,128)}) custom-call(s32[8]{0:T(128)} %lengths.3, bf16[8,128,384]{2,1,0:T(8,128)(2,1)} %bitcast.22, bf16[3072,384]{1,0:T(8,128)(2,1)} %bitcast.14, bf16[1024,384]{1,0:T(8,128)(2,1)} %bitcast.21, ...), custom_call_target="tpu_custom_call" | custom-call | tf_op jit(solution)/shard_map/back/pallas_call | solution.py:871
  171.5 0.0 copy-start.1
  171.5 6.5 %unpack.1 = (f32[384,1152]{1,0:T(8,128)}, f32[384,384]{1,0:T(8,128)}, f32[384,1536]{1,0:T(8,128)}, f32[1536,384]{1,0:T(8,128)}, f32[1536]{0:T(1024)}, /*index=5*...) custom-call(s32[4]{0:T(128)} %pad_add_fusion.place, ...), custom_call_target="tpu_custom_call" | custom-call | tf_op jit(solution)/shard_map/unpack/pallas_call | solution.py:938
  178.0 0.0 copy-start
  178.1 1.4 reduce
  179.4 0.0 copy-done.1
  179.4 0.9 copy.40
  180.3 0.0 copy-done
  180.3 0.9 copy.41
Async XLA Ops:
  171.5 7.9 %copy-start.1 = (bf16[8,128,384]{2,1,0:T(8,128)(2,1)S(1)}, bf16[8,128,384]{2,1,0:T(8,128)(2,1)}, u32[]{:S(2)}) copy-start(bf16[8,128,384]{2,1,0:T(8,128)(2,1)} %get-tuple-element.73) | copy-start | bytes 2359300
  178.0 2.3 %copy-start = (bf16[8,128,384]{2,1,0:T(8,128)(2,1)S(1)}, bf16[8,128,384]{2,1,0:T(8,128)(2,1)}, u32[]{:S(2)}) copy-start(bf16[8,128,384]{2,1,0:T(8,128)(2,1)} %get-tuple-element.74) | copy-start | bytes 2359300

commit v4 on v3

--- a/solution.py
+++ b/solution.py
@@ -17,6 +17,11 @@
 DEAD = -1e9
 EPS = 1e-06
 VEC_ROWS = 16
+LANES = 128
+CHUNK = 512
+TILE = 512
+GRID_AT = (0, 1, 2, 4, 5, 6, 8, 9)
+WAVES = (4, 6)
 MESH = pl.DeviceIdType.MESH
 VMEM_LIMIT = 60 * 2**20
 ANY = pl.BlockSpec(memory_space=pl.ANY)
@@ -316,149 +321,6 @@
     return rows * lower, slope
 
 
-def feed_kernel(
-    plan, place, mixed, start, grad, mask, target, targets, w_out, bias_out, gain, shift,
-    w_up, bias_up, w_down, bias_down,
-    block_out, grad_middle, grad_mixed, grad_mixed_t, center, payload, grad_w_out, vec,
-    middle, second, down_sum, second_sum, act_buf, up_buf,
-):
-    step = pl.program_id(0)
-    steps = pl.num_programs(0)
-    rows = plan.rows
-    tile = min(256, rows)
-    tiles = [slice(i * tile, (i + 1) * tile) for i in range(rows // tile)]
-    gain_row, shift_row = row(gain), row(shift)
-
-    @pl.when(step == 0)
-    def _():
-        vec[...] = jnp.zeros_like(vec)
-        for part in tiles:
-            rows_in = start[part, :].astype(F32) + mm_tn(mixed[:, part], w_out[...])
-            rows_in = rows_in + row(bias_out)
-            middle[part, :] = rows_in
-            hat, _ = normalize(rows_in)
-            second[part, :] = (hat * gain_row + shift_row).astype(BF16)
-        down_sum[...] = jnp.zeros_like(down_sum)
-        second_sum[...] = jnp.zeros_like(second_sum)
-
-    bias_row = row(bias_up.at[0])
-    for part in tiles:
-        hidden = mm(second[part, :], w_up[...]) + bias_row
-        active, slope = gelu_parts(hidden)
-        active = active.astype(BF16)
-        act_buf[part, :] = active
-        down_sum[part, :] += mm(active, w_down[...])
-        grad_up = (mm_nt(grad[part, :], w_down[...]) * slope).astype(BF16)
-        up_buf[part, :] = grad_up
-        second_sum[part, :] += mm_nt(grad_up, w_up[...])
-    payload[0, 0] = mm_tn(act_buf[...], grad[...]).astype(BF16)
-    payload[1, 0] = mm_tn(second[...], up_buf[...]).astype(BF16)
-    vec[pl.ds(9 + step, 1), :] = sum_rows(up_buf[...].astype(F32))
-
-    @pl.when(step == steps - 1)
-    def _():
-        clip, length, batch = place[0], place[1], place[2]
-        cand = lax.broadcasted_iota(jnp.int32, (1, targets.shape[1]), 1)
-        vec[8:9, :] = sum_rows(grad[...].astype(F32))
-        total_hit = jnp.zeros((1, 1), F32)
-        total_count = jnp.zeros((1, 1), F32)
-        per_tile = tile // plan.block_rows
-        for t, part in enumerate(tiles):
-            result = middle[part, :] + down_sum[part, :] + row(bias_down)
-            result = result.astype(BF16)
-            block_out[part, :] = result
-            hat, scale = normalize(middle[part, :])
-            grad_second = second_sum[part, :]
-            vec[6:7, :] += sum_rows(grad_second * hat)
-            vec[7:8, :] += sum_rows(grad_second)
-            back = normalize_back(grad_second * gain_row, hat, scale)
-            back = grad[part, :].astype(F32) + back
-            grad_middle[part, :] = back
-            branch = back.astype(BF16)
-            act_buf[part, :] = branch
-            vec[5:6, :] += sum_rows(branch.astype(F32))
-            grad_mixed[part, :] = mm_nt(branch, w_out[...]).astype(BF16)
-            down = mm_nt(w_out[...], branch).astype(BF16)
-            grad_mixed_t[:, part] = down
-            product = down.astype(F32) * mixed[:, part].astype(F32)
-            for h in range(HEADS):
-                center[h, :, part] = sum_rows(product[h * HEAD_DIM : (h + 1) * HEAD_DIM, :])
-            logits = mm_nt(result, targets[0])
-            raised = jnp.exp(logits - jnp.max(logits, axis=1, keepdims=True))
-            sources = range(t * per_tile, (t + 1) * per_tile)
-            target_col = jnp.concatenate([columns(target[s]) for s in sources], axis=0)
-            mask_col = jnp.concatenate([columns(mask[s]) for s in sources], axis=0)
-            hit = jnp.sum(jnp.where(cand == target_col, raised, 0.0), axis=1, keepdims=True)
-            hit = hit / jnp.sum(raised, axis=1, keepdims=True)
-            ids = lax.broadcasted_iota(jnp.int32, (tile, 1), 0) + t * tile + place[3] * rows
-            counted = jnp.where((plan.key_time(ids) < length) & (mask_col == 1), 1.0, 0.0)
-            total_hit += jnp.sum(hit * counted, axis=0, keepdims=True)
-            total_count += jnp.sum(counted, axis=0, keepdims=True)
-        grad_w_out[...] = mm(mixed[...], act_buf[...])
-        lane = lax.broadcasted_iota(jnp.int32, (1, D), 1)
-        slot = batch * 2 * plan.clips + clip
-        scores = jnp.where(lane == slot, total_hit, 0.0)
-        vec[13:14, :] = scores + jnp.where(lane == slot + plan.clips, total_count, 0.0)
-
-
-def feed_forward(
-    plan, place, mixed, start, grad, mask, target, targets, w_out, bias_out, gain, shift,
-    w_up, bias_up, w_down, bias_down,
-):
-    rows = plan.rows
-    steps = FF // D
-
-    def full(shape):
-        return pl.BlockSpec(shape, lambda i, s: (0,) * len(shape))
-
-    return pl.pallas_call(
-        functools.partial(feed_kernel, plan),
-        grid_spec=pltpu.PrefetchScalarGridSpec(
-            num_scalar_prefetch=1,
-            grid=(steps,),
-            in_specs=[
-                full((D, rows)), full((rows, D)), full((rows, D)),
-                full(mask.shape), full(mask.shape),
-                pl.BlockSpec((1,) + targets.shape[1:], lambda i, s: (s[0], 0, 0)),
-                full((D, D)), full((D,)), full((D,)), full((D,)),
-                pl.BlockSpec((D, D), lambda i, s: (0, i)),
-                pl.BlockSpec((1, 1, D), lambda i, s: (i, 0, 0)),
-                pl.BlockSpec((D, D), lambda i, s: (i, 0)),
-                full((D,)),
-            ],
-            out_specs=[
-                full((rows, D)), full((rows, D)), full((rows, D)), full((D, rows)),
-                full((HEADS, 1, rows)),
-                pl.BlockSpec((2, 1, D, D), lambda i, s: (0, i, 0, 0)),
-                full((D, D)), full((VEC_ROWS, D)),
-            ],
-            scratch_shapes=[
-                pltpu.VMEM((rows, D), F32), pltpu.VMEM((rows, D), BF16),
-                pltpu.VMEM((rows, D), F32), pltpu.VMEM((rows, D), F32),
-                pltpu.VMEM((rows, D), BF16), pltpu.VMEM((rows, D), BF16),
-            ],
-        ),
-        out_shape=[
-            jax.ShapeDtypeStruct((rows, D), BF16),
-            jax.ShapeDtypeStruct((rows, D), F32),
-            jax.ShapeDtypeStruct((rows, D), BF16),
-            jax.ShapeDtypeStruct((D, rows), BF16),
-            jax.ShapeDtypeStruct((HEADS, 1, rows), F32),
-            jax.ShapeDtypeStruct((2, steps, D, D), BF16),
-            jax.ShapeDtypeStruct((D, D), F32),
-            jax.ShapeDtypeStruct((VEC_ROWS, D), F32),
-        ],
-        compiler_params=pltpu.CompilerParams(vmem_limit_bytes=VMEM_LIMIT),
-        cost_estimate=pl.CostEstimate(
-            flops=12 * rows * FF * D, bytes_accessed=20 * rows * D, transcendentals=2 * rows * FF
-        ),
-        name="feed_forward",
-    )(
-        place, mixed, start, grad, mask, target, targets, w_out, bias_out, gain, shift,
-        w_up, bias_up.reshape(steps, 1, D), w_down, bias_down,
-    )
-
-
 class Ring:
     def __init__(self, cut, at, half_src, own_half, core_in, mine, plane_in, part_buf, depth_in, total, sems):
         self.cut, self.at = cut, at
@@ -528,7 +390,7 @@
 
     def to_plane(self):
         self.core_copy().wait()
-        own = self.own_half().astype(F32) + self.core_in[...].astype(F32)
+        own = self.own_half[...].astype(F32) + self.core_in[...].astype(F32)
         self.mine[...] = own.astype(BF16)
         for copy in self.plane_copies():
             copy.start()
@@ -576,15 +438,23 @@
             copy.wait()
         self.last_copy().start()
 
+    def turn(self):
+        self.to_depth()
+        self.back_up()
+        self.back_wide()
+
     def end(self):
         self.last_copy().wait()
 
 
 class Cut:
-    def __init__(self, plan, rows):
-        self.rows = rows
+    def __init__(self, plan, rows, width, flat=False):
+        self.rows, self.width = rows, width
         self.n_plane = plan.freq * plan.batch
         self.n_depth = plan.tm // 2
+        self.flat = flat and rows // 2 % (16 * self.n_plane * self.n_depth) == 0
+        if self.flat:
+            self.n_plane, self.n_depth = self.n_plane * self.n_depth, 1
         self.half = rows // 2
         self.chunk = self.half // self.n_plane
         self.piece = self.chunk // self.n_depth
@@ -593,15 +463,11 @@
 
     def buffers(self):
         depth = self.piece if self.scatter else self.chunk
-        return [
-            pltpu.VMEM((self.half, D), BF16),
-            pltpu.VMEM((self.half, D), BF16),
-            pltpu.VMEM((self.half, D), BF16),
-            pltpu.VMEM((self.n_plane, self.chunk, D), BF16),
-            pltpu.VMEM((self.chunk, D), BF16),
-            pltpu.VMEM((self.n_depth, depth, D), BF16),
-            pltpu.VMEM((self.rows, D), BF16),
+        shapes = [
+            (self.half,), (self.half,), (self.n_plane, self.chunk), (self.chunk,),
+            (self.n_depth, depth), (self.rows,),
         ]
+        return [pltpu.VMEM(shape + (self.width,), BF16) for shape in shapes]
 
     def semaphores(self):
         dma = pltpu.SemaphoreType.DMA
@@ -624,92 +490,287 @@
         self.in_depth = [{"tm": v * 2 + self.core} for v in self.depths]
 
 
+class Flat:
+    def __init__(self, plan, place):
+        n_depth = plan.tm // 2
+        count = plan.freq * plan.batch * n_depth
+        self.core, self.partner, self.depth, self.in_depth = place.core, place.partner, 0, [None]
+        self.plane = place.plane * n_depth + place.depth
+        self.planes = [lax.rem(self.plane + k, count) for k in range(count)]
+        self.in_plane = [
+            {
+                "freq": v // n_depth // plan.batch,
+                "batch": v // n_depth % plan.batch,
+                "tm": v % n_depth * 2 + place.core,
+            }
+            for v in self.planes
+        ]
+
+
 def spot(first, count):
     return pl.ds(pl.multiple_of(first, 16), count)
 
 
-def back_kernel(
-    plan, wide_cut, cut, lengths, block_rows_in, payload, q_ref, qt_ref, k_ref, v_ref, do_ref, dot_ref,
-    log_total, center, start, grad_middle, mask, w_ref, gain, shift, dw_out, vec,
-    block_grid, input_grad, wide_out, reduced, vec_out,
+def rest_kernel(
+    plan, wide_cut, small_cuts, lengths,
+    mixed_in, start_in, grad_in, targets_in, w_out_in, w_up_in, w_down_in, w_qkv_in,
+    q_in, qt_in, k_in, v_in, log_total, mask, target,
+    ln1_gain, ln1_shift, bias_out, ln2_gain, ln2_shift, bias_up, bias_down,
+    block_grid, input_grad, wide_out, small_out, vec_out,
+    mixed, start, grad, targets, w_out, w_up, w_down, w_qkv, q_ref, qt_ref, k_ref, v_ref,
+    middle, second, down_sum, second_sum, act_buf, up_buf, payload, small_pay, do_ref, dot_ref,
+    center, block_out,
     kt_buf, score_a, score_b, prob_a, prob_b, dqt_sum, dk_all, dv_all, dk_in, dv_in,
-    hat_buf, grad_buf, weight, rows_buf, vec_buf, vec_core, vec_plane, vec_depth,
+    rows_buf, vec_buf, vec_core, vec_plane, vec_depth,
+    load_sem, grid_ss, grid_rs, kv_ss, kv_rs, rows_ss, rows_rs, local_sem, out_sem,
+    vec_core_sem, vec_plane_sem, vec_depth_sem,
     *rest,
 ):
-    bufs, sems = rest[:14], rest[14:]
-    wide_bufs, small_bufs = bufs[:7], bufs[7:]
-    wide_sems, small_sems = sems[:5], sems[5:10]
-    (grid_ss, grid_rs, kv_ss, kv_rs, rows_ss, rows_rs, local_sem, vec_core_sem,
-     vec_plane_sem, vec_depth_sem) = sems[10:]
     n, rows, keys, block_rows = plan.clips, plan.rows, plan.keys, plan.block_rows
     me, part = plan.place()
     at = Place(plan)
-    n_plane, n_depth = cut.n_plane, cut.n_depth
+    last_cut = small_cuts[-1]
+    flat = Flat(plan, at) if last_cut.flat else at
+    n_plane, n_depth = wide_cut.n_plane, wide_cut.n_depth
     peers = [lax.rem(me + k, n) for k in range(n)]
     sharers = [lax.rem(part + k, plan.share) for k in range(plan.share)]
     length = lengths[me]
 
-    own_half_copy = pltpu.make_async_copy(
-        payload.at[spot(at.core * wide_cut.half, wide_cut.half)], wide_bufs[0], local_sem.at[0]
-    )
-    wide = Ring(
-        wide_cut, at, payload.at[spot((1 - at.core) * wide_cut.half, wide_cut.half)],
-        lambda: wide_bufs[0][...], *wide_bufs[1:], wide_sems,
-    )
-    small = Ring(
-        cut, at, small_bufs[0], lambda: weight[spot(at.core * cut.half, cut.half), :],
-        *small_bufs[1:], small_sems,
-    )
+    loads = [
+        pltpu.make_async_copy(src, dst, load_sem.at[i])
+        for i, (src, dst) in enumerate(
+            (
+                (mixed_in, mixed), (w_out_in, w_out), (start_in, start), (w_up_in, w_up),
+                (w_down_in, w_down), (grad_in, grad), (targets_in.at[me], targets),
+                (k_in, k_ref), (qt_in, qt_ref), (v_in, v_ref), (q_in, q_ref), (w_qkv_in, w_qkv),
+            )
+        )
+    ]
+    for copy in loads:
+        copy.start()
     greet(
         [plan.member(peers[k], part) for k in range(1, n)]
         + [plan.sharer(sharers[k]) for k in range(1, plan.share)]
         + [at.partner]
-        + at.in_plane[1:]
-        + at.in_depth[1:]
+        + (flat.in_plane[1:] if last_cut.flat else at.in_plane[1:] + at.in_depth[1:])
     )
-    own_half_copy.start()
-    wide.begin()
-    home_copies = [
-        pltpu.make_async_copy(block_rows_in.at[me], block_grid.at[me], local_sem.at[1])
-    ]
+    steps = FF // CHUNK
+    wide, small = [], []
+    for i in range(steps):
+        mine, rest = rest[:11], rest[11:]
+        wide.append(
+            Ring(
+                wide_cut, at, payload.at[1 - at.core, i], payload.at[at.core, i], *mine[:6], mine[6:]
+            )
+        )
+    for p in range(PAIRS):
+        mine, rest = rest[:11], rest[11:]
+        small_cut = small_cuts[p]
+        away = small_pay.at[p, spot((1 - at.core) * small_cut.half, small_cut.half)]
+        own = small_pay.at[p, spot(at.core * small_cut.half, small_cut.half)]
+        small.append(Ring(small_cut, flat if small_cut.flat else at, away, own, *mine[:6], mine[6:]))
+
+    tile = min(TILE, rows)
+    tiles = [slice(i * tile, (i + 1) * tile) for i in range(rows // tile)]
+    gain2, shift2 = row(ln2_gain), row(ln2_shift)
+    bias_up_row = row(bias_up)
+    vec_buf[...] = jnp.zeros_like(vec_buf)
+    for copy in loads[:3]:
+        copy.wait()
+    for span in tiles:
+        rows_in = start[span, :].astype(F32) + mm_tn(mixed[:, span], w_out[...]) + row(bias_out)
+        middle[span, :] = rows_in
+        hat, _ = normalize(rows_in)
+        second[span, :] = (hat * gain2 + shift2).astype(BF16)
+    for copy in loads[3:6]:
+        copy.wait()
+    up_sums = []
+    for i in range(steps):
+        cols = slice(i * CHUNK, (i + 1) * CHUNK)
+        for t, span in enumerate(tiles):
+            hidden = mm(second[span, :], w_up[:, cols]) + bias_up_row[:, cols]
+            active, slope = gelu_parts(hidden)
+            active = active.astype(BF16)
+            act_buf[span, :] = active
+            down = mm(active, w_down[cols, :])
+            grad_up = (mm_nt(grad[span, :], w_down[cols, :]) * slope).astype(BF16)
+            up_buf[span, :] = grad_up
+            back = mm_nt(grad_up, w_up[:, cols])
+            if i == 0:
+                down_sum[span, :] = down
+                second_sum[span, :] = back
+            else:
+                down_sum[span, :] += down
+                second_sum[span, :] += back
+            if t == 0 and i >= 1:
+                wide[i - 1].to_plane()
+        grad_down = mm_tn(act_buf[...], grad[...]).astype(BF16)
+        for t in range(D // LANES):
+            payload[0, i, t * CHUNK : (t + 1) * CHUNK, :] = grad_down[:, t * LANES : (t + 1) * LANES]
+        grad_w = mm_tn(second[...], up_buf[...]).astype(BF16)
+        for t in range(CHUNK // LANES):
+            payload[1, i, t * D : (t + 1) * D, :] = grad_w[:, t * LANES : (t + 1) * LANES]
+        up_sums.append(sum_rows(up_buf[...].astype(F32)))
+        wide[i].begin()
+        if i >= 2:
+            wide[i - 2].to_depth()
+    up_sums = jnp.concatenate(up_sums, axis=1)
+    for i in range(FF // D):
+        vec_buf[9 + i : 10 + i, :] = up_sums[:, i * D : (i + 1) * D]
+    vec_buf[8:9, :] = sum_rows(grad[...].astype(F32))
+    loads[6].wait()
+    home_copies = []
+    cand = lax.broadcasted_iota(jnp.int32, (1, targets.shape[0]), 1)
+    total_hit = jnp.zeros((1, 1), F32)
+    total_count = jnp.zeros((1, 1), F32)
+    per_tile = tile // block_rows
+    for t, span in enumerate(tiles):
+        result = (middle[span, :] + down_sum[span, :] + row(bias_down)).astype(BF16)
+        for b in range(per_tile):
+            block_out[t * per_tile + b] = result[b * block_rows : (b + 1) * block_rows, :]
+        hat, scale = normalize(middle[span, :])
+        grad_second = second_sum[span, :]
+        vec_buf[6:7, :] += sum_rows(grad_second * hat)
+        vec_buf[7:8, :] += sum_rows(grad_second)
+        back = grad[span, :].astype(F32) + normalize_back(grad_second * gain2, hat, scale)
+        second_sum[span, :] = back
+        branch = back.astype(BF16)
+        up_buf[span, :D] = branch
+        vec_buf[5:6, :] += sum_rows(branch.astype(F32))
+        do_ref[span, :] = mm_nt(branch, w_out[...]).astype(BF16)
+        down = mm_nt(w_out[...], branch).astype(BF16)
+        dot_ref[:, span] = down
+        product = down.astype(F32) * mixed[:, span].astype(F32)
+        for h in range(HEADS):
+            center[h, :, span] = sum_rows(product[h * HEAD_DIM : (h + 1) * HEAD_DIM, :])
+        logits = mm_nt(result, targets[...])
+        raised = jnp.exp(logits - jnp.max(logits, axis=1, keepdims=True))
+        sources = range(t * per_tile, (t + 1) * per_tile)
+        target_col = jnp.concatenate([columns(target[s]) for s in sources], axis=0)
+        mask_col = jnp.concatenate([columns(mask[s]) for s in sources], axis=0)
+        hit = jnp.sum(jnp.where(cand == target_col, raised, 0.0), axis=1, keepdims=True)
+        hit = hit / jnp.sum(raised, axis=1, keepdims=True)
+        ids = lax.broadcasted_iota(jnp.int32, (tile, 1), 0) + t * tile + part * rows
+        counted = jnp.where((plan.key_time(ids) < length) & (mask_col == 1), 1.0, 0.0)
+        total_hit += sum_rows(hit * counted)
+        total_count += sum_rows(counted)
+        if t == 0:
+            wide[-1].to_plane()
+    home_copies.append(
+        pltpu.make_async_copy(block_out.at[me], block_grid.at[me], local_sem.at[0])
+    )
     for k in range(1, n):
         home_copies.append(
             remote(
-                block_rows_in.at[peers[k]], block_grid.at[me], grid_ss.at[k], grid_rs.at[k],
+                block_out.at[peers[k]], block_grid.at[me], grid_ss.at[k], grid_rs.at[k],
                 plan.member(peers[k], part),
             )
         )
-    for copy in home_copies:
-        copy.start()
-
-    def kv_copies():
+    home_copies[0].start()
+    wide[-3].back_up()
+    wide[-2].to_depth()
+    grad_w = mm(mixed[...], up_buf[:, :D]).astype(BF16)
+    for p in range(PAIRS):
+        small_pay[p, D:, :] = grad_w[p * PAIR : (p + 1) * PAIR, :]
+    lane = lax.broadcasted_iota(jnp.int32, (1, D), 1)
+    slot = lax.axis_index("batch") * 2 * n + me
+    scores = jnp.where(lane == slot, total_hit, 0.0)
+    vec_buf[13:14, :] = scores + jnp.where(lane == slot + n, total_count, 0.0)
+
+    gain1, shift1 = row(ln1_gain), row(ln1_shift)
+    hat_buf, normed, grad_buf, grad_middle = middle, second, down_sum, second_sum
+    for span in tiles:
+        hat, _ = normalize(start[span, :].astype(F32))
+        hat_buf[span, :] = hat
+        normed[span, :] = (hat * gain1 + shift1).astype(BF16)
+    loads[7].wait()
+    for i in range(keys // 256):
+        span = slice(i * 256, (i + 1) * 256)
+        ids = lax.broadcasted_iota(jnp.int32, (1, 256), 1) + i * 256
+        turned = k_ref[span, :].T
+        kt_buf[:, span] = jnp.where(plan.key_time(ids) < length, turned, jnp.zeros_like(turned))
+    dqt_sum[...] = jnp.zeros_like(dqt_sum)
+    for copy in loads[8:]:
+        copy.wait()
+
+    block = score_a.shape[0]
+    per_part = rows // block
+    lane = lax.broadcasted_iota(jnp.int32, (1, PAIR), 1)
+    owns = [lane // HEAD_DIM == e for e in range(2)]
+    zero = jnp.zeros((), BF16)
+    per_pair = per_part * plan.share
+    bodies = PAIRS * per_pair
+
+    def kv_copies(p):
         return [
             remote(
-                src.at[sharers[k]], dst.at[k], kv_ss.at[i, k], kv_rs.at[i, k],
+                src.at[p, sharers[k]], dst.at[p, k], kv_ss.at[i, p, k], kv_rs.at[i, p, k],
                 plan.sharer(sharers[k]),
             )
             for i, (src, dst) in enumerate(((dk_all, dk_in), (dv_all, dv_in)))
             for k in range(1, plan.share)
         ]
 
-    tile = min(256, rows)
-    for i in range(keys // tile):
-        span = slice(i * tile, (i + 1) * tile)
-        ids = lax.broadcasted_iota(jnp.int32, (1, tile), 1) + i * tile
-        turned = k_ref[span, :].T
+    def send_keys(p):
+        for copy in kv_copies(p):
+            copy.start()
+
+    def finish_pair(p):
+        for copy in kv_copies(p):
+            copy.wait()
+        cols = slice(p * PAIR, (p + 1) * PAIR)
+        parts = [(dqt_sum[cols, :] * SCALE).T.astype(BF16)]
+        ids = lax.broadcasted_iota(jnp.int32, (rows, 1), 0) + part * rows
         live = plan.key_time(ids) < length
-        kt_buf[:, span] = jnp.where(live, turned, jnp.zeros_like(turned))
-    dqt_sum[...] = jnp.zeros_like(dqt_sum)
-
-    block = score_a.shape[0]
-    per_part = rows // block
-    lane = lax.broadcasted_iota(jnp.int32, (1, PAIR), 1)
-    owns = [lane // HEAD_DIM == e for e in range(2)]
-    zero = jnp.zeros((), BF16)
-    bodies = PAIRS * per_part * plan.share
+        for own, buf in ((dk_all, dk_in), (dv_all, dv_in)):
+            summed = own[p, part].astype(F32)
+            for k in range(1, plan.share):
+                summed = summed + buf[p, k].astype(F32)
+            parts.append(jnp.where(live, summed, 0.0).astype(BF16))
+        vec_buf[3:4, cols] = sum_rows(parts[0].astype(F32))
+        vec_buf[4:5, cols] = sum_rows(parts[2].astype(F32))
+        project = jnp.concatenate(parts, axis=1)
+        small_pay[p, :D, :] = mm_tn(normed[...], project).astype(BF16)
+        small[p].begin()
+        weights = [w_qkv[:, i * D + p * PAIR : i * D + (p + 1) * PAIR] for i in range(3)]
+        back = mm_nt(project, jnp.concatenate(weights, axis=1))
+        if p == 0:
+            grad_buf[...] = back
+        else:
+            grad_buf[...] += back
+
+    def save(i, src, dst):
+        return pltpu.make_async_copy(src, dst, out_sem.at[i])
+
+    saves = [save(i, wide[i].total, wide_out.at[i]) for i in range(steps)]
+    saves += [save(steps + p, small[p].total, small_out.at[p]) for p in range(PAIRS)]
+
+    def wide_end(i):
+        wide[i].end()
+        saves[i].start()
+
+    def small_end(p):
+        small[p].end()
+        saves[steps + p].start()
+
+    last_other = per_pair - per_part - 1
+    events = [
+        (last_other + p * per_pair, functools.partial(send_keys, p)) for p in range(PAIRS)
+    ] + [(p * per_pair + per_pair - 1, functools.partial(finish_pair, p)) for p in range(PAIRS - 1)]
+    for when, event in (
+        (0, wide[0].back_wide), (0, wide[2].to_depth), (1, wide[1].back_up), (2, wide[2].back_up),
+        (3, wide[1].back_wide), (3, wide[0].back_core), (4, small[0].to_plane),
+        (4, wide[2].back_wide), (4, functools.partial(wide_end, 0)), (6, wide[1].back_core),
+        (6, small[0].to_depth), (7, wide[2].back_core), (7, functools.partial(wide_end, 1)),
+        (8, small[0].back_up), (8, small[1].to_plane), (8, functools.partial(wide_end, 2)),
+        (10, small[0].back_wide), (10, small[1].to_depth),
+    ):
+        events.append((when * bodies // 12, event))
+    for k in range(1, n):
+        events.append((GRID_AT[k % len(GRID_AT)] * bodies // 12, home_copies[k].start))
 
     def body(i, carry):
-        order, pair = i // PAIRS, i % PAIRS
+        pair, order = i // per_pair, i % per_pair
         owner = lax.rem(part + 1 + order // per_part, plan.share)
         begin = order % per_part * block
         span = pl.ds(pl.multiple_of(owner * rows + begin, block), block)
@@ -726,59 +787,14 @@
             grad_v.append(mm(prob.astype(BF16), jnp.where(owns[e], do_ref[:, cols], zero)))
             grad_k.append(mm(grad_scores, jnp.where(owns[e], q_ref[:, cols], zero)))
             dqt_sum[head, :] += mm(kt_buf[head, span], grad_scores)
-        dk_all[owner, inside, cols] = (grad_k[0] + grad_k[1]).astype(BF16)
-        dv_all[owner, inside, cols] = (grad_v[0] + grad_v[1]).astype(BF16)
-
-        def at_step(step, do):
-            pl.when(i == step)(do)
-
-        def to_plane():
-            own_half_copy.wait()
-            wide.to_plane()
-
-        def send_keys():
-            for copy in kv_copies():
-                copy.start()
-
-        at_step(1, to_plane)
-        at_step(bodies - 6, wide.to_depth)
-        at_step(bodies - 4, wide.back_up)
-        at_step(bodies - 3, wide.back_wide)
-        at_step(bodies - PAIRS * per_part - 1, send_keys)
+        dk_all[pair, owner, inside, :] = (grad_k[0] + grad_k[1]).astype(BF16)
+        dv_all[pair, owner, inside, :] = (grad_v[0] + grad_v[1]).astype(BF16)
+        for when, event in events:
+            pl.when(i == when)(event)
         return carry
 
     lax.fori_loop(0, bodies, body, 0)
-
-    gain_row, shift_row = row(gain), row(shift)
-    dq = (dqt_sum[...] * SCALE).T.astype(BF16)
-    normed = []
-    for i in range(rows // tile):
-        span = slice(i * tile, (i + 1) * tile)
-        hat, _ = normalize(start[span, :].astype(F32))
-        hat_buf[span, :] = hat
-        normed.append((hat * gain_row + shift_row).astype(BF16))
-    normed = jnp.concatenate(normed, axis=0)
-    weight[3 * D :, :] = dw_out[...]
-    weight[:D, :] = mm_tn(normed, dq)
-    grad_buf[...] = mm_nt(dq, w_ref[:, :D])
-    vec_buf[...] = vec[...]
-    vec_buf[3:4, :] = sum_rows(dq.astype(F32))
-    for copy in kv_copies():
-        copy.wait()
-    ids = lax.broadcasted_iota(jnp.int32, (rows, 1), 0)
-    live = plan.key_time(ids + part * rows) < length
-    for i, (own, buf) in enumerate(((dk_all, dk_in), (dv_all, dv_in))):
-        summed = own[part].astype(F32)
-        for k in range(1, plan.share):
-            summed = summed + buf[k].astype(F32)
-        summed = jnp.where(live, summed, 0.0).astype(BF16)
-        cols = slice((1 + i) * D, (2 + i) * D)
-        weight[cols, :] = mm_tn(normed, summed)
-        grad_buf[...] += mm_nt(summed, w_ref[:, cols])
-        if i == 1:
-            vec_buf[4:5, :] = sum_rows(summed.astype(F32))
-    small_bufs[0][...] = weight[spot((1 - at.core) * cut.half, cut.half), :].astype(BF16)
-    small.begin()
+    finish_pair(PAIRS - 1)
 
     row_copies = []
     grad_embed = jnp.zeros((1, D), F32)
@@ -792,26 +808,31 @@
         grad_normed = grad_buf[span, :]
         grad_gain += sum_rows(grad_normed * hat)
         grad_shift += sum_rows(grad_normed)
-        grad_start = grad_middle[span, :] + normalize_back(grad_normed * gain_row, hat, scale)
+        grad_start = grad_middle[span, :] + normalize_back(grad_normed * gain1, hat, scale)
         masked = columns(mask[owner]) == 1
         grad_embed += sum_rows(jnp.where(masked, grad_start, 0.0))
         rows_buf[owner] = jnp.where(masked, 0.0, grad_start).astype(BF16)
         if k == 0:
-            copy = pltpu.make_async_copy(rows_buf.at[owner], input_grad.at[me], local_sem.at[2])
+            copy = pltpu.make_async_copy(rows_buf.at[owner], input_grad.at[me], local_sem.at[1])
         else:
             copy = remote(
                 rows_buf.at[owner], input_grad.at[me], rows_ss.at[k], rows_rs.at[k],
                 plan.member(owner, part),
             )
-        copy.start()
         row_copies.append(copy)
+        if k < WAVES[0]:
+            copy.start()
+        if k == 1:
+            small[2].to_plane()
+        if k == 3:
+            small[1].back_up()
+        if k == 5:
+            small[0].back_core()
     vec_buf[0:1, :] = grad_embed
     vec_buf[1:2, :] = grad_gain
     vec_buf[2:3, :] = grad_shift
     vec_copy = remote(vec_buf, vec_core, vec_core_sem.at[0], vec_core_sem.at[1], at.partner)
     vec_copy.start()
-    small.to_plane()
-    wide.back_core()
     vec_copy.wait()
     vec_plane[at.plane] = vec_buf[...] + vec_core[...]
     vec_plane_copies = []
@@ -822,10 +843,11 @@
         )
         copy.start()
         vec_plane_copies.append(copy)
-    small.to_depth()
-    wide.end()
-    wide_copy = pltpu.make_async_copy(wide.total, wide_out, local_sem.at[0])
-    wide_copy.start()
+    small[2].turn()
+    small[1].back_wide()
+    for copy in row_copies[WAVES[0] : WAVES[1]]:
+        copy.start()
+    small_end(0)
     for copy in vec_plane_copies:
         copy.wait()
     summed = vec_plane[0]
@@ -840,133 +862,144 @@
         )
         copy.start()
         vec_depth_copies.append(copy)
-    small.back_up()
-    small.back_wide()
+    for copy in row_copies[WAVES[1] :]:
+        copy.start()
+    small[1].back_core()
+    small[2].back_core()
+    small_end(1)
     for copy in vec_depth_copies:
         copy.wait()
     summed = vec_depth[0]
     for k in range(1, n_depth):
         summed = summed + vec_depth[k]
     vec_out[...] = summed
-    small.back_core()
-    small.end()
-    copy = pltpu.make_async_copy(small.total, reduced, local_sem.at[3])
-    copy.start()
-    for other in row_copies + home_copies + [wide_copy, copy]:
-        other.wait()
-
-
-def back(
-    plan, lengths, block_out, payload, queries, queries_t, key_rows, value_rows, grad_mixed,
-    grad_mixed_t, log_total, center, start, grad_middle, mask, w_qkv, gain, shift, dw_out, vec,
-):
+    small_end(2)
+    for copy in row_copies + home_copies + saves:
+        copy.wait()
+
+
+def rest(plan, lengths, mixed, start, grad, targets, weights, q, qt, k, v, log_total, mask, target, vectors):
     n, rows, keys = plan.clips, plan.rows, plan.keys
-    wide_cut, cut = Cut(plan, 2 * FF), Cut(plan, 4 * D)
+    steps = FF // CHUNK
+    wide_cut = Cut(plan, 2 * CHUNK * D // LANES, LANES)
+    small_cuts = [Cut(plan, D + PAIR, D, flat=p == PAIRS - 1) for p in range(PAIRS)]
+    small_cut = small_cuts[0]
     dma = pltpu.SemaphoreType.DMA
     vec_shape = (VEC_ROWS, D)
     block = min(512, rows)
     blocks = (n, plan.block_rows, D)
-    shared = pltpu.VMEM((plan.share, rows, D), BF16)
+    shared = pltpu.VMEM((PAIRS, plan.share, rows, PAIR), BF16)
     pane = pltpu.VMEM((block, rows), F32)
+    loaded = (mixed, start, grad, targets[0], *weights, q, qt, k, v)
+    rings = []
+    for cut in [wide_cut] * steps + small_cuts:
+        rings += cut.buffers() + cut.semaphores()
     return pl.pallas_call(
-        functools.partial(back_kernel, plan, wide_cut, cut),
+        functools.partial(rest_kernel, plan, wide_cut, small_cuts),
         out_shape=[
             jax.ShapeDtypeStruct(blocks, BF16),
             jax.ShapeDtypeStruct(blocks, BF16),
-            jax.ShapeDtypeStruct((wide_cut.rows, D), BF16),
-            jax.ShapeDtypeStruct((cut.rows, D), BF16),
+            jax.ShapeDtypeStruct((steps, wide_cut.rows, LANES), BF16),
+            jax.ShapeDtypeStruct((PAIRS, small_cut.rows, D), BF16),
             jax.ShapeDtypeStruct(vec_shape, F32),
         ],
-        in_specs=[pl.BlockSpec(memory_space=pltpu.SMEM)] + [ANY] * 2 + [VMEM] * 16,
+        in_specs=[pl.BlockSpec(memory_space=pltpu.SMEM)] + [ANY] * 12 + [VMEM] * 10,
         out_specs=[ANY] * 4 + [VMEM],
-        scratch_shapes=[
+        scratch_shapes=[pltpu.VMEM(x.shape, BF16) for x in loaded]
+        + [
+            pltpu.VMEM((rows, D), F32), pltpu.VMEM((rows, D), BF16),
+            pltpu.VMEM((rows, D), F32), pltpu.VMEM((rows, D), F32),
+            pltpu.VMEM((rows, CHUNK), BF16), pltpu.VMEM((rows, CHUNK), BF16),
+            pltpu.VMEM((2, steps, CHUNK * D // LANES, LANES), BF16),
+            pltpu.VMEM((PAIRS, small_cut.rows, D), BF16),
+            pltpu.VMEM((rows, D), BF16), pltpu.VMEM((D, rows), BF16),
+            pltpu.VMEM((HEADS, 1, rows), F32), pltpu.VMEM(blocks, BF16),
             pltpu.VMEM((D, keys), BF16), pane, pane, pane, pane, pltpu.VMEM((D, rows), F32),
             shared, shared, shared, shared,
-            pltpu.VMEM((rows, D), F32),
-            pltpu.VMEM((rows, D), F32),
-            pltpu.VMEM((cut.rows, D), F32),
             pltpu.VMEM(blocks, BF16),
             pltpu.VMEM(vec_shape, F32),
             pltpu.VMEM(vec_shape, F32),
-            pltpu.VMEM((cut.n_plane,) + vec_shape, F32),
-            pltpu.VMEM((cut.n_depth,) + vec_shape, F32),
-            *wide_cut.buffers(), *cut.buffers(), *wide_cut.semaphores(), *cut.semaphores(),
-            dma((n,)), dma((n,)), dma((2, plan.share)), dma((2, plan.share)), dma((n,)), dma((n,)),
-            dma((4,)), dma((2,)), dma((2, cut.n_plane)), dma((2, cut.n_depth)),
+            pltpu.VMEM((wide_cut.n_plane,) + vec_shape, F32),
+            pltpu.VMEM((wide_cut.n_depth,) + vec_shape, F32),
+            dma((12,)), dma((n,)), dma((n,)),
+            dma((2, PAIRS, plan.share)), dma((2, PAIRS, plan.share)), dma((n,)), dma((n,)),
+            dma((2,)), dma((steps + PAIRS,)), dma((2,)),
+            dma((2, wide_cut.n_plane)), dma((2, wide_cut.n_depth)),
+            *rings,
         ],
         compiler_params=pltpu.CompilerParams(
             collective_id=1, has_side_effects=True, vmem_limit_bytes=VMEM_LIMIT
         ),
-        name="back",
-    )(
-        lengths, block_out, payload, queries, queries_t, key_rows, value_rows, grad_mixed,
-        grad_mixed_t, log_total, center, start, grad_middle, mask, w_qkv, gain, shift, dw_out, vec,
-    )
-
-
-def unpack_kernel(plan, place, reduced, wide, vec, *outs):
+        name="rest",
+    )(lengths, mixed, start, grad, targets, *weights, q, qt, k, v, log_total, mask, target, *vectors)
+
+
+def unpack_kernel(plan, small, wide, vec, *outs):
     w_qkv, w_out, w_up, w_down, bias_up, soft = outs[:6]
     step = pl.program_id(0)
-    w_down[...] = wide[0, 0].astype(F32)
-    w_up[...] = wide[1, 0].astype(F32)
-
-    @pl.when(step < 3)
+    for t in range(D // LANES):
+        at = slice(t * LANES, (t + 1) * LANES)
+        w_down[:, at] = wide[0, 0, t * CHUNK : (t + 1) * CHUNK, :].astype(F32)
+        part = pl.ds(pl.multiple_of(t * D + step * PAIR, PAIR), PAIR)
+        w_qkv[:, part] = small[0, :D, at].astype(F32)
+    for t in range(CHUNK // LANES):
+        w_up[:, t * LANES : (t + 1) * LANES] = wide[0, 1, t * D : (t + 1) * D, :].astype(F32)
+    w_out[...] = small[0, D:, :].astype(F32)
+
+    @pl.when(step == 0)
     def _():
-        w_qkv[...] = reduced[0].astype(F32)
-
-    @pl.when(step == 3)
-    def _():
-        w_out[...] = reduced[0].astype(F32)
         for i, out in enumerate(outs[6:]):
             out[...] = vec[i, :]
         for i in range(FF // D):
             bias_up[i * D : (i + 1) * D] = vec[9 + i, :]
         scores = vec[13:14, :]
-        lane = lax.broadcasted_iota(jnp.int32, (plan.clips, D), 1)
-        slot = place[2] * 2 * plan.clips + lax.broadcasted_iota(jnp.int32, (plan.clips, D), 0)
+        n = plan.clips
+        lane = lax.broadcasted_iota(jnp.int32, (n, D), 1)
+        sub = lax.broadcasted_iota(jnp.int32, (n, D), 0)
+        slot = lax.axis_index("batch") * 2 * n + sub
         hits = jnp.sum(jnp.where(lane == slot, scores, 0.0), axis=1, keepdims=True)
-        counts = jnp.sum(jnp.where(lane == slot + plan.clips, scores, 0.0), axis=1, keepdims=True)
-        soft[...] = hits / jnp.maximum(counts, 1.0)
-
-
-def unpack(plan, place, reduced, wide, vec):
+        counts = jnp.sum(jnp.where(lane == slot + n, scores, 0.0), axis=1, keepdims=True)
+        means = hits / jnp.maximum(counts, 1.0)
+        soft[...] = jnp.sum(jnp.where(lane == sub, means, 0.0), axis=0)[:n]
+
+
+def unpack(plan, small, wide, vec):
     vector = jax.ShapeDtypeStruct((D,), F32)
+    steps = FF // CHUNK
+    assert steps == PAIRS
 
     def full(shape):
-        return pl.BlockSpec(shape, lambda i, s: (0,) * len(shape))
+        return pl.BlockSpec(shape, lambda i: (0,) * len(shape))
 
     return pl.pallas_call(
         functools.partial(unpack_kernel, plan),
-        grid_spec=pltpu.PrefetchScalarGridSpec(
-            num_scalar_prefetch=1,
-            grid=(4,),
-            in_specs=[
-                pl.BlockSpec((1, D, D), lambda i, s: (i, 0, 0)),
-                pl.BlockSpec((2, 1, D, D), lambda i, s: (0, i, 0, 0)),
-                full((VEC_ROWS, D)),
-            ],
-            out_specs=[
-                pl.BlockSpec((D, D), lambda i, s: (0, jnp.minimum(i, 2))),
-                full((D, D)),
-                pl.BlockSpec((D, D), lambda i, s: (0, i)),
-                pl.BlockSpec((D, D), lambda i, s: (i, 0)),
-                full((FF,)),
-                full((plan.clips, 1)),
-            ]
-            + [full((D,))] * 9,
-        ),
+        grid=(steps,),
+        in_specs=[
+            pl.BlockSpec((1, D + PAIR, D), lambda i: (i, 0, 0)),
+            pl.BlockSpec((1, 2, CHUNK * D // LANES, LANES), lambda i: (i, 0, 0, 0)),
+            full((VEC_ROWS, D)),
+        ],
+        out_specs=[
+            full((D, 3 * D)),
+            pl.BlockSpec((PAIR, D), lambda i: (i, 0)),
+            pl.BlockSpec((D, CHUNK), lambda i: (0, i)),
+            pl.BlockSpec((CHUNK, D), lambda i: (i, 0)),
+            full((FF,)),
+            full((plan.clips,)),
+        ]
+        + [full((D,))] * 9,
         out_shape=[
             jax.ShapeDtypeStruct((D, 3 * D), F32),
             jax.ShapeDtypeStruct((D, D), F32),
             jax.ShapeDtypeStruct((D, FF), F32),
             jax.ShapeDtypeStruct((FF, D), F32),
             jax.ShapeDtypeStruct((FF,), F32),
-            jax.ShapeDtypeStruct((plan.clips, 1), F32),
+            jax.ShapeDtypeStruct((plan.clips,), F32),
         ]
         + [vector] * 9,
         compiler_params=pltpu.CompilerParams(vmem_limit_bytes=VMEM_LIMIT),
         name="unpack",
-    )(place, reduced.reshape(4, D, D), wide.reshape(2, FF // D, D, D), vec)
+    )(small, wide.reshape(steps, 2, CHUNK * D // LANES, LANES), vec)
 
 
 def per_device(
@@ -976,38 +1009,26 @@
     ln2_gain, ln2_shift, w_up, bias_up, w_down, bias_down,
 ):
     n, rows, block_rows = plan.clips, plan.rows, plan.block_rows
-    clip, part = plan.place()
-    length = lax.dynamic_index_in_dim(clip_lengths, clip, keepdims=False)
-    place = jnp.stack([clip, length, lax.axis_index("batch"), part]).astype(jnp.int32)
     (start, queries, queries_t, key_rows, value_rows, mixed, log_total, mask, target, grad) = front(
         plan, clip_lengths, patches.reshape(n, block_rows, D), patch_mask, target_index,
         out_grad.reshape(n, block_rows, D), mask_embed, ln1_gain, ln1_shift, w_qkv, bias_q, bias_v,
     )
-    start = start.reshape(rows, D)
-    queries = queries.reshape(rows, D)
-    grad = grad.reshape(rows, D)
-    block_out, grad_middle, grad_mixed, grad_mixed_t, center, payload, grad_w_out, vec = (
-        feed_forward(
-            plan, place, mixed, start, grad, mask, target, targets, w_out, bias_out,
-            ln2_gain, ln2_shift, w_up, bias_up, w_down, bias_down,
-        )
+    block_grid, input_grad, wide, small, vec = rest(
+        plan, clip_lengths, mixed, start.reshape(rows, D), grad.reshape(rows, D), targets,
+        (w_out, w_up, w_down, w_qkv), queries.reshape(rows, D), queries_t, key_rows, value_rows,
+        log_total, mask, target,
+        (ln1_gain, ln1_shift, bias_out, ln2_gain, ln2_shift, bias_up, bias_down),
     )
-    block_grid, input_grad, wide, reduced, vec = back(
-        plan, clip_lengths, block_out.reshape(n, block_rows, D), payload.reshape(2 * FF, D),
-        queries, queries_t, key_rows, value_rows, grad_mixed, grad_mixed_t, log_total, center,
-        start, grad_middle, mask, w_qkv, ln1_gain, ln1_shift, grad_w_out, vec,
+    grad_w_qkv, grad_w_out, grad_w_up, grad_w_down, grad_bias_up, soft_accuracy, *vectors = unpack(
+        plan, small, wide, vec
     )
-    grad_w_qkv, grad_w_out, grad_w_up, grad_w_down, grad_bias_up, soft, *vectors = unpack(
-        plan, place, reduced, wide, vec
-    )
-    block_grid = block_grid.reshape(patches.shape)
     (grad_mask_embed, grad_ln1_gain, grad_ln1_shift, grad_bias_q, grad_bias_v, grad_bias_out,
      grad_ln2_gain, grad_ln2_shift, grad_bias_down) = vectors
     return (
-        block_grid, input_grad.reshape(patches.shape), grad_mask_embed, grad_ln1_gain,
-        grad_ln1_shift, grad_w_qkv, grad_bias_q, grad_bias_v, grad_w_out, grad_bias_out,
-        grad_ln2_gain, grad_ln2_shift, grad_w_up, grad_bias_up, grad_w_down, grad_bias_down,
-        soft.reshape(n),
+        block_grid.reshape(patches.shape), input_grad.reshape(patches.shape), grad_mask_embed,
+        grad_ln1_gain, grad_ln1_shift, grad_w_qkv, grad_bias_q, grad_bias_v, grad_w_out,
+        grad_bias_out, grad_ln2_gain, grad_ln2_shift, grad_w_up, grad_bias_up, grad_w_down,
+        grad_bias_down, soft_accuracy,
     )
 
 

time: 184 us -> 168 us (0.913)
  Pallas kernels: 174 us -> 163 us
  other arithmetic: 2.64 us -> 0 us
  local copies, waits for them, and re-layouts: 4.3 us -> 2.28 us
    pallas_call x3 -> x2, Pallas kernels: 130 us -> 120 us  [the longest x1 114 us: rest(): pl.pallas_call(functools.partial(rest_kernel, plan, wide_cut, small_cuts)...]
where the time goes in v4:
time: 168 us; the launch traced here: 167 us
  Pallas kernels  163 us (97%)
  local copies, waits for them, and re-layouts  2.28 us (1%)
    pallas_call x1, Pallas kernels, rest(): pl.pallas_call(functools.partial(rest_kernel, plan, wide_cut, small_cuts)...  114 us
    pallas_call x1, Pallas kernels, front(): pl.pallas_call(functools.partial(front_kernel, plan), out_shape=[jax.Shap...  43.6 us
    pallas_call x1, Pallas kernels, unpack(): pl.pallas_call(functools.partial(unpack_kernel, plan), grid=(steps,), in_...  5.78 us

profile of v4, /device:TPU:25, one launch (start us, length us, event | category | flops | bytes accessed | tf_op | source)
XLA Modules:
  0.0 166.5 jit_solution(6534487096892807263)
XLA Ops:
  0.7 43.6 %front.1 = (bf16[8,128,384]{2,1,0:T(8,128)(2,1)}, bf16[8,128,384]{2,1,0:T(8,128)(2,1)}, bf16[384,1024]{1,0:T(8,128)(2,1)}, bf16[2048,384]{1,0:T(8,128)(2,1)}, bf...) custom-call(s32[8]{0:T(128)} %lengths.3, ...), custom_call_target="tpu_custom_call" | custom-call | tf_op jit(solution)/shard_map/front/pallas_call | solution.py:288
  44.3 114.0 %rest.1 = (bf16[8,128,384]{2,1,0:T(8,128)(2,1)}, bf16[8,128,384]{2,1,0:T(8,128)(2,1)}, bf16[3,3072,128]{2,1,0:T(8,128)(2,1)}, bf16[3,512,384]{2,1,0:T(8,128)(2,1)}, f32[16,384]{1,0:T(8,128)}) custom-call(s32[8]{0:T(128)} %lengths.3, bf16[384,1024]{1,0:T(8,128)(2,1)} %get-tuple-element.47.mixed_in, bf16[1024,384]{1,0:T(8,128)(2,1)} %bitcast.11, ...), custom_call_target="tpu_custom_call" | custom-call | tf_op jit(solution)/shard_map/rest/pallas_call | solution.py:897
  158.3 0.0 copy-start.1
  158.3 5.8 %unpack.1 = (f32[384,1152]{1,0:T(8,128)}, f32[384,384]{1,0:T(8,128)}, f32[384,1536]{1,0:T(8,128)}, f32[1536,384]{1,0:T(8,128)}, f32[1536]{0:T(1024)}, /*index=5*...) custom-call(bf16[3,512,384]{2,1,0:T(8,128)(2,1)} %get-tuple-element., ...), custom_call_target="tpu_custom_call" | custom-call | tf_op jit(solution)/shard_map/unpack/pallas_call | solution.py:974
  164.1 0.0 copy-start
  164.1 0.0 copy-done.1
  164.1 0.9 copy.39
  165.0 0.5 copy-done
  165.5 0.9 copy.40
Async XLA Ops:
  158.3 5.8 %copy-start.1 = (bf16[8,128,384]{2,1,0:T(8,128)(2,1)S(1)}, bf16[8,128,384]{2,1,0:T(8,128)(2,1)}, u32[]{:S(2)}) copy-start(bf16[8,128,384]{2,1,0:T(8,128)(2,1)} %get-tuple-element.57) | copy-start | bytes 2359300
  164.1 1.4 copy-start

commit v5 on v4

--- a/solution.py
+++ b/solution.py
@@ -19,7 +19,7 @@
 VEC_ROWS = 16
 LANES = 128
 CHUNK = 512
-TILE = 512
+TILE = 1024
 GRID_AT = (0, 1, 2, 4, 5, 6, 8, 9)
 WAVES = (4, 6)
 MESH = pl.DeviceIdType.MESH
@@ -843,10 +843,10 @@
         )
         copy.start()
         vec_plane_copies.append(copy)
-    small[2].turn()
-    small[1].back_wide()
+    small[2].to_depth()
     for copy in row_copies[WAVES[0] : WAVES[1]]:
         copy.start()
+    small[1].back_wide()
     small_end(0)
     for copy in vec_plane_copies:
         copy.wait()
@@ -862,10 +862,11 @@
         )
         copy.start()
         vec_depth_copies.append(copy)
+    small[2].back_up()
     for copy in row_copies[WAVES[1] :]:
         copy.start()
     small[1].back_core()
-    small[2].back_core()
+    small[2].back_wide()
     small_end(1)
     for copy in vec_depth_copies:
         copy.wait()
@@ -873,6 +874,7 @@
     for k in range(1, n_depth):
         summed = summed + vec_depth[k]
     vec_out[...] = summed
+    small[2].back_core()
     small_end(2)
     for copy in row_copies + home_copies + saves:
         copy.wait()
@@ -882,7 +884,7 @@
     n, rows, keys = plan.clips, plan.rows, plan.keys
     steps = FF // CHUNK
     wide_cut = Cut(plan, 2 * CHUNK * D // LANES, LANES)
-    small_cuts = [Cut(plan, D + PAIR, D, flat=p == PAIRS - 1) for p in range(PAIRS)]
+    small_cuts = [Cut(plan, D + PAIR, D, flat=False) for p in range(PAIRS)]
     small_cut = small_cuts[0]
     dma = pltpu.SemaphoreType.DMA
     vec_shape = (VEC_ROWS, D)

time: 168 us -> 154 us (0.917)
  Pallas kernels: 163 us -> 151 us
    pallas_call x1, Pallas kernels: 114 us -> 101 us  [rest(): pl.pallas_call(functools.partial(rest_kernel, plan, wide_cut, small_cuts)...]
where the time goes in v5:
time: 154 us
  Pallas kernels  151 us (98%)
  local copies, waits for them, and re-layouts  2.28 us (1%)
    pallas_call x1, Pallas kernels, rest(): pl.pallas_call(functools.partial(rest_kernel, plan, wide_cut, small_cuts)...  101 us
    pallas_call x1, Pallas kernels, front(): pl.pallas_call(functools.partial(front_kernel, plan), out_shape=[jax.Shap...  43.5 us
    pallas_call x1, Pallas kernels, unpack(): pl.pallas_call(functools.partial(unpack_kernel, plan), grid=(steps,), in_...  5.78 us

profile of v5, /device:TPU:25, one launch (start us, length us, event | category | flops | bytes accessed | tf_op | source)
XLA Modules:
  0.0 153.8 jit_solution(1417353035929434311)
XLA Ops:
  0.7 43.5 %front.1 = (bf16[8,128,384]{2,1,0:T(8,128)(2,1)}, bf16[8,128,384]{2,1,0:T(8,128)(2,1)}, bf16[384,1024]{1,0:T(8,128)(2,1)}, bf16[2048,384]{1,0:T(8,128)(2,1)}, bf...) custom-call(s32[8]{0:T(128)} %lengths.3, ...), custom_call_target="tpu_custom_call" | custom-call | tf_op jit(solution)/shard_map/front/pallas_call | solution.py:288
  44.2 101.5 %rest.1 = (bf16[8,128,384]{2,1,0:T(8,128)(2,1)}, bf16[8,128,384]{2,1,0:T(8,128)(2,1)}, bf16[3,3072,128]{2,1,0:T(8,128)(2,1)}, bf16[3,512,384]{2,1,0:T(8,128)(2,1)}, f32[16,384]{1,0:T(8,128)}) custom-call(s32[8]{0:T(128)} %lengths.3, bf16[384,1024]{1,0:T(8,128)(2,1)} %get-tuple-element.47.mixed_in, bf16[1024,384]{1,0:T(8,128)(2,1)} %bitcast.11, ...), custom_call_target="tpu_custom_call" | custom-call | tf_op jit(solution)/shard_map/rest/pallas_call | solution.py:899
  145.7 0.0 copy-start.1
  145.7 5.8 %unpack.1 = (f32[384,1152]{1,0:T(8,128)}, f32[384,384]{1,0:T(8,128)}, f32[384,1536]{1,0:T(8,128)}, f32[1536,384]{1,0:T(8,128)}, f32[1536]{0:T(1024)}, /*index=5*...) custom-call(bf16[3,512,384]{2,1,0:T(8,128)(2,1)} %get-tuple-element., ...), custom_call_target="tpu_custom_call" | custom-call | tf_op jit(solution)/shard_map/unpack/pallas_call | solution.py:976
  151.5 0.0 copy-start
  151.5 0.0 copy-done.1
  151.5 0.9 copy.39
  152.4 0.5 copy-done
  152.9 0.9 copy.40
Async XLA Ops:
  145.7 5.8 %copy-start.1 = (bf16[8,128,384]{2,1,0:T(8,128)(2,1)S(1)}, bf16[8,128,384]{2,1,0:T(8,128)(2,1)}, u32[]{:S(2)}) copy-start(bf16[8,128,384]{2,1,0:T(8,128)(2,1)} %get-tuple-element.57) | copy-start | bytes 2359300
  151.5 1.4 copy-start

commit v6 on v5

--- a/solution.py
+++ b/solution.py
@@ -822,9 +822,9 @@
         row_copies.append(copy)
         if k < WAVES[0]:
             copy.start()
-        if k == 1:
+        if k == 0:
             small[2].to_plane()
-        if k == 3:
+        if k == 2:
             small[1].back_up()
         if k == 5:
             small[0].back_core()

time: 154 us -> 155 us (level)
  no operation moved by 1% of the time
where the time goes in v6:
time: 155 us; the launch traced here: 154 us
  Pallas kernels  151 us (97%)
  local copies, waits for them, and re-layouts  2.28 us (1%)
    pallas_call x1, Pallas kernels, rest(): pl.pallas_call(functools.partial(rest_kernel, plan, wide_cut, small_cuts)...  102 us
    pallas_call x1, Pallas kernels, front(): pl.pallas_call(functools.partial(front_kernel, plan), out_shape=[jax.Shap...  43.5 us
    pallas_call x1, Pallas kernels, unpack(): pl.pallas_call(functools.partial(unpack_kernel, plan), grid=(steps,), in_...  5.78 us

profile of v6, /device:TPU:25, one launch (start us, length us, event | category | flops | bytes accessed | tf_op | source)
XLA Modules:
  0.0 154.2 jit_solution(6881040882001064632)
XLA Ops:
  0.7 43.5 %front.1 = (bf16[8,128,384]{2,1,0:T(8,128)(2,1)}, bf16[8,128,384]{2,1,0:T(8,128)(2,1)}, bf16[384,1024]{1,0:T(8,128)(2,1)}, bf16[2048,384]{1,0:T(8,128)(2,1)}, bf...) custom-call(s32[8]{0:T(128)} %lengths.3, ...), custom_call_target="tpu_custom_call" | custom-call | tf_op jit(solution)/shard_map/front/pallas_call | solution.py:288
  44.2 101.9 %rest.1 = (bf16[8,128,384]{2,1,0:T(8,128)(2,1)}, bf16[8,128,384]{2,1,0:T(8,128)(2,1)}, bf16[3,3072,128]{2,1,0:T(8,128)(2,1)}, bf16[3,512,384]{2,1,0:T(8,128)(2,1)}, f32[16,384]{1,0:T(8,128)}) custom-call(s32[8]{0:T(128)} %lengths.3, bf16[384,1024]{1,0:T(8,128)(2,1)} %get-tuple-element.47.mixed_in, bf16[1024,384]{1,0:T(8,128)(2,1)} %bitcast.11, ...), custom_call_target="tpu_custom_call" | custom-call | tf_op jit(solution)/shard_map/rest/pallas_call | solution.py:899
  146.1 0.0 copy-start.1
  146.2 5.8 %unpack.1 = (f32[384,1152]{1,0:T(8,128)}, f32[384,384]{1,0:T(8,128)}, f32[384,1536]{1,0:T(8,128)}, f32[1536,384]{1,0:T(8,128)}, f32[1536]{0:T(1024)}, /*index=5*...) custom-call(bf16[3,512,384]{2,1,0:T(8,128)(2,1)} %get-tuple-element., ...), custom_call_target="tpu_custom_call" | custom-call | tf_op jit(solution)/shard_map/unpack/pallas_call | solution.py:976
  151.9 0.0 copy-start
  151.9 0.0 copy-done.1
  152.0 0.9 copy.39
  152.8 0.5 copy-done
  153.4 0.9 copy.40
Async XLA Ops:
  146.1 5.8 %copy-start.1 = (bf16[8,128,384]{2,1,0:T(8,128)(2,1)S(1)}, bf16[8,128,384]{2,1,0:T(8,128)(2,1)}, u32[]{:S(2)}) copy-start(bf16[8,128,384]{2,1,0:T(8,128)(2,1)} %get-tuple-element.57) | copy-start | bytes 2359300
  151.9 1.4 copy-start
